TPU v7x, 32 devices: a whole 2x2x4 slice. The times are simulated.
32 devices in a mesh: clus: 16 (over z, y, x), samp: 2 (over core).
Axes of the slice: x: 2, y: 2, z: 4, core: 2. Of those that a mesh axis runs over, the one named last changes fastest.
Arguments:
- child_patterns: float32 [512, 2, 6, 512], P('clus', None, 'samp'), may hold values from -6 to 6
- theta_weights: float32 [6, 9], replicated, may hold values from -0.4 to 0.6
- phi_stencil: int32 [1024, 6], replicated, may hold values from 0 to 511, as said below
- phi_weights: float32 [1024, 6], replicated, may hold values from -0.3 to 0.7
- shift_phase: float32 [8, 12, 1024], P(None, 'samp'), may hold values from -3.140625 to 3.140625
- translation_table: float32 [16, 2, 12, 1024], P(None, None, 'samp', 'clus'), may hold values from -1.25 to 1.25
- far_list: int32 [64, 12], replicated, may hold values from 0 to 63, as said below
- far_vector: int32 [64, 12], replicated, may hold values from 0 to 15
Outputs:
- parent_incoming: float32 [64, 2, 12, 1024], P('clus', None, 'samp')
- child_incoming: float32 [512, 2, 6, 512], P('clus', None, 'samp')
Inputs may be any that keep to these rules, and one draw needn't show every extreme that they name: `far_list`: row i names 12 different parent clusters, never i itself. `phi_stencil`: row n names 6 cyclically consecutive child columns starting at n // 2 - 6 // 2 + 1 or one column later.
All inputs are finite; a program needn't handle non-finite values.
Results may differ from a plain program's by a relative error of at most 0.00007.
Values sent between devices are 32-bit elements; how exact they have to be, the bound alone decides.
No kernel may reach another device: no remote copies, remote signals or barrier semaphores. Data moves between devices by JAX's collectives and lax.ppermute only.
A program may use at most 128 MiB of HBM per device.

v0:
```python
import jax
import jax.numpy as jnp
from jax import lax
from jax.experimental import pallas as pl
from jax.experimental.pallas import tpu as pltpu
from jax.sharding import PartitionSpec as P

P_SIZE = 6
OCTANTS = 8
TILE = 128
PAIR = 2 * TILE
HALF = TILE // 2
VMEM_BYTES = 24 * 1024 * 1024
F32 = jnp.float32
BF16 = jnp.bfloat16

SIN_TERMS = (-1 / 6, 1 / 120, -1 / 5040, 1 / 362880, -1 / 39916800, 1 / 6227020800)
COS_TERMS = (-1 / 2, 1 / 24, -1 / 720, 1 / 40320, -1 / 3628800, 1 / 479001600, -1 / 87178291200)


def split_two(value):
    high = value.astype(BF16)
    return high, (value - high.astype(F32)).astype(BF16)


def split_three(value):
    high = value.astype(BF16)
    rest = value - high.astype(F32)
    middle = rest.astype(BF16)
    return high, middle, (rest - middle.astype(F32)).astype(BF16)


def product(left, right, left_dim=1, right_dim=0):
    return lax.dot_general(left, right, (((left_dim,), (right_dim,)), ((), ())), preferred_element_type=F32)


def product_exact(left, right, left_dim=1, right_dim=0):
    return lax.dot_general(
        left,
        right,
        (((left_dim,), (right_dim,)), ((), ())),
        preferred_element_type=F32,
        precision=lax.Precision.HIGHEST,
    )


def series(square, terms):
    total = jnp.full_like(square, terms[-1])
    for term in terms[-2::-1]:
        total = total * square + term
    return total


def iota(shape, dim):
    return lax.broadcasted_iota(jnp.int32, shape, dim)


def turned(block):
    return jnp.roll(block, HALF, axis=1)


def folded(theta, sources, own):
    below, middle, above = theta[:, :own], theta[:, own : 2 * own], theta[:, 2 * own :]
    return (middle, below + above) if sources == 2 else (middle, below, above)


def prepare_kernel(groups, sources, own, phase_ref, stencil_ref, weight_ref, theta_ref, cos_ref, sin_ref, wide_ref, up_ref, down_ref, cos_s, sin_s):
    rows = theta_ref.shape[0]
    azimuth = phase_ref.shape[1]
    blocks = wide_ref.shape[0]
    half = 0.5 * phase_ref[...]
    square = half * half
    sine = half + half * square * series(square, SIN_TERMS)
    cosine = 1.0 + square * series(square, COS_TERMS)
    for value, held, target in ((1.0 - 2.0 * sine * sine, cos_s, cos_ref), (2.0 * sine * cosine, sin_s, sin_ref)):
        for tile in range(azimuth // TILE):
            lanes = slice(tile * TILE, (tile + 1) * TILE)
            held[tile] = value[:, lanes]
            for octant in range(OCTANTS):
                part = held[tile, pl.ds(octant, rows, stride=OCTANTS), :]
                for group in range(groups):
                    target[octant, group * rows : (group + 1) * rows, lanes] = part
    for block in range(blocks):
        columns = slice(block * PAIR, (block + 1) * PAIR)
        after, before = (block + 1) % blocks, (block - 1) % blocks
        pieces = (
            (0, TILE, block * TILE),
            (TILE, 16, after * TILE),
            (PAIR - 16, 16, before * TILE + TILE - 16),
        )
        for start, size, first in pieces:
            child = iota((size, PAIR), 0) + first
            total = jnp.zeros((size, PAIR), F32)
            for point in range(P_SIZE):
                hit = stencil_ref[point : point + 1, columns] == child
                total = jnp.where(hit, weight_ref[point : point + 1, columns], total)
            high, low = split_two(total)
            wide_ref[block, start : start + size, :] = high
            wide_ref[block, PAIR + start : PAIR + start + size, :] = low
        empty = jnp.zeros((TILE - 32, PAIR), BF16)
        wide_ref[block, TILE + 16 : PAIR - 16, :] = empty
        wide_ref[block, PAIR + TILE + 16 : 2 * PAIR - 16, :] = empty
    tall, long = OCTANTS * groups * rows, groups * OCTANTS * own
    theta = theta_ref[...]
    for place, weights in enumerate(folded(theta, sources, own)):
        at_row = iota((tall, rows), 0) % rows == iota((tall, rows), 1)
        at_own = iota((own, long), 1) % own == iota((own, long), 0)
        spread = product_exact(product_exact(at_row.astype(F32), weights), at_own.astype(F32))
        tall_id = iota((tall, long), 0)
        octant = tall_id // (groups * rows)
        group = (tall_id // rows) % groups
        same = iota((tall, long), 1) // own == group * OCTANTS + octant
        high, low = split_two(jnp.where(same, spread, 0.0))
        up_ref[0, :, place * long : (place + 1) * long] = high
        up_ref[1, :, place * long : (place + 1) * long] = low
        at_row = iota((rows, tall), 1) % rows == iota((rows, tall), 0)
        at_own = iota((long, own), 0) % own == iota((long, own), 1)
        spread = product_exact(product_exact(at_own.astype(F32), weights, 1, 1), at_row.astype(F32))
        tall_id = iota((long, tall), 1)
        octant = tall_id // (groups * rows)
        group = (tall_id // rows) % groups
        same = iota((long, tall), 0) // own == group * OCTANTS + octant
        high, low = split_two(jnp.where(same, spread, 0.0))
        down_ref[0, place * long : (place + 1) * long, :] = high
        down_ref[1, place * long : (place + 1) * long, :] = low


def packed_pieces(real, imag, columns):
    lane = iota((real.shape[0], TILE), 1)
    found = []
    if columns == HALF:
        for start in range(0, real.shape[1], TILE):
            a, b = real[:, start : start + TILE], imag[:, start : start + TILE]
            found.append(jnp.where(lane < HALF, a, turned(b)))
            found.append(jnp.where(lane < HALF, turned(a), b))
        return found
    for start in range(0, real.shape[1], columns):
        found.append(jnp.concatenate([real[:, start : start + columns], imag[:, start : start + columns]], axis=1))
    return found


def unpacked_pieces(read, devices, columns):
    if columns == HALF:
        real, imag = [], []
        for pair in range(devices // 2):
            a, b = read(2 * pair), read(2 * pair + 1)
            lane = iota(a.shape, 1)
            real.append(jnp.where(lane < HALF, a, turned(b)))
            imag.append(jnp.where(lane < HALF, turned(a), b))
        return jnp.concatenate(real, axis=1), jnp.concatenate(imag, axis=1)
    blocks = [read(device) for device in range(devices)]
    return (
        jnp.concatenate([block[:, :columns] for block in blocks], axis=1),
        jnp.concatenate([block[:, columns:] for block in blocks], axis=1),
    )


def aggregate_kernel(groups, sources, own, devices, relative, *refs):
    fields = refs[:sources]
    cos_ref, sin_ref, wide_ref, up_ref = refs[sources : sources + 4]
    outs = refs[sources + 4 : -1]
    scratch = refs[-1]
    me = lax.axis_index("clus") if relative else 0
    blocks = wide_ref.shape[0]
    rows_all = cos_ref.shape[1]
    azimuth = cos_ref.shape[2]
    columns = azimuth // devices
    long = groups * OCTANTS * own
    stride = 2 * blocks
    refined = []
    for part in range(2):
        stacked = jnp.concatenate(
            [
                jnp.concatenate([field[pl.ds(2 * block + part, long, stride=stride), :] for block in range(blocks)], axis=1)
                for field in fields
            ],
            axis=0,
        )
        high, low = split_two(stacked)
        refined.append(product(up_ref[0], high) + (product(up_ref[1], high) + product(up_ref[0], low)))
    refined = jnp.concatenate(refined, axis=0)
    high, low = split_two(refined)
    lane = iota((refined.shape[0], TILE), 1)
    tall = OCTANTS * rows_all

    def windows(value, block):
        main = value[:, block * TILE : (block + 1) * TILE]
        after, before = (block + 1) % blocks, (block - 1) % blocks
        rim = jnp.where(lane < HALF, value[:, after * TILE : (after + 1) * TILE], value[:, before * TILE : (before + 1) * TILE])
        return [main, rim]

    for block in range(blocks):
        one, two = windows(high, block), windows(low, block)
        left = jnp.concatenate(one + two + one, axis=1)
        right = jnp.concatenate([wide_ref[block, :PAIR], wide_ref[block, :PAIR], wide_ref[block, PAIR:]], axis=0)
        spread = product(left, right)
        real = jnp.zeros((rows_all, PAIR), F32)
        imag = jnp.zeros((rows_all, PAIR), F32)
        for octant in range(OCTANTS):
            cosine = cos_ref[octant, :, block * PAIR : (block + 1) * PAIR]
            sine = sin_ref[octant, :, block * PAIR : (block + 1) * PAIR]
            a = spread[octant * rows_all : (octant + 1) * rows_all]
            b = spread[tall + octant * rows_all : tall + (octant + 1) * rows_all]
            real += a * cosine - b * sine
            imag += a * sine + b * cosine
        first = block * PAIR // columns
        for place, piece in enumerate(packed_pieces(real, imag, columns)):
            scratch[(first + place) ^ me] = piece
    hand_out(scratch, outs)


def hand_out(scratch, outs):
    if len(outs) == 1:
        outs[0][...] = scratch[...]
    else:
        for place, out in enumerate(outs):
            out[...] = scratch[place]


def tables_kernel(listed_ref, vector_ref, even_ref, odd_ref, hot_ref, even_out, odd_out):
    clusters, partners = listed_ref.shape
    vectors = even_ref.shape[0]
    even = jnp.concatenate(split_three(even_ref[...]), axis=0)
    odd = jnp.concatenate(split_three(odd_ref[...]), axis=0)
    for partner in range(partners):
        rows = slice(partner * clusters, (partner + 1) * clusters)
        listed = listed_ref[:, partner : partner + 1]
        hot = (iota((clusters, 3 * clusters), 1) % clusters == listed).astype(F32)
        hot_ref[rows, :] = hot.astype(BF16)
        vector = vector_ref[:, partner : partner + 1]
        chosen = (iota((clusters, 3 * vectors), 1) % vectors == vector).astype(F32).astype(BF16)
        even_out[rows, :] = product(chosen, even)
        odd_out[rows, :] = product(chosen, odd)


def translate_kernel(groups, rows, devices, relative, hot_ref, even_ref, odd_ref, *refs):
    count = devices if relative else 1
    arrived, outs, held, ready = refs[:count], refs[count : 2 * count], refs[-2], refs[-1]
    me = lax.axis_index("clus") if relative else 0
    size = groups * rows
    clusters = groups * devices
    partners = hot_ref.shape[0] // clusters
    width = held.shape[1]
    if relative:
        for place, block in enumerate(arrived):
            held[pl.ds(pl.multiple_of((me ^ place) * size, 8), size), :] = block[...]
    else:
        for device in range(devices):
            held[device * size : (device + 1) * size, :] = arrived[0][device]
    for row in range(rows):
        source = held[pl.ds(row, clusters, stride=rows), :]
        gathered = product(hot_ref[...], jnp.concatenate(split_three(source), axis=0))
        direct = jnp.zeros((clusters, width), F32)
        crossed = jnp.zeros((clusters, width), F32)
        for partner in range(partners):
            part = slice(partner * clusters, (partner + 1) * clusters)
            value = gathered[part]
            direct += value * even_ref[part, row * width : (row + 1) * width]
            crossed += value * odd_ref[part, row * width : (row + 1) * width]
        ready[pl.ds(row, clusters, stride=rows), :] = direct + jnp.roll(crossed, width // 2, axis=1)
    if relative:
        for place, out in enumerate(outs):
            out[...] = ready[pl.ds(pl.multiple_of((me ^ place) * size, 8), size), :]
    else:
        for device in range(devices):
            outs[0][device] = ready[device * size : (device + 1) * size, :]


def lower_kernel(groups, sources, own, devices, relative, *refs):
    count = devices if relative else 1
    arrived = refs[:count]
    cos_ref, sin_ref, wide_ref, down_ref = refs[count : count + 4]
    real_ref, imag_ref = refs[count + 4 : count + 6]
    outs = refs[count + 6 : count + 6 + sources]
    held = refs[-1]
    me = lax.axis_index("clus") if relative else 0
    blocks = wide_ref.shape[0]
    rows_all = cos_ref.shape[1]
    azimuth = cos_ref.shape[2]
    columns = azimuth // devices
    long = groups * OCTANTS * own
    tall = OCTANTS * rows_all
    stride = 2 * blocks
    if relative:
        for place, block in enumerate(arrived):
            held[me ^ place] = block[...]
    else:
        held[...] = arrived[0][...]
    real, imag = unpacked_pieces(lambda device: held[device], devices, columns)
    real_ref[...] = real
    imag_ref[...] = imag
    mains, rims = [], []
    for block in range(blocks):
        part = slice(block * PAIR, (block + 1) * PAIR)
        a, b = real[:, part], imag[:, part]
        low_real, low_imag = [], []
        for octant in range(OCTANTS):
            cosine, sine = cos_ref[octant, :, part], sin_ref[octant, :, part]
            low_real.append(a * cosine + b * sine)
            low_imag.append(b * cosine - a * sine)
        high, low = split_two(jnp.concatenate(low_real + low_imag, axis=0))
        left = jnp.concatenate([high, low, high], axis=1)
        right = jnp.concatenate([wide_ref[block, :PAIR], wide_ref[block, :PAIR], wide_ref[block, PAIR:]], axis=1)
        both = product(left, right, 1, 1)
        mains.append(both[:, :TILE])
        rims.append(both[:, TILE:])
    lane = iota((2 * tall, TILE), 1)
    coarse = jnp.concatenate(
        [
            mains[block] + jnp.where(lane < HALF, rims[(block - 1) % blocks], rims[(block + 1) % blocks])
            for block in range(blocks)
        ],
        axis=1,
    )
    high, low = split_two(coarse)
    for place, out in enumerate(outs):
        up, fine = down_ref[0, place * long : (place + 1) * long, :], down_ref[1, place * long : (place + 1) * long, :]
        for part in range(2):
            rows = slice(part * tall, (part + 1) * tall)
            value = product(up, high[rows]) + (product(fine, high[rows]) + product(up, low[rows]))
            for block in range(blocks):
                out[pl.ds(2 * block + part, long, stride=stride), :] = value[:, block * TILE : (block + 1) * TILE]


def call(kernel, outs, args, flops, scratch=(), name=None):
    held = sum(4 * leaf.size for leaf in outs) + sum(4 * arg.size for arg in args)
    return pl.pallas_call(
        kernel,
        out_shape=outs,
        in_specs=[pl.BlockSpec(memory_space=pltpu.VMEM)] * len(args),
        out_specs=[pl.BlockSpec(memory_space=pltpu.VMEM)] * len(outs),
        scratch_shapes=list(scratch),
        compiler_params=pltpu.CompilerParams(vmem_limit_bytes=VMEM_BYTES),
        cost_estimate=pl.CostEstimate(flops=flops, bytes_accessed=held, transcendentals=0),
        name=name,
    )(*args)


def bind(kernel, *settings):
    return lambda *refs: kernel(*settings, *refs)


def exchange(blocks, devices, relative):
    if not relative:
        return [lax.all_to_all(blocks[0], "clus", split_axis=0, concat_axis=0, tiled=True)]
    moved = [blocks[0]]
    for step in range(1, devices):
        moved.append(lax.ppermute(blocks[step], "clus", [(i, i ^ step) for i in range(devices)]))
    return moved


def per_device(child_patterns, theta_weights, phi_stencil, phi_weights, shift_phase, translation_table, far_list, far_vector):
    devices, halves = lax.axis_size("clus"), lax.axis_size("samp")
    children, _, own, columns = child_patterns.shape
    groups = children // OCTANTS
    rows, azimuth = theta_weights.shape[0], phi_stencil.shape[0]
    clusters, partners = far_list.shape
    vectors, width = translation_table.shape[0], 2 * translation_table.shape[3]
    blocks, rows_all = columns // TILE, groups * rows
    long, tall = children * own, OCTANTS * rows_all
    sources = 2 if halves == 2 else 3
    relative = devices & (devices - 1) == 0 and devices <= 16 and (rows_all % 8 == 0)
    struct = jax.ShapeDtypeStruct

    field = child_patterns.reshape(children, 2, own, blocks, TILE).transpose(0, 2, 3, 1, 4).reshape(long * blocks * 2, TILE)
    from_below = lax.ppermute(field, "samp", [(i, (i + 1) % halves) for i in range(halves)])
    fields = [field, from_below]
    if sources == 3:
        fields.append(lax.ppermute(field, "samp", [((i + 1) % halves, i) for i in range(halves)]))

    phase = shift_phase.transpose(1, 0, 2).reshape(rows * OCTANTS, azimuth)
    cosine, sine, wide, up, down = call(
        bind(prepare_kernel, groups, sources, own),
        [
            struct((OCTANTS, rows_all, azimuth), F32),
            struct((OCTANTS, rows_all, azimuth), F32),
            struct((blocks, 2 * PAIR, PAIR), BF16),
            struct((2, tall, sources * long), BF16),
            struct((2, sources * long, tall), BF16),
        ],
        [phase, phi_stencil.T, phi_weights.T, theta_weights],
        200_000_000,
        [pltpu.VMEM((azimuth // TILE, rows * OCTANTS, TILE), F32)] * 2,
        "prepare",
    )
    size = struct((rows_all, width), F32)
    sent = [size] * devices if relative else [struct((devices, rows_all, width), F32)]
    outgoing = call(
        bind(aggregate_kernel, groups, sources, own, devices, relative),
        sent,
        [*fields, cosine, sine, wide, up],
        1_500_000_000,
        [pltpu.VMEM((devices, rows_all, width), F32)],
        "aggregate",
    )
    arrived = exchange(outgoing, devices, relative)

    real, imag = translation_table[:, 0], translation_table[:, 1]
    even = jnp.concatenate([real, real], axis=-1).reshape(vectors, rows * width)
    odd = jnp.concatenate([imag, -imag], axis=-1).reshape(vectors, rows * width)
    hot, even, odd = call(
        tables_kernel,
        [
            struct((partners * clusters, 3 * clusters), BF16),
            struct((partners * clusters, rows * width), F32),
            struct((partners * clusters, rows * width), F32),
        ],
        [far_list, far_vector, even, odd],
        600_000_000,
        (),
        "tables",
    )
    translated = call(
        bind(translate_kernel, groups, rows, devices, relative),
        sent,
        [hot, even, odd, *arrived],
        600_000_000,
        [pltpu.VMEM((clusters * rows, width), F32)] * 2,
        "translate",
    )
    returned = exchange(translated, devices, relative)
    lowered = call(
        bind(lower_kernel, groups, sources, own, devices, relative),
        [struct((rows_all, azimuth), F32)] * 2 + [struct((long * blocks * 2, TILE), F32)] * sources,
        [*returned, cosine, sine, wide, down],
        1_500_000_000,
        [pltpu.VMEM((devices, rows_all, width), F32)],
        "lower",
    )
    total = lowered[2] + lax.ppermute(lowered[3], "samp", [((i + 1) % halves, i) for i in range(halves)])
    if sources == 3:
        total = total + lax.ppermute(lowered[4], "samp", [(i, (i + 1) % halves) for i in range(halves)])
    child_incoming = total.reshape(children, own, blocks, 2, TILE).transpose(0, 3, 1, 2, 4).reshape(children, 2, own, columns)
    parent_incoming = jnp.stack([part.reshape(groups, rows, azimuth) for part in lowered[:2]], axis=1)
    return (parent_incoming, child_incoming)


def solution(mesh):
    placed = (
        P("clus", None, "samp", None),
        P(),
        P(),
        P(),
        P(None, "samp", None),
        P(None, None, "samp", "clus"),
        P(),
        P(),
    )
    return jax.shard_map(
        per_device,
        mesh=mesh,
        in_specs=placed,
        out_specs=(P("clus", None, "samp", None), P("clus", None, "samp", None)),
        check_vma=False,
    )
```

profile of v0, /device:TPU:0, one launch (start us, length us, event | category | flops | bytes accessed | tf_op | source)
XLA Modules:
  0.0 78.4 jit_solution(14564920133413372266)
XLA Ops:
  0.6 0.5 collective-permute-start
  1.1 1.1 %fusion.1 = (f32[16,1,6,64]{3,1,2,0:T(1,128)S(1)}, f32[16,1,6,64]{3,1,2,0:T(1,128)S(1)}) fusion(f32[16,2,6,64]{3,1,2,0:T(2,128)} %param.13), kind=kLoop, calls=%fused_computation.8 | loop fusion | bytes 98304 | tf_op jit(solution)/shard_map/slice | solution.py:398
  2.2 0.0 copy-start.1
  2.2 0.9 %copy-done.1 = f32[8,6,1024]{2,0,1:T(8,128)S(1)} copy-done((f32[8,6,1024]{2,0,1:T(8,128)S(1)}, f32[8,6,1024]{2,0,1:T(8,128)}, u32[]{:S(2)}) %copy-start.1) | copy-done | bytes 196632
  3.1 0.8 copy-done.2
  3.9 0.8 copy-done.3
  4.7 0.7 copy-done.4
  5.3 1.8 %prepare.1 = (f32[8,24,1024]{2,1,0:T(8,128)S(1)}, f32[8,24,1024]{2,1,0:T(8,128)S(1)}, bf16[4,512,256]{2,1,0:T(8,128)(2,1)S(1)}, bf16[2,192,192]{2,1,0:T(8,128)(2,1)S(1)}, bf16[2,192,192]{2,1,0:T(8,128)(2,1)S(1)}) custom-call(f32[48,1024]{1,0:T(8,128)S(1)} %bitcast.33, s32[6,1024]{1,0:T(8,128)S(1)} %bitcast.34, f32[6,1024]{1,0:T(8,128)S(1)} %bitcast.35, ...), custom_call_target="tpu_custom_call" | custom-call | flops 200000000 | bytes 4505816 | tf_op jit(solution)/shard_map/prepare/pallas_call | solution.py:327
  7.2 0.0 collective-permute-done.refs_1_
  7.2 0.0 copy-start
  7.2 1.2 %copy-done = f32[32,2,3,512]{3,1,2,0:T(2,128)S(1)} copy-done((f32[32,2,3,512]{3,1,2,0:T(2,128)S(1)}, f32[32,2,3,512]{3,1,2,0:T(2,128)}, u32[]{:S(2)}) %copy-start) | copy-done | bytes 393240
  8.5 1.4 %aggregate.1 = (f32[24,128]{1,0:T(8,128)S(1)}, f32[24,128]{1,0:T(8,128)S(1)}, f32[24,128]{1,0:T(8,128)S(1)}, f32[24,128]{1,0:T(8,128)S(1)}, f32[24,128]{1,0:T(8,...) custom-call(f32[768,128]{1,0:T(8,128)S(1)} %bitcast.32, ...), custom_call_target="tpu_custom_call" | custom-call | flops 1500000000 | bytes 4947968 | tf_op jit(solution)/shard_map/aggregate/pallas_call | solution.py:327
  9.9 2.6 %collective-permute-start.1 = (f32[24,128]{1,0:T(8,128)S(1)}, f32[24,128]{1,0:T(8,128)S(1)}, u32[]{:S(2)}, u32[]{:S(2)}) collective-permute-start(f32[24,128]{1,0:T(8,128)S(1)} %get-tuple-element.54), channel_id=1, source_target_pairs={{0,2},{2,0},{4,6},{6,4},{8,10},{10,8},{12,14},{14,12},{16,18},{18,... | collective-permute-start | bytes 36872 | tf_op jit(solution)/shard_map/ppermute | solution.py:348
  12.5 1.5 %collective-permute-start.2 = (f32[24,128]{1,0:T(8,128)S(1)}, f32[24,128]{1,0:T(8,128)S(1)}, u32[]{:S(2)}, u32[]{:S(2)}) collective-permute-start(f32[24,128]{1,0:T(8,128)S(1)} %get-tuple-element.55), channel_id=1, source_target_pairs={{0,4},{2,6},{4,0},{6,2},{8,12},{10,14},{12,8},{14,10},{16,20},{18,... | collective-permute-start | bytes 36872 | tf_op jit(solution)/shard_map/ppermute | solution.py:348
  14.0 0.0 collective-permute-start.3
  14.1 2.0 %collective-permute-start.4 = (f32[24,128]{1,0:T(8,128)S(1)}, f32[24,128]{1,0:T(8,128)S(1)}, u32[]{:S(2)}, u32[]{:S(2)}) collective-permute-start(f32[24,128]{1,0:T(8,128)S(1)} %get-tuple-element.57), channel_id=1, source_target_pairs={{0,8},{2,10},{4,12},{6,14},{8,0},{10,2},{12,4},{14,6},{16,24},{18,... | collective-permute-start | bytes 36872 | tf_op jit(solution)/shard_map/ppermute | solution.py:348
  16.1 1.4 %collective-permute-start.5 = (f32[24,128]{1,0:T(8,128)S(1)}, f32[24,128]{1,0:T(8,128)S(1)}, u32[]{:S(2)}, u32[]{:S(2)}) collective-permute-start(f32[24,128]{1,0:T(8,128)S(1)} %get-tuple-element.58), channel_id=1, source_target_pairs={{0,10},{2,8},{4,14},{6,12},{8,2},{10,0},{12,6},{14,4},{16,26},{18,... | collective-permute-start | bytes 36872 | tf_op jit(solution)/shard_map/ppermute | solution.py:348
  17.5 0.1 copy_bitcast_fusion.1.even_ref
  17.6 2.6 %collective-permute-start.6 = (f32[24,128]{1,0:T(8,128)S(1)}, f32[24,128]{1,0:T(8,128)S(1)}, u32[]{:S(2)}, u32[]{:S(2)}) collective-permute-start(f32[24,128]{1,0:T(8,128)S(1)} %get-tuple-element.59), channel_id=1, source_target_pairs={{0,12},{2,14},{4,8},{6,10},{8,4},{10,6},{12,0},{14,2},{16,28},{18,... | collective-permute-start | bytes 36872 | tf_op jit(solution)/shard_map/ppermute | solution.py:348
  20.1 0.0 collective-permute-done.2.refs_5_
  20.2 0.1 collective-permute-start.7
  20.2 0.0 collective-permute-done.3.refs_6_
  20.2 2.9 %collective-permute-start.8 = (f32[24,128]{1,0:T(8,128)S(1)}, f32[24,128]{1,0:T(8,128)S(1)}, u32[]{:S(2)}, u32[]{:S(2)}) collective-permute-start(f32[24,128]{1,0:T(8,128)S(1)} %get-tuple-element.61), channel_id=1, source_target_pairs={{0,16},{2,18},{4,20},{6,22},{8,24},{10,26},{12,28},{14,30},{16,0},... | collective-permute-start | bytes 36872 | tf_op jit(solution)/shard_map/ppermute | solution.py:348
  23.1 1.3 %collective-permute-start.9 = (f32[24,128]{1,0:T(8,128)S(1)}, f32[24,128]{1,0:T(8,128)S(1)}, u32[]{:S(2)}, u32[]{:S(2)}) collective-permute-start(f32[24,128]{1,0:T(8,128)S(1)} %get-tuple-element.62), channel_id=1, source_target_pairs={{0,18},{2,16},{4,22},{6,20},{8,26},{10,24},{12,30},{14,28},{16,2},... | collective-permute-start | bytes 36872 | tf_op jit(solution)/shard_map/ppermute | solution.py:348
  24.4 3.5 %collective-permute-start.10 = (f32[24,128]{1,0:T(8,128)S(1)}, f32[24,128]{1,0:T(8,128)S(1)}, u32[]{:S(2)}, u32[]{:S(2)}) collective-permute-start(f32[24,128]{1,0:T(8,128)S(1)} %get-tuple-element.63), channel_id=1, source_target_pairs={{0,20},{2,22},{4,16},{6,18},{8,28},{10,30},{12,24},{14,26},{16,4},... | collective-permute-start | bytes 36872 | tf_op jit(solution)/shard_map/ppermute | solution.py:348
  27.9 0.1 copy_bitcast_fusion.odd_ref
  28.0 0.1 copy.20.listed_ref
  28.1 0.1 copy.21.vector_ref
  28.2 0.0 collective-permute-done.6.refs_9_
  28.2 0.1 collective-permute-start.11
  28.3 0.0 collective-permute-done.7.refs_10_
  28.3 3.8 %collective-permute-start.12 = (f32[24,128]{1,0:T(8,128)S(1)}, f32[24,128]{1,0:T(8,128)S(1)}, u32[]{:S(2)}, u32[]{:S(2)}) collective-permute-start(f32[24,128]{1,0:T(8,128)S(1)} %get-tuple-element.65), channel_id=1, source_target_pairs={{0,24},{2,26},{4,28},{6,30},{8,16},{10,18},{12,20},{14,22},{16,8},... | collective-permute-start | bytes 36872 | tf_op jit(solution)/shard_map/ppermute | solution.py:348
  32.1 0.0 collective-permute-done.8.refs_11_
  32.1 1.2 %collective-permute-start.13 = (f32[24,128]{1,0:T(8,128)S(1)}, f32[24,128]{1,0:T(8,128)S(1)}, u32[]{:S(2)}, u32[]{:S(2)}) collective-permute-start(f32[24,128]{1,0:T(8,128)S(1)} %get-tuple-element.66), channel_id=1, source_target_pairs={{0,26},{2,24},{4,30},{6,28},{8,18},{10,16},{12,22},{14,20},{16,10}... | collective-permute-start | bytes 36872 | tf_op jit(solution)/shard_map/ppermute | solution.py:348
  33.3 0.0 collective-permute-done.9.refs_12_
  33.3 4.6 %collective-permute-start.14 = (f32[24,128]{1,0:T(8,128)S(1)}, f32[24,128]{1,0:T(8,128)S(1)}, u32[]{:S(2)}, u32[]{:S(2)}) collective-permute-start(f32[24,128]{1,0:T(8,128)S(1)} %get-tuple-element.67), channel_id=1, source_target_pairs={{0,28},{2,30},{4,24},{6,26},{8,20},{10,22},{12,16},{14,18},{16,12}... | collective-permute-start | bytes 36872 | tf_op jit(solution)/shard_map/ppermute | solution.py:348
  37.8 0.0 collective-permute-done.10.refs_13_
  37.8 0.0 collective-permute-start.15
  37.9 0.8 %tables.1 = (bf16[768,192]{1,0:T(8,128)(2,1)S(1)}, f32[768,768]{1,0:T(8,128)S(1)}, f32[768,768]{1,0:T(8,128)S(1)}) custom-call(s32[64,12]{1,0:T(8,128)S(1)} %copy.20.listed_ref, s32[64,12]{1,0:T(8,128)S(1)} %copy.21.vector_ref, f32[16,768]{1,0:T(8,128)S(1)} %copy_bitcast_fusion.1.even_ref, f32[16,768]{1,0:T(8,128)S(1)} %copy_bitcast_fusion.odd_ref), custom_call_target="tpu_custom_call" | custom-call | flops 600000000 | bytes 5412864 | tf_op jit(solution)/shard_map/tables/pallas_call | solution.py:327
  38.7 0.0 collective-permute-done.12.refs_15_
  38.7 0.0 collective-permute-done.13.refs_16_
  38.7 1.0 %collective-permute-done.14.refs_17_ = f32[24,128]{1,0:T(8,128)S(1)} collective-permute-done((f32[24,128]{1,0:T(8,128)S(1)}, f32[24,128]{1,0:T(8,128)S(1)}, u32[]{:S(2)}, u32[]{:S(2)}) %collective-permute-start.14) | collective-permute-done | bytes 12320 | tf_op jit(solution)/shard_map/ppermute | solution.py:348
  39.7 5.4 %collective-permute-done.15.refs_18_ = f32[24,128]{1,0:T(8,128)S(1)} collective-permute-done((f32[24,128]{1,0:T(8,128)S(1)}, f32[24,128]{1,0:T(8,128)S(1)}, u32[]{:S(2)}, u32[]{:S(2)}) %collective-permute-start.15) | collective-permute-done | bytes 12320 | tf_op jit(solution)/shard_map/ppermute | solution.py:348
  45.1 0.9 %translate.1 = (f32[24,128]{1,0:T(8,128)S(1)}, f32[24,128]{1,0:T(8,128)S(1)}, f32[24,128]{1,0:T(8,128)S(1)}, f32[24,128]{1,0:T(8,128)S(1)}, f32[24,128]{1,0:T(8,...) custom-call(bf16[768,192]{1,0:T(8,128)(2,1)S(1)} %get-tuple-element., ...), custom_call_target="tpu_custom_call" | custom-call | flops 600000000 | bytes 5701632 | tf_op jit(solution)/shard_map/translate/pallas_call | solution.py:327
  46.0 0.6 collective-permute-start.16
  46.6 0.5 collective-permute-start.17
  47.1 2.4 %collective-permute-start.18 = (f32[24,128]{1,0:T(8,128)S(1)}, f32[24,128]{1,0:T(8,128)S(1)}, u32[]{:S(2)}, u32[]{:S(2)}) collective-permute-start(f32[24,128]{1,0:T(8,128)S(1)} %get-tuple-element.72), channel_id=1, source_target_pairs={{0,6},{2,4},{4,2},{6,0},{8,14},{10,12},{12,10},{14,8},{16,22},{18,... | collective-permute-start | bytes 36872 | tf_op jit(solution)/shard_map/ppermute | solution.py:348
  49.6 2.0 %collective-permute-start.20 = (f32[24,128]{1,0:T(8,128)S(1)}, f32[24,128]{1,0:T(8,128)S(1)}, u32[]{:S(2)}, u32[]{:S(2)}) collective-permute-start(f32[24,128]{1,0:T(8,128)S(1)} %get-tuple-element.74), channel_id=1, source_target_pairs={{0,10},{2,8},{4,14},{6,12},{8,2},{10,0},{12,6},{14,4},{16,26},{18,... | collective-permute-start | bytes 36872 | tf_op jit(solution)/shard_map/ppermute | solution.py:348
  51.6 0.0 collective-permute-done.16.refs_1_
  51.6 3.8 %collective-permute-start.22 = (f32[24,128]{1,0:T(8,128)S(1)}, f32[24,128]{1,0:T(8,128)S(1)}, u32[]{:S(2)}, u32[]{:S(2)}) collective-permute-start(f32[24,128]{1,0:T(8,128)S(1)} %get-tuple-element.76), channel_id=1, source_target_pairs={{0,14},{2,12},{4,10},{6,8},{8,6},{10,4},{12,2},{14,0},{16,30},{18,... | collective-permute-start | bytes 36872 | tf_op jit(solution)/shard_map/ppermute | solution.py:348
  55.5 2.9 %collective-permute-start.24 = (f32[24,128]{1,0:T(8,128)S(1)}, f32[24,128]{1,0:T(8,128)S(1)}, u32[]{:S(2)}, u32[]{:S(2)}) collective-permute-start(f32[24,128]{1,0:T(8,128)S(1)} %get-tuple-element.78), channel_id=1, source_target_pairs={{0,18},{2,16},{4,22},{6,20},{8,26},{10,24},{12,30},{14,28},{16,2},... | collective-permute-start | bytes 36872 | tf_op jit(solution)/shard_map/ppermute | solution.py:348
  58.4 0.0 collective-permute-start.25
  58.4 4.7 %collective-permute-start.26 = (f32[24,128]{1,0:T(8,128)S(1)}, f32[24,128]{1,0:T(8,128)S(1)}, u32[]{:S(2)}, u32[]{:S(2)}) collective-permute-start(f32[24,128]{1,0:T(8,128)S(1)} %get-tuple-element.80), channel_id=1, source_target_pairs={{0,22},{2,20},{4,18},{6,16},{8,30},{10,28},{12,26},{14,24},{16,6},... | collective-permute-start | bytes 36872 | tf_op jit(solution)/shard_map/ppermute | solution.py:348
  63.1 0.2 collective-permute-start.27
  63.3 3.6 %collective-permute-start.28 = (f32[24,128]{1,0:T(8,128)S(1)}, f32[24,128]{1,0:T(8,128)S(1)}, u32[]{:S(2)}, u32[]{:S(2)}) collective-permute-start(f32[24,128]{1,0:T(8,128)S(1)} %get-tuple-element.82), channel_id=1, source_target_pairs={{0,26},{2,24},{4,30},{6,28},{8,18},{10,16},{12,22},{14,20},{16,10}... | collective-permute-start | bytes 36872 | tf_op jit(solution)/shard_map/ppermute | solution.py:348
  66.9 0.2 collective-permute-start.29
  67.1 5.5 %collective-permute-start.30 = (f32[24,128]{1,0:T(8,128)S(1)}, f32[24,128]{1,0:T(8,128)S(1)}, u32[]{:S(2)}, u32[]{:S(2)}) collective-permute-start(f32[24,128]{1,0:T(8,128)S(1)} %get-tuple-element.84), channel_id=1, source_target_pairs={{0,30},{2,28},{4,26},{6,24},{8,22},{10,20},{12,18},{14,16},{16,14}... | collective-permute-start | bytes 36872 | tf_op jit(solution)/shard_map/ppermute | solution.py:348
  72.6 0.7 collective-permute-done.29.refs_14_
  73.3 1.1 %collective-permute-done.30.refs_15_ = f32[24,128]{1,0:T(8,128)S(1)} collective-permute-done((f32[24,128]{1,0:T(8,128)S(1)}, f32[24,128]{1,0:T(8,128)S(1)}, u32[]{:S(2)}, u32[]{:S(2)}) %collective-permute-start.30) | collective-permute-done | bytes 12320 | tf_op jit(solution)/shard_map/ppermute | solution.py:348
  74.4 1.4 %lower.1 = (f32[24,1024]{1,0:T(8,128)S(1)}, f32[24,1024]{1,0:T(8,128)S(1)}, f32[768,128]{1,0:T(8,128)S(1)}, f32[768,128]{1,0:T(8,128)S(1)}) custom-call(f32[24,128]{1,0:T(8,128)S(1)} %get-tuple-element.69.refs_0_, f32[24,128]{1,0:T(8,128)S(1)} %collective-permute-done.16.refs_1_, f32[24,128]{1,0:T(8,128)S(1)} %collective-permute-done.17.refs_2_, ...), custom_call_target="tpu_custom_call" | custom-call | flops 1500000000 | bytes 5144576 | tf_op jit(solution)/shard_map/lower/pallas_call | solution.py:327
  75.8 0.1 collective-permute-start.31
  75.9 0.8 %copy.24 = f32[4,2,6,1024]{3,1,2,0:T(2,128)} copy(f32[4,2,6,1024]{3,2,0,1:T(8,128)S(1)} %pad_maximum_fusion) | data formatting | bytes 393216
  76.8 0.8 %collective-permute-done.31 = f32[768,128]{1,0:T(8,128)S(1)} collective-permute-done((f32[768,128]{1,0:T(8,128)S(1)}, f32[768,128]{1,0:T(8,128)S(1)}, u32[]{:S(2)}, u32[]{:S(2)}) %collective-permute-start.31) | collective-permute-done | bytes 393248 | tf_op jit(solution)/shard_map/ppermute | solution.py:430
  77.6 0.8 %add.3 = f32[768,128]{1,0:T(8,128)} add(f32[768,128]{1,0:T(8,128)S(1)} %get-tuple-element.88, f32[768,128]{1,0:T(8,128)S(1)} %collective-permute-done.31) | non-fusion elementwise | flops 98304 | bytes 1179648 | tf_op jit(solution)/shard_map/add | solution.py:430
  (35 shorter events, 0.1 us)
Async XLA Ops:
  0.6 6.6 %collective-permute-start = (f32[768,128]{1,0:T(8,128)}, f32[768,128]{1,0:T(8,128)S(1)}, u32[]{:S(2)}, u32[]{:S(2)}) collective-permute-start(f32[768,128]{1,0:T(8,128)} %bitcast.31), channel_id=1, source_target_pairs={{0,1},{1,0},{2,3},{3,2},{4,5},{5,4},{6,7},{7,6},{8,9},{9,8},{10,11... | collective-permute-start | bytes 1179656 | tf_op jit(solution)/shard_map/ppermute | solution.py:366
  2.2 0.9 %copy-start.1 = (f32[8,6,1024]{2,0,1:T(8,128)S(1)}, f32[8,6,1024]{2,0,1:T(8,128)}, u32[]{:S(2)}) copy-start(f32[8,6,1024]{2,0,1:T(8,128)} %param.12) | copy-start | bytes 589828
  3.1 0.8 copy-start.2
  3.9 0.8 copy-start.3
  4.7 0.7 copy-start.4
  7.2 2.8 %copy-start.5 = (f32[8,24,1024]{2,1,0:T(8,128)}, f32[8,24,1024]{2,1,0:T(8,128)S(1)}, u32[]{:S(2)}) copy-start(f32[8,24,1024]{2,1,0:T(8,128)S(1)} %get-tuple-element.50.refs_3_.refs_17_) | copy-start | bytes 2359300
  7.2 1.2 %copy-start = (f32[32,2,3,512]{3,1,2,0:T(2,128)S(1)}, f32[32,2,3,512]{3,1,2,0:T(2,128)}, u32[]{:S(2)}) copy-start(f32[32,2,3,512]{3,1,2,0:T(2,128)} %param.8) | copy-start | bytes 1179652
  8.5 19.5 %copy-start.7 = (s32[64,12]{0,1:T(8,128)S(1)}, s32[64,12]{0,1:T(8,128)}, u32[]{:S(2)}) copy-start(s32[64,12]{0,1:T(8,128)} %param.14) | copy-start | bytes 9220
  8.5 19.6 %copy-start.8 = (s32[64,12]{0,1:T(8,128)S(1)}, s32[64,12]{0,1:T(8,128)}, u32[]{:S(2)}) copy-start(s32[64,12]{0,1:T(8,128)} %param.15) | copy-start | bytes 9220
  9.9 7.6 %collective-permute-start.1 = (f32[24,128]{1,0:T(8,128)S(1)}, f32[24,128]{1,0:T(8,128)S(1)}, u32[]{:S(2)}, u32[]{:S(2)}) collective-permute-start(f32[24,128]{1,0:T(8,128)S(1)} %get-tuple-element.54), channel_id=1, source_target_pairs={{0,2},{2,0},{4,6},{6,4},{8,10},{10,8},{12,14},{14,12},{16,18},{18,... | collective-permute-start | bytes 36872 | tf_op jit(solution)/shard_map/ppermute | solution.py:348
  12.5 7.6 %collective-permute-start.2 = (f32[24,128]{1,0:T(8,128)S(1)}, f32[24,128]{1,0:T(8,128)S(1)}, u32[]{:S(2)}, u32[]{:S(2)}) collective-permute-start(f32[24,128]{1,0:T(8,128)S(1)} %get-tuple-element.55), channel_id=1, source_target_pairs={{0,4},{2,6},{4,0},{6,2},{8,12},{10,14},{12,8},{14,10},{16,20},{18,... | collective-permute-start | bytes 36872 | tf_op jit(solution)/shard_map/ppermute | solution.py:348
  14.0 6.2 %collective-permute-start.3 = (f32[24,128]{1,0:T(8,128)S(1)}, f32[24,128]{1,0:T(8,128)S(1)}, u32[]{:S(2)}, u32[]{:S(2)}) collective-permute-start(f32[24,128]{1,0:T(8,128)S(1)} %get-tuple-element.56), channel_id=1, source_target_pairs={{0,6},{2,4},{4,2},{6,0},{8,14},{10,12},{12,10},{14,8},{16,22},{18,... | collective-permute-start | bytes 36872 | tf_op jit(solution)/shard_map/ppermute | solution.py:348
  14.1 9.1 %collective-permute-start.4 = (f32[24,128]{1,0:T(8,128)S(1)}, f32[24,128]{1,0:T(8,128)S(1)}, u32[]{:S(2)}, u32[]{:S(2)}) collective-permute-start(f32[24,128]{1,0:T(8,128)S(1)} %get-tuple-element.57), channel_id=1, source_target_pairs={{0,8},{2,10},{4,12},{6,14},{8,0},{10,2},{12,4},{14,6},{16,24},{18,... | collective-permute-start | bytes 36872 | tf_op jit(solution)/shard_map/ppermute | solution.py:348
  16.1 8.3 %collective-permute-start.5 = (f32[24,128]{1,0:T(8,128)S(1)}, f32[24,128]{1,0:T(8,128)S(1)}, u32[]{:S(2)}, u32[]{:S(2)}) collective-permute-start(f32[24,128]{1,0:T(8,128)S(1)} %get-tuple-element.58), channel_id=1, source_target_pairs={{0,10},{2,8},{4,14},{6,12},{8,2},{10,0},{12,6},{14,4},{16,26},{18,... | collective-permute-start | bytes 36872 | tf_op jit(solution)/shard_map/ppermute | solution.py:348
  17.6 10.7 %collective-permute-start.6 = (f32[24,128]{1,0:T(8,128)S(1)}, f32[24,128]{1,0:T(8,128)S(1)}, u32[]{:S(2)}, u32[]{:S(2)}) collective-permute-start(f32[24,128]{1,0:T(8,128)S(1)} %get-tuple-element.59), channel_id=1, source_target_pairs={{0,12},{2,14},{4,8},{6,10},{8,4},{10,6},{12,0},{14,2},{16,28},{18,... | collective-permute-start | bytes 36872 | tf_op jit(solution)/shard_map/ppermute | solution.py:348
  20.2 8.1 %collective-permute-start.7 = (f32[24,128]{1,0:T(8,128)S(1)}, f32[24,128]{1,0:T(8,128)S(1)}, u32[]{:S(2)}, u32[]{:S(2)}) collective-permute-start(f32[24,128]{1,0:T(8,128)S(1)} %get-tuple-element.60), channel_id=1, source_target_pairs={{0,14},{2,12},{4,10},{6,8},{8,6},{10,4},{12,2},{14,0},{16,30},{18,... | collective-permute-start | bytes 36872 | tf_op jit(solution)/shard_map/ppermute | solution.py:348
  20.2 11.9 %collective-permute-start.8 = (f32[24,128]{1,0:T(8,128)S(1)}, f32[24,128]{1,0:T(8,128)S(1)}, u32[]{:S(2)}, u32[]{:S(2)}) collective-permute-start(f32[24,128]{1,0:T(8,128)S(1)} %get-tuple-element.61), channel_id=1, source_target_pairs={{0,16},{2,18},{4,20},{6,22},{8,24},{10,26},{12,28},{14,30},{16,0},... | collective-permute-start | bytes 36872 | tf_op jit(solution)/shard_map/ppermute | solution.py:348
  23.1 10.2 %collective-permute-start.9 = (f32[24,128]{1,0:T(8,128)S(1)}, f32[24,128]{1,0:T(8,128)S(1)}, u32[]{:S(2)}, u32[]{:S(2)}) collective-permute-start(f32[24,128]{1,0:T(8,128)S(1)} %get-tuple-element.62), channel_id=1, source_target_pairs={{0,18},{2,16},{4,22},{6,20},{8,26},{10,24},{12,30},{14,28},{16,2},... | collective-permute-start | bytes 36872 | tf_op jit(solution)/shard_map/ppermute | solution.py:348
  24.4 13.5 %collective-permute-start.10 = (f32[24,128]{1,0:T(8,128)S(1)}, f32[24,128]{1,0:T(8,128)S(1)}, u32[]{:S(2)}, u32[]{:S(2)}) collective-permute-start(f32[24,128]{1,0:T(8,128)S(1)} %get-tuple-element.63), channel_id=1, source_target_pairs={{0,20},{2,22},{4,16},{6,18},{8,28},{10,30},{12,24},{14,26},{16,4},... | collective-permute-start | bytes 36872 | tf_op jit(solution)/shard_map/ppermute | solution.py:348
  28.2 10.5 %collective-permute-start.11 = (f32[24,128]{1,0:T(8,128)S(1)}, f32[24,128]{1,0:T(8,128)S(1)}, u32[]{:S(2)}, u32[]{:S(2)}) collective-permute-start(f32[24,128]{1,0:T(8,128)S(1)} %get-tuple-element.64), channel_id=1, source_target_pairs={{0,22},{2,20},{4,18},{6,16},{8,30},{10,28},{12,26},{14,24},{16,6},... | collective-permute-start | bytes 36872 | tf_op jit(solution)/shard_map/ppermute | solution.py:348
  28.3 10.4 %collective-permute-start.12 = (f32[24,128]{1,0:T(8,128)S(1)}, f32[24,128]{1,0:T(8,128)S(1)}, u32[]{:S(2)}, u32[]{:S(2)}) collective-permute-start(f32[24,128]{1,0:T(8,128)S(1)} %get-tuple-element.65), channel_id=1, source_target_pairs={{0,24},{2,26},{4,28},{6,30},{8,16},{10,18},{12,20},{14,22},{16,8},... | collective-permute-start | bytes 36872 | tf_op jit(solution)/shard_map/ppermute | solution.py:348
  32.1 6.6 %collective-permute-start.13 = (f32[24,128]{1,0:T(8,128)S(1)}, f32[24,128]{1,0:T(8,128)S(1)}, u32[]{:S(2)}, u32[]{:S(2)}) collective-permute-start(f32[24,128]{1,0:T(8,128)S(1)} %get-tuple-element.66), channel_id=1, source_target_pairs={{0,26},{2,24},{4,30},{6,28},{8,18},{10,16},{12,22},{14,20},{16,10}... | collective-permute-start | bytes 36872 | tf_op jit(solution)/shard_map/ppermute | solution.py:348
  33.3 6.4 %collective-permute-start.14 = (f32[24,128]{1,0:T(8,128)S(1)}, f32[24,128]{1,0:T(8,128)S(1)}, u32[]{:S(2)}, u32[]{:S(2)}) collective-permute-start(f32[24,128]{1,0:T(8,128)S(1)} %get-tuple-element.67), channel_id=1, source_target_pairs={{0,28},{2,30},{4,24},{6,26},{8,20},{10,22},{12,16},{14,18},{16,12}... | collective-permute-start | bytes 36872 | tf_op jit(solution)/shard_map/ppermute | solution.py:348
  37.8 7.3 %collective-permute-start.15 = (f32[24,128]{1,0:T(8,128)S(1)}, f32[24,128]{1,0:T(8,128)S(1)}, u32[]{:S(2)}, u32[]{:S(2)}) collective-permute-start(f32[24,128]{1,0:T(8,128)S(1)} %get-tuple-element.68), channel_id=1, source_target_pairs={{0,30},{2,28},{4,26},{6,24},{8,22},{10,20},{12,18},{14,16},{16,14}... | collective-permute-start | bytes 36872 | tf_op jit(solution)/shard_map/ppermute | solution.py:348
  45.1 29.2 %copy-start.6 = (f32[8,24,1024]{2,1,0:T(8,128)S(1)}, f32[8,24,1024]{2,1,0:T(8,128)}, u32[]{:S(2)}) copy-start(f32[8,24,1024]{2,1,0:T(8,128)} %copy-done.5) | copy-start | bytes 2359300
  46.0 5.6 %collective-permute-start.16 = (f32[24,128]{1,0:T(8,128)S(1)}, f32[24,128]{1,0:T(8,128)S(1)}, u32[]{:S(2)}, u32[]{:S(2)}) collective-permute-start(f32[24,128]{1,0:T(8,128)S(1)} %get-tuple-element.70), channel_id=1, source_target_pairs={{0,2},{2,0},{4,6},{6,4},{8,10},{10,8},{12,14},{14,12},{16,18},{18,... | collective-permute-start | bytes 36872 | tf_op jit(solution)/shard_map/ppermute | solution.py:348
  46.6 5.0 %collective-permute-start.17 = (f32[24,128]{1,0:T(8,128)S(1)}, f32[24,128]{1,0:T(8,128)S(1)}, u32[]{:S(2)}, u32[]{:S(2)}) collective-permute-start(f32[24,128]{1,0:T(8,128)S(1)} %get-tuple-element.71), channel_id=1, source_target_pairs={{0,4},{2,6},{4,0},{6,2},{8,12},{10,14},{12,8},{14,10},{16,20},{18,... | collective-permute-start | bytes 36872 | tf_op jit(solution)/shard_map/ppermute | solution.py:348
  47.1 8.3 %collective-permute-start.18 = (f32[24,128]{1,0:T(8,128)S(1)}, f32[24,128]{1,0:T(8,128)S(1)}, u32[]{:S(2)}, u32[]{:S(2)}) collective-permute-start(f32[24,128]{1,0:T(8,128)S(1)} %get-tuple-element.72), channel_id=1, source_target_pairs={{0,6},{2,4},{4,2},{6,0},{8,14},{10,12},{12,10},{14,8},{16,22},{18,... | collective-permute-start | bytes 36872 | tf_op jit(solution)/shard_map/ppermute | solution.py:348
  49.6 5.9 %collective-permute-start.19 = (f32[24,128]{1,0:T(8,128)S(1)}, f32[24,128]{1,0:T(8,128)S(1)}, u32[]{:S(2)}, u32[]{:S(2)}) collective-permute-start(f32[24,128]{1,0:T(8,128)S(1)} %get-tuple-element.73), channel_id=1, source_target_pairs={{0,8},{2,10},{4,12},{6,14},{8,0},{10,2},{12,4},{14,6},{16,24},{18,... | collective-permute-start | bytes 36872 | tf_op jit(solution)/shard_map/ppermute | solution.py:348
  49.6 8.8 %collective-permute-start.20 = (f32[24,128]{1,0:T(8,128)S(1)}, f32[24,128]{1,0:T(8,128)S(1)}, u32[]{:S(2)}, u32[]{:S(2)}) collective-permute-start(f32[24,128]{1,0:T(8,128)S(1)} %get-tuple-element.74), channel_id=1, source_target_pairs={{0,10},{2,8},{4,14},{6,12},{8,2},{10,0},{12,6},{14,4},{16,26},{18,... | collective-permute-start | bytes 36872 | tf_op jit(solution)/shard_map/ppermute | solution.py:348
  51.6 6.8 %collective-permute-start.21 = (f32[24,128]{1,0:T(8,128)S(1)}, f32[24,128]{1,0:T(8,128)S(1)}, u32[]{:S(2)}, u32[]{:S(2)}) collective-permute-start(f32[24,128]{1,0:T(8,128)S(1)} %get-tuple-element.75), channel_id=1, source_target_pairs={{0,12},{2,14},{4,8},{6,10},{8,4},{10,6},{12,0},{14,2},{16,28},{18,... | collective-permute-start | bytes 36872 | tf_op jit(solution)/shard_map/ppermute | solution.py:348
  51.6 11.5 %collective-permute-start.22 = (f32[24,128]{1,0:T(8,128)S(1)}, f32[24,128]{1,0:T(8,128)S(1)}, u32[]{:S(2)}, u32[]{:S(2)}) collective-permute-start(f32[24,128]{1,0:T(8,128)S(1)} %get-tuple-element.76), channel_id=1, source_target_pairs={{0,14},{2,12},{4,10},{6,8},{8,6},{10,4},{12,2},{14,0},{16,30},{18,... | collective-permute-start | bytes 36872 | tf_op jit(solution)/shard_map/ppermute | solution.py:348
  55.4 7.9 %collective-permute-start.23 = (f32[24,128]{1,0:T(8,128)S(1)}, f32[24,128]{1,0:T(8,128)S(1)}, u32[]{:S(2)}, u32[]{:S(2)}) collective-permute-start(f32[24,128]{1,0:T(8,128)S(1)} %get-tuple-element.77), channel_id=1, source_target_pairs={{0,16},{2,18},{4,20},{6,22},{8,24},{10,26},{12,28},{14,30},{16,0},... | collective-permute-start | bytes 36872 | tf_op jit(solution)/shard_map/ppermute | solution.py:348
  55.5 11.5 %collective-permute-start.24 = (f32[24,128]{1,0:T(8,128)S(1)}, f32[24,128]{1,0:T(8,128)S(1)}, u32[]{:S(2)}, u32[]{:S(2)}) collective-permute-start(f32[24,128]{1,0:T(8,128)S(1)} %get-tuple-element.78), channel_id=1, source_target_pairs={{0,18},{2,16},{4,22},{6,20},{8,26},{10,24},{12,30},{14,28},{16,2},... | collective-permute-start | bytes 36872 | tf_op jit(solution)/shard_map/ppermute | solution.py:348
  58.4 8.7 %collective-permute-start.25 = (f32[24,128]{1,0:T(8,128)S(1)}, f32[24,128]{1,0:T(8,128)S(1)}, u32[]{:S(2)}, u32[]{:S(2)}) collective-permute-start(f32[24,128]{1,0:T(8,128)S(1)} %get-tuple-element.79), channel_id=1, source_target_pairs={{0,20},{2,22},{4,16},{6,18},{8,28},{10,30},{12,24},{14,26},{16,4},... | collective-permute-start | bytes 36872 | tf_op jit(solution)/shard_map/ppermute | solution.py:348
  58.4 14.2 %collective-permute-start.26 = (f32[24,128]{1,0:T(8,128)S(1)}, f32[24,128]{1,0:T(8,128)S(1)}, u32[]{:S(2)}, u32[]{:S(2)}) collective-permute-start(f32[24,128]{1,0:T(8,128)S(1)} %get-tuple-element.80), channel_id=1, source_target_pairs={{0,22},{2,20},{4,18},{6,16},{8,30},{10,28},{12,26},{14,24},{16,6},... | collective-permute-start | bytes 36872 | tf_op jit(solution)/shard_map/ppermute | solution.py:348
  63.1 9.5 %collective-permute-start.27 = (f32[24,128]{1,0:T(8,128)S(1)}, f32[24,128]{1,0:T(8,128)S(1)}, u32[]{:S(2)}, u32[]{:S(2)}) collective-permute-start(f32[24,128]{1,0:T(8,128)S(1)} %get-tuple-element.81), channel_id=1, source_target_pairs={{0,24},{2,26},{4,28},{6,30},{8,16},{10,18},{12,20},{14,22},{16,8},... | collective-permute-start | bytes 36872 | tf_op jit(solution)/shard_map/ppermute | solution.py:348
  63.3 9.2 %collective-permute-start.28 = (f32[24,128]{1,0:T(8,128)S(1)}, f32[24,128]{1,0:T(8,128)S(1)}, u32[]{:S(2)}, u32[]{:S(2)}) collective-permute-start(f32[24,128]{1,0:T(8,128)S(1)} %get-tuple-element.82), channel_id=1, source_target_pairs={{0,26},{2,24},{4,30},{6,28},{8,18},{10,16},{12,22},{14,20},{16,10}... | collective-permute-start | bytes 36872 | tf_op jit(solution)/shard_map/ppermute | solution.py:348
  66.9 6.4 %collective-permute-start.29 = (f32[24,128]{1,0:T(8,128)S(1)}, f32[24,128]{1,0:T(8,128)S(1)}, u32[]{:S(2)}, u32[]{:S(2)}) collective-permute-start(f32[24,128]{1,0:T(8,128)S(1)} %get-tuple-element.83), channel_id=1, source_target_pairs={{0,28},{2,30},{4,24},{6,26},{8,20},{10,22},{12,16},{14,18},{16,12}... | collective-permute-start | bytes 36872 | tf_op jit(solution)/shard_map/ppermute | solution.py:348
  67.1 7.3 %collective-permute-start.30 = (f32[24,128]{1,0:T(8,128)S(1)}, f32[24,128]{1,0:T(8,128)S(1)}, u32[]{:S(2)}, u32[]{:S(2)}) collective-permute-start(f32[24,128]{1,0:T(8,128)S(1)} %get-tuple-element.84), channel_id=1, source_target_pairs={{0,30},{2,28},{4,26},{6,24},{8,22},{10,20},{12,18},{14,16},{16,14}... | collective-permute-start | bytes 36872 | tf_op jit(solution)/shard_map/ppermute | solution.py:348
  75.8 1.8 %collective-permute-start.31 = (f32[768,128]{1,0:T(8,128)S(1)}, f32[768,128]{1,0:T(8,128)S(1)}, u32[]{:S(2)}, u32[]{:S(2)}) collective-permute-start(f32[768,128]{1,0:T(8,128)S(1)} %get-tuple-element.89), channel_id=1, source_target_pairs={{1,0},{0,1},{3,2},{2,3},{5,4},{4,5},{7,6},{6,7},{9,8},{8,9},{11,10... | collective-permute-start | bytes 1179656 | tf_op jit(solution)/shard_map/ppermute | solution.py:430
where the time goes:
time: 78.7 us; the launch traced here: 78.4 us
  starting transfers between devices  54.6 us (69%)
  waiting for transfers between devices  9.06 us (12%)
  local copies, waits for them, and re-layouts  6.49 us (8%)
  Pallas kernels  6.36 us (8%)
  other arithmetic  0.98 us (1%)
  between operations  0.86 us (1%)
    ppermute x30, starting transfers between devices, exchange(): lax.ppermute(blocks[step], 'clus', [(i, i ^ step) for i in range(devices)])  54 us
    ppermute x30, waiting for transfers between devices, exchange(): lax.ppermute(blocks[step], 'clus', [(i, i ^ step) for i in range(devices)])  8.26 us
    pallas_call x5, Pallas kernels, call(): pl.pallas_call(kernel, out_shape=outs, in_specs=[pl.BlockSpec(memory_spac...  6.36 us
    unnamed x21, local copies, waits for them, and re-layouts  5.4 us
  transfers between devices with their start and end apart: 32, of which 5 were waited for; matrix products, arithmetic and copies ran while one was open for 3% of the time, Pallas kernels for 3%

commit v1 on v0

--- a/solution.py
+++ b/solution.py
@@ -359,7 +359,7 @@
     blocks, rows_all = columns // TILE, groups * rows
     long, tall = children * own, OCTANTS * rows_all
     sources = 2 if halves == 2 else 3
-    relative = devices & (devices - 1) == 0 and devices <= 16 and (rows_all % 8 == 0)
+    relative = False
     struct = jax.ShapeDtypeStruct
 
     field = child_patterns.reshape(children, 2, own, blocks, TILE).transpose(0, 2, 3, 1, 4).reshape(long * blocks * 2, TILE)

time: 78.7 us -> 49 us (0.62)
  starting transfers between devices: 54.6 us -> 8.47 us
  blocking collectives: 0 us -> 11.6 us
  local copies, waits for them, and re-layouts: 6.49 us -> 11.9 us
  waiting for transfers between devices: 9.06 us -> 7.73 us
    ppermute x30 -> x0, starting transfers between devices: 54 us -> none  [exchange(): lax.ppermute(blocks[step], 'clus', [(i, i ^ step) for i in range(devices)])]
    all_to_all x0 -> x1, blocking collectives: none -> 11.6 us  [exchange(): lax.all_to_all(blocks[0], 'clus', split_axis=0, concat_axis=0, tiled=True)]
    ppermute x30 -> x0, waiting for transfers between devices: 8.26 us -> none  [exchange(): lax.ppermute(blocks[step], 'clus', [(i, i ^ step) for i in range(devices)])]
    all_to_all x0 -> x1, starting transfers between devices: none -> 7.88 us  [exchange(): lax.all_to_all(blocks[0], 'clus', split_axis=0, concat_axis=0, tiled=True)]
    all_to_all x0 -> x1, waiting for transfers between devices: none -> 6.93 us  [exchange(): lax.all_to_all(blocks[0], 'clus', split_axis=0, concat_axis=0, tiled=True)]
    unnamed x21 -> x29, local copies, waits for them, and re-layouts: 5.4 us -> 10.8 us
  transfers between devices with their start and end apart: 32 -> 3, of which waited for: 5 -> 2; matrix products, arithmetic and copies ran while one was open for 3% -> 8% of each run, Pallas kernels for 3% -> 5%
where the time goes in v1:
time: 49 us; the launch traced here: 48.4 us
  local copies, waits for them, and re-layouts  11.9 us (24%)
  blocking collectives  11.6 us (24%)
  starting transfers between devices  8.47 us (17%)
  waiting for transfers between devices  7.73 us (16%)
  Pallas kernels  6.95 us (14%)
  other arithmetic  0.98 us (2%)
  between operations  0.77 us (2%)
    all_to_all x1, blocking collectives, exchange(): lax.all_to_all(blocks[0], 'clus', split_axis=0, concat_axis=0, tiled=True)  11.6 us
    unnamed x29, local copies, waits for them, and re-layouts  10.8 us
    all_to_all x1, starting transfers between devices, exchange(): lax.all_to_all(blocks[0], 'clus', split_axis=0, concat_axis=0, tiled=True)  7.88 us
    pallas_call x5, Pallas kernels, call(): pl.pallas_call(kernel, out_shape=outs, in_specs=[pl.BlockSpec(memory_spac...  6.95 us
    all_to_all x1, waiting for transfers between devices, exchange(): lax.all_to_all(blocks[0], 'clus', split_axis=0, concat_axis=0, tiled=True)  6.93 us
    slice x1, local copies, waits for them, and re-layouts, per_device(): real, imag = (translation_table[:, 0], translation_table[:, 1])  1.05 us
  transfers between devices with their start and end apart: 3, of which 2 were waited for; matrix products, arithmetic and copies ran while one was open for 8% of the time, Pallas kernels for 5%

profile of v1, /device:TPU:0, one launch (start us, length us, event | category | flops | bytes accessed | tf_op | source)
XLA Modules:
  0.0 48.4 jit_solution(12778597627245570767)
XLA Ops:
  0.6 0.5 %collective-permute-start = (f32[768,128]{1,0:T(8,128)}, f32[768,128]{1,0:T(8,128)S(1)}, u32[]{:S(2)}, u32[]{:S(2)}) collective-permute-start(f32[768,128]{1,0:T(8,128)} %bitcast.31), channel_id=1, source_target_pairs={{0,1},{1,0},{2,3},{3,2},{4,5},{5,4},{6,7},{7,6},{8,9},{9,8},{10,11... | collective-permute-start | bytes 1179656 | tf_op jit(solution)/shard_map/ppermute | solution.py:366
  1.1 1.1 %fusion.1 = (f32[16,1,6,64]{3,1,2,0:T(1,128)S(1)}, f32[16,1,6,64]{3,1,2,0:T(1,128)S(1)}) fusion(f32[16,2,6,64]{3,1,2,0:T(2,128)} %param.13), kind=kLoop, calls=%fused_computation.8 | loop fusion | bytes 98304 | tf_op jit(solution)/shard_map/slice | solution.py:398
  2.2 0.8 %copy.20.listed_ref = s32[64,12]{1,0:T(8,128)S(1)} copy(s32[64,12]{0,1:T(8,128)} %param.14) | data formatting | bytes 6144 | tf_op args[6]
  3.0 0.8 %copy.21.vector_ref = s32[64,12]{1,0:T(8,128)S(1)} copy(s32[64,12]{0,1:T(8,128)} %param.15) | data formatting | bytes 6144 | tf_op args[7]
  3.8 0.0 copy-start.3
  3.8 0.9 %copy-done.3 = f32[8,6,1024]{2,0,1:T(8,128)S(1)} copy-done((f32[8,6,1024]{2,0,1:T(8,128)S(1)}, f32[8,6,1024]{2,0,1:T(8,128)}, u32[]{:S(2)}) %copy-start.3) | copy-done | bytes 196632
  4.7 0.0 copy-start.4
  4.7 0.8 %copy-done.4 = s32[1024,6]{0,1:T(8,128)S(1)} copy-done((s32[1024,6]{0,1:T(8,128)S(1)}, s32[1024,6]{0,1:T(8,128)}, u32[]{:S(2)}) %copy-start.4) | copy-done | bytes 24600
  5.5 0.0 copy-start.5
  5.5 0.8 %copy-done.5 = f32[1024,6]{0,1:T(8,128)S(1)} copy-done((f32[1024,6]{0,1:T(8,128)S(1)}, f32[1024,6]{0,1:T(8,128)}, u32[]{:S(2)}) %copy-start.5) | copy-done | bytes 24600
  6.2 0.0 copy-start.6
  6.2 0.7 %copy-done.6 = f32[6,9]{1,0:T(8,128)S(1)} copy-done((f32[6,9]{1,0:T(8,128)S(1)}, f32[6,9]{1,0:T(8,128)}, u32[]{:S(2)}) %copy-start.6) | copy-done | bytes 240
  6.9 1.8 %prepare.1 = (f32[8,24,1024]{2,1,0:T(8,128)S(1)}, f32[8,24,1024]{2,1,0:T(8,128)S(1)}, bf16[4,512,256]{2,1,0:T(8,128)(2,1)S(1)}, bf16[2,192,192]{2,1,0:T(8,128)(2,1)S(1)}, bf16[2,192,192]{2,1,0:T(8,128)(2,1)S(1)}) custom-call(f32[48,1024]{1,0:T(8,128)S(1)} %bitcast.33, s32[6,1024]{1,0:T(8,128)S(1)} %bitcast.34, f32[6,1024]{1,0:T(8,128)S(1)} %bitcast.35, ...), custom_call_target="tpu_custom_call" | custom-call | flops 200000000 | bytes 4505816 | tf_op jit(solution)/shard_map/prepare/pallas_call | solution.py:327
  8.7 0.0 copy-start.7
  8.7 0.0 copy-start.9
  8.8 0.1 copy_bitcast_fusion.1.even_ref
  8.9 0.0 collective-permute-done.refs_1_
  8.9 0.0 copy-start.2
  8.9 1.3 %copy-done.2 = f32[32,2,3,512]{3,1,2,0:T(2,128)S(1)} copy-done((f32[32,2,3,512]{3,1,2,0:T(2,128)S(1)}, f32[32,2,3,512]{3,1,2,0:T(2,128)}, u32[]{:S(2)}) %copy-start.2) | copy-done | bytes 393240
  10.2 2.1 %aggregate.1 = f32[16,24,128]{2,1,0:T(8,128)} custom-call(f32[768,128]{1,0:T(8,128)S(1)} %bitcast.32, f32[768,128]{1,0:T(8,128)S(1)} %collective-permute-done.refs_1_, f32[8,24,1024]{2,1,0:T(8,128)S(1)} %get-tuple-element.17.refs_2_.refs_1_, f32[8,24,1024]{2,1,0:T(8,128)S(1)} %get-tuple-element.18.refs_3_.refs_2_, ...), custom_call_target="tpu_custom_call" | custom-call | flops 1500000000 | bytes 4947968 | tf_op jit(solution)/shard_map/aggregate/pallas_call | solution.py:327
  12.3 0.0 copy-done.7
  12.3 0.0 copy-done.9
  12.3 0.0 copy-start.11
  12.3 0.9 %copy-done.11 = f32[8,24,1024]{2,1,0:T(8,128)} copy-done((f32[8,24,1024]{2,1,0:T(8,128)}, f32[8,24,1024]{2,1,0:T(8,128)S(1)}, u32[]{:S(2)}) %copy-start.11) | copy-done | bytes 786456
  13.2 7.9 %all-to-all-start = ((f32[16,24,128]{2,1,0:T(8,128)}), f32[16,24,128]{2,1,0:T(8,128)S(1)}, u32[]{:S(2)}, u32[]{:S(2)}) async-start(f32[16,24,128]{2,1,0:T(8,128)} %aggregate.1), calls=%async_computation | async-start | bytes 393216 | tf_op jit(solution)/shard_map/all_to_all | solution.py:345
  21.1 0.1 copy_bitcast_fusion.odd_ref
  21.1 0.8 %tables.1 = (bf16[768,192]{1,0:T(8,128)(2,1)S(1)}, f32[768,768]{1,0:T(8,128)S(1)}, f32[768,768]{1,0:T(8,128)S(1)}) custom-call(s32[64,12]{1,0:T(8,128)S(1)} %copy.20.listed_ref, s32[64,12]{1,0:T(8,128)S(1)} %copy.21.vector_ref, f32[16,768]{1,0:T(8,128)S(1)} %copy_bitcast_fusion.1.even_ref, f32[16,768]{1,0:T(8,128)S(1)} %copy_bitcast_fusion.odd_ref), custom_call_target="tpu_custom_call" | custom-call | flops 600000000 | bytes 5412864 | tf_op jit(solution)/shard_map/tables/pallas_call | solution.py:327
  22.0 0.0 copy-start
  22.0 1.4 %copy-done = f32[768,768]{1,0:T(8,128)} copy-done((f32[768,768]{1,0:T(8,128)}, f32[768,768]{1,0:T(8,128)S(1)}, u32[]{:S(2)}) %copy-start) | copy-done | bytes 2359320
  23.4 6.9 %all-to-all-done.refs_3_ = f32[16,24,128]{2,1,0:T(8,128)S(1)} async-done(((f32[16,24,128]{2,1,0:T(8,128)}), f32[16,24,128]{2,1,0:T(8,128)S(1)}, u32[]{:S(2)}, u32[]{:S(2)}) %all-to-all-start) | async-done | bytes 196640 | tf_op jit(solution)/shard_map/all_to_all | solution.py:345
  30.3 0.0 copy-start.1
  30.3 1.7 %copy-done.1 = f32[768,768]{1,0:T(8,128)S(1)} copy-done((f32[768,768]{1,0:T(8,128)S(1)}, f32[768,768]{1,0:T(8,128)}, u32[]{:S(2)}) %copy-start.1) | copy-done | bytes 2359320
  32.0 0.0 copy-start.8
  32.0 0.0 copy-start.10
  32.0 0.0 copy-start.12
  32.0 0.9 %translate.1 = f32[16,24,128]{2,1,0:T(8,128)S(1)} custom-call(bf16[768,192]{1,0:T(8,128)(2,1)S(1)} %get-tuple-element.14.refs_0_, f32[768,768]{1,0:T(8,128)S(1)} %get-tuple-element.15.refs_1_, f32[768,768]{1,0:T(8,128)S(1)} %copy-done.1, f32[16,24,128]{2,1,0:T(8,128)S(1)} %all-to-all-done.refs_3_), custom_call_target="tpu_custom_call" | custom-call | flops 600000000 | bytes 5701632 | tf_op jit(solution)/shard_map/translate/pallas_call | solution.py:327
  32.9 11.6 %all_to_all.10.refs_0_ = f32[16,24,128]{2,1,0:T(8,128)S(1)} all-to-all(f32[16,24,128]{2,1,0:T(8,128)S(1)} %translate.1), channel_id=1, replica_groups=mesh['clus'=16,'samp'=2] {'clus'}, dimensions={0} | all-to-all | bytes 393216 | tf_op jit(solution)/shard_map/all_to_all | solution.py:345
  44.5 0.0 copy-done.8
  44.5 0.0 copy-done.10
  44.5 0.0 copy-done.12
  44.5 1.3 %lower.1 = (f32[24,1024]{1,0:T(8,128)S(1)}, f32[24,1024]{1,0:T(8,128)S(1)}, f32[768,128]{1,0:T(8,128)S(1)}, f32[768,128]{1,0:T(8,128)S(1)}) custom-call(f32[16,24,128]{2,1,0:T(8,128)S(1)} %all_to_all.10.refs_0_, f32[8,24,1024]{2,1,0:T(8,128)S(1)} %copy-done.10, f32[8,24,1024]{2,1,0:T(8,128)S(1)} %copy-done.12, bf16[4,512,256]{2,1,0:T(8,128)(2,1)S(1)} %copy-done.8, ...), custom_call_target="tpu_custom_call" | custom-call | flops 1500000000 | bytes 5144576 | tf_op jit(solution)/shard_map/lower/pallas_call | solution.py:327
  45.8 0.1 collective-permute-start.1
  46.0 0.8 %copy.24 = f32[4,2,6,1024]{3,1,2,0:T(2,128)} copy(f32[4,2,6,1024]{3,2,0,1:T(8,128)S(1)} %pad_maximum_fusion) | data formatting | bytes 393216
  46.8 0.8 %collective-permute-done.1 = f32[768,128]{1,0:T(8,128)S(1)} collective-permute-done((f32[768,128]{1,0:T(8,128)S(1)}, f32[768,128]{1,0:T(8,128)S(1)}, u32[]{:S(2)}, u32[]{:S(2)}) %collective-permute-start.1) | collective-permute-done | bytes 393248 | tf_op jit(solution)/shard_map/ppermute | solution.py:430
  47.6 0.8 %add.3 = f32[768,128]{1,0:T(8,128)} add(f32[768,128]{1,0:T(8,128)S(1)} %get-tuple-element.24, f32[768,128]{1,0:T(8,128)S(1)} %collective-permute-done.1) | non-fusion elementwise | flops 98304 | bytes 1179648 | tf_op jit(solution)/shard_map/add | solution.py:430
  (5 shorter events, 0.1 us)
Async XLA Ops:
  0.6 8.2 %collective-permute-start = (f32[768,128]{1,0:T(8,128)}, f32[768,128]{1,0:T(8,128)S(1)}, u32[]{:S(2)}, u32[]{:S(2)}) collective-permute-start(f32[768,128]{1,0:T(8,128)} %bitcast.31), channel_id=1, source_target_pairs={{0,1},{1,0},{2,3},{3,2},{4,5},{5,4},{6,7},{7,6},{8,9},{9,8},{10,11... | collective-permute-start | bytes 1179656 | tf_op jit(solution)/shard_map/ppermute | solution.py:366
  3.8 0.9 %copy-start.3 = (f32[8,6,1024]{2,0,1:T(8,128)S(1)}, f32[8,6,1024]{2,0,1:T(8,128)}, u32[]{:S(2)}) copy-start(f32[8,6,1024]{2,0,1:T(8,128)} %param.12) | copy-start | bytes 589828
  4.7 0.8 %copy-start.4 = (s32[1024,6]{0,1:T(8,128)S(1)}, s32[1024,6]{0,1:T(8,128)}, u32[]{:S(2)}) copy-start(s32[1024,6]{0,1:T(8,128)} %param.10) | copy-start | bytes 73732
  5.5 0.8 %copy-start.5 = (f32[1024,6]{0,1:T(8,128)S(1)}, f32[1024,6]{0,1:T(8,128)}, u32[]{:S(2)}) copy-start(f32[1024,6]{0,1:T(8,128)} %param.11) | copy-start | bytes 73732
  6.2 0.7 %copy-start.6 = (f32[6,9]{1,0:T(8,128)S(1)}, f32[6,9]{1,0:T(8,128)}, u32[]{:S(2)}) copy-start(f32[6,9]{1,0:T(8,128)} %refs_3_.1) | copy-start | bytes 652
  8.7 3.5 %copy-start.7 = (bf16[4,512,256]{2,1,0:T(8,128)(2,1)}, bf16[4,512,256]{2,1,0:T(8,128)(2,1)S(1)}, u32[]{:S(2)}) copy-start(bf16[4,512,256]{2,1,0:T(8,128)(2,1)S(1)} %get-tuple-element.19.refs_4_.refs_3_) | copy-start | bytes 3145732
  8.7 3.5 %copy-start.9 = (f32[8,24,1024]{2,1,0:T(8,128)}, f32[8,24,1024]{2,1,0:T(8,128)S(1)}, u32[]{:S(2)}) copy-start(f32[8,24,1024]{2,1,0:T(8,128)S(1)} %get-tuple-element.17.refs_2_.refs_1_) | copy-start | bytes 2359300
  8.9 1.3 %copy-start.2 = (f32[32,2,3,512]{3,1,2,0:T(2,128)S(1)}, f32[32,2,3,512]{3,1,2,0:T(2,128)}, u32[]{:S(2)}) copy-start(f32[32,2,3,512]{3,1,2,0:T(2,128)} %param.8) | copy-start | bytes 1179652
  12.3 0.9 %copy-start.11 = (f32[8,24,1024]{2,1,0:T(8,128)}, f32[8,24,1024]{2,1,0:T(8,128)S(1)}, u32[]{:S(2)}) copy-start(f32[8,24,1024]{2,1,0:T(8,128)S(1)} %get-tuple-element.18.refs_3_.refs_2_) | copy-start | bytes 2359300
  13.2 17.2 %all-to-all-start = ((f32[16,24,128]{2,1,0:T(8,128)}), f32[16,24,128]{2,1,0:T(8,128)S(1)}, u32[]{:S(2)}, u32[]{:S(2)}) async-start(f32[16,24,128]{2,1,0:T(8,128)} %aggregate.1), calls=%async_computation | async-start | bytes 393216 | tf_op jit(solution)/shard_map/all_to_all | solution.py:345
  22.0 1.4 %copy-start = (f32[768,768]{1,0:T(8,128)}, f32[768,768]{1,0:T(8,128)S(1)}, u32[]{:S(2)}) copy-start(f32[768,768]{1,0:T(8,128)S(1)} %get-tuple-element.16.refs_2_) | copy-start | bytes 7077892
  30.3 1.7 %copy-start.1 = (f32[768,768]{1,0:T(8,128)S(1)}, f32[768,768]{1,0:T(8,128)}, u32[]{:S(2)}) copy-start(f32[768,768]{1,0:T(8,128)} %copy-done) | copy-start | bytes 7077892
  32.0 12.5 %copy-start.8 = (bf16[4,512,256]{2,1,0:T(8,128)(2,1)S(1)}, bf16[4,512,256]{2,1,0:T(8,128)(2,1)}, u32[]{:S(2)}) copy-start(bf16[4,512,256]{2,1,0:T(8,128)(2,1)} %copy-done.7) | copy-start | bytes 3145732
  32.0 12.5 %copy-start.10 = (f32[8,24,1024]{2,1,0:T(8,128)S(1)}, f32[8,24,1024]{2,1,0:T(8,128)}, u32[]{:S(2)}) copy-start(f32[8,24,1024]{2,1,0:T(8,128)} %copy-done.9) | copy-start | bytes 2359300
  32.0 12.5 %copy-start.12 = (f32[8,24,1024]{2,1,0:T(8,128)S(1)}, f32[8,24,1024]{2,1,0:T(8,128)}, u32[]{:S(2)}) copy-start(f32[8,24,1024]{2,1,0:T(8,128)} %copy-done.11) | copy-start | bytes 2359300
  45.8 1.8 %collective-permute-start.1 = (f32[768,128]{1,0:T(8,128)S(1)}, f32[768,128]{1,0:T(8,128)S(1)}, u32[]{:S(2)}, u32[]{:S(2)}) collective-permute-start(f32[768,128]{1,0:T(8,128)S(1)} %get-tuple-element.25), channel_id=1, source_target_pairs={{1,0},{0,1},{3,2},{2,3},{5,4},{4,5},{7,6},{6,7},{9,8},{8,9},{11,10... | collective-permute-start | bytes 1179656 | tf_op jit(solution)/shard_map/ppermute | solution.py:430

commit v2 on v1

v2 whole, which is shorter than its diff:
```python
import jax
import jax.numpy as jnp
from jax import lax
from jax.experimental import pallas as pl
from jax.experimental.pallas import tpu as pltpu
from jax.sharding import PartitionSpec as P

P_SIZE = 6
OCTANTS = 8
TILE = 128
PAIR = 2 * TILE
HALF = TILE // 2
VMEM_BYTES = 24 * 1024 * 1024
F32 = jnp.float32
BF16 = jnp.bfloat16

SIN_TERMS = (-1 / 6, 1 / 120, -1 / 5040, 1 / 362880, -1 / 39916800, 1 / 6227020800)
COS_TERMS = (-1 / 2, 1 / 24, -1 / 720, 1 / 40320, -1 / 3628800, 1 / 479001600, -1 / 87178291200)


def split_two(value):
    high = value.astype(BF16)
    return high, (value - high.astype(F32)).astype(BF16)


def split_three(value):
    high = value.astype(BF16)
    rest = value - high.astype(F32)
    middle = rest.astype(BF16)
    return high, middle, (rest - middle.astype(F32)).astype(BF16)


def product(left, right, left_dim=1, right_dim=0):
    return lax.dot_general(left, right, (((left_dim,), (right_dim,)), ((), ())), preferred_element_type=F32)


def product_exact(left, right, left_dim=1, right_dim=0):
    return lax.dot_general(
        left,
        right,
        (((left_dim,), (right_dim,)), ((), ())),
        preferred_element_type=F32,
        precision=lax.Precision.HIGHEST,
    )


def series(square, terms):
    total = jnp.full_like(square, terms[-1])
    for term in terms[-2::-1]:
        total = total * square + term
    return total


def iota(shape, dim):
    return lax.broadcasted_iota(jnp.int32, shape, dim)


def turned(block):
    return jnp.roll(block, HALF, axis=1)


def folded(theta, sources, own):
    below, middle, above = theta[:, :own], theta[:, own : 2 * own], theta[:, 2 * own :]
    return (middle, below + above) if sources == 2 else (middle, below, above)


def prepare_kernel(groups, sources, own, *refs):
    names = 8
    remote, outs, rest = refs[:names], refs[names : names + 8], refs[names + 8 :]
    local, cos_s, sin_s, sems = rest[:names], rest[names], rest[names + 1], rest[names + 2]
    copies = [pltpu.make_async_copy(source, target, sems.at[place]) for place, (source, target) in enumerate(zip(remote, local))]
    for copy in copies:
        copy.start()
    theta_ref, phase_ref, stencil_ref, weight_ref, listed_ref, vector_ref, table_ref, field_ref = local
    cos_ref, sin_ref, wide_ref, up_ref, down_ref, hot_ref, table_out, partial_ref = outs
    rows = theta_ref.shape[0]
    azimuth = phase_ref.shape[1]
    blocks = wide_ref.shape[0]
    tall, long = OCTANTS * groups * rows, groups * OCTANTS * own

    copies[0].wait()
    theta = theta_ref[...]
    for place, weights in enumerate(folded(theta, sources, own)):
        at_row = iota((tall, rows), 0) % rows == iota((tall, rows), 1)
        at_own = iota((own, long), 1) % own == iota((own, long), 0)
        spread = product_exact(product_exact(at_row.astype(F32), weights), at_own.astype(F32))
        tall_id = iota((tall, long), 0)
        same = iota((tall, long), 1) // own == (tall_id // rows) % groups * OCTANTS + tall_id // (groups * rows)
        high, low = split_two(jnp.where(same, spread, 0.0))
        up_ref[place, 0] = high
        up_ref[place, 1] = low
        at_row = iota((rows, tall), 1) % rows == iota((rows, tall), 0)
        at_own = iota((long, own), 0) % own == iota((long, own), 1)
        spread = product_exact(product_exact(at_own.astype(F32), weights, 1, 1), at_row.astype(F32))
        tall_id = iota((long, tall), 1)
        same = iota((long, tall), 0) // own == (tall_id // rows) % groups * OCTANTS + tall_id // (groups * rows)
        high, low = split_two(jnp.where(same, spread, 0.0))
        down_ref[place, 0] = high
        down_ref[place, 1] = low

    copies[1].wait()
    half = 0.5 * phase_ref[...]
    square = half * half
    sine = half + half * square * series(square, SIN_TERMS)
    cosine = 1.0 + square * series(square, COS_TERMS)
    for value, held, target in ((1.0 - 2.0 * sine * sine, cos_s, cos_ref), (2.0 * sine * cosine, sin_s, sin_ref)):
        for tile in range(azimuth // TILE):
            lanes = slice(tile * TILE, (tile + 1) * TILE)
            held[tile] = value[:, lanes]
            for octant in range(OCTANTS):
                part = held[tile, pl.ds(octant, rows, stride=OCTANTS), :]
                for group in range(groups):
                    target[octant, group * rows : (group + 1) * rows, lanes] = part

    copies[2].wait()
    copies[3].wait()
    for block in range(blocks):
        columns = slice(block * PAIR, (block + 1) * PAIR)
        after, before = (block + 1) % blocks, (block - 1) % blocks
        pieces = (
            (0, TILE, block * TILE),
            (TILE, 16, after * TILE),
            (PAIR - 16, 16, before * TILE + TILE - 16),
        )
        for start, size, first in pieces:
            child = iota((size, PAIR), 0) + first
            total = jnp.zeros((size, PAIR), F32)
            for point in range(P_SIZE):
                hit = stencil_ref[point : point + 1, columns] == child
                total = jnp.where(hit, weight_ref[point : point + 1, columns], total)
            high, low = split_two(total)
            wide_ref[block, start : start + size, :] = high
            wide_ref[block, PAIR + start : PAIR + start + size, :] = low
        empty = jnp.zeros((TILE - 32, PAIR), BF16)
        wide_ref[block, TILE + 16 : PAIR - 16, :] = empty
        wide_ref[block, PAIR + TILE + 16 : 2 * PAIR - 16, :] = empty

    copies[4].wait()
    copies[5].wait()
    partners, clusters = listed_ref.shape
    vectors = table_out.shape[1] // 3
    unit = (iota((clusters, clusters), 0) == iota((clusters, clusters), 1)).astype(F32)
    listed = product_exact(unit, listed_ref[...].astype(F32), 1, 1)
    chosen = product_exact(unit, vector_ref[...].astype(F32), 1, 1)
    cluster = (iota((clusters, 3 * clusters), 1) % clusters).astype(F32)
    vector = (iota((clusters, 3 * vectors), 1) % vectors).astype(F32)
    for partner in range(partners):
        part = slice(partner * clusters, (partner + 1) * clusters)
        hot_ref[part, : 3 * clusters] = (cluster == listed[:, partner : partner + 1]).astype(F32).astype(BF16)
        hot_ref[part, 3 * clusters :] = (vector == chosen[:, partner : partner + 1]).astype(F32).astype(BF16)

    copies[6].wait()
    raw = table_ref[...]
    width = raw.shape[1]
    many = raw.shape[0]
    at = iota((many, many), 1)
    row = iota((many, many), 0)
    order = at == row % vectors * (2 * rows) + row // (2 * vectors) * 2 + row // vectors % 2
    sorted_rows = product_exact(order.astype(F32), raw)
    lane = iota((width, 2 * width), 1)
    twice = (lane % width == iota((width, 2 * width), 0)).astype(F32)
    signed = jnp.where(lane < width, twice, -twice)
    even = product_exact(sorted_rows, twice)
    odd = product_exact(sorted_rows, signed)
    for row in range(rows):
        start = 2 * row * vectors
        for place, piece in enumerate(split_three(even[start : start + vectors])):
            table_out[row, place * vectors : (place + 1) * vectors, : 2 * width] = piece
        for place, piece in enumerate(split_three(odd[start + vectors : start + 2 * vectors])):
            table_out[row, place * vectors : (place + 1) * vectors, 2 * width :] = piece

    copies[7].wait()
    for part in range(2):
        partial_ref[part * tall : (part + 1) * tall, :] = polar(up_ref[0, 0], up_ref[0, 1], field_rows(field_ref, part, blocks, long))


def field_rows(field, part, blocks, long):
    return jnp.concatenate([field[pl.ds(2 * block + part, long, stride=2 * blocks), :] for block in range(blocks)], axis=1)


def polar(high_weights, low_weights, value):
    high, low = split_two(value)
    return product(high_weights, high) + (product(low_weights, high) + product(high_weights, low))


def packed_pieces(real, imag, columns):
    lane = iota((real.shape[0], TILE), 1)
    found = []
    if columns == HALF:
        for start in range(0, real.shape[1], TILE):
            a, b = real[:, start : start + TILE], imag[:, start : start + TILE]
            found.append(jnp.where(lane < HALF, a, turned(b)))
            found.append(jnp.where(lane < HALF, turned(a), b))
        return found
    for start in range(0, real.shape[1], columns):
        found.append(jnp.concatenate([real[:, start : start + columns], imag[:, start : start + columns]], axis=1))
    return found


def unpacked_pieces(read, devices, columns):
    if columns == HALF:
        real, imag = [], []
        for pair in range(devices // 2):
            a, b = read(2 * pair), read(2 * pair + 1)
            lane = iota(a.shape, 1)
            real.append(jnp.where(lane < HALF, a, turned(b)))
            imag.append(jnp.where(lane < HALF, turned(a), b))
        return jnp.concatenate(real, axis=1), jnp.concatenate(imag, axis=1)
    blocks = [read(device) for device in range(devices)]
    return (
        jnp.concatenate([block[:, :columns] for block in blocks], axis=1),
        jnp.concatenate([block[:, columns:] for block in blocks], axis=1),
    )


def aggregate_kernel(groups, sources, own, devices, *refs):
    fields = refs[: sources - 1]
    partial_ref, cos_ref, sin_ref, wide_ref, up_ref, out = refs[sources - 1 :]
    blocks = wide_ref.shape[0]
    rows_all = cos_ref.shape[1]
    columns = cos_ref.shape[2] // devices
    long, tall = groups * OCTANTS * own, OCTANTS * rows_all
    refined = []
    for part in range(2):
        value = partial_ref[part * tall : (part + 1) * tall, :]
        for place, field in enumerate(fields):
            value += polar(up_ref[place + 1, 0], up_ref[place + 1, 1], field_rows(field, part, blocks, long))
        refined.append(value)
    high, low = split_two(jnp.concatenate(refined, axis=0))
    lane = iota((2 * tall, TILE), 1)

    def windows(value, block):
        main = value[:, block * TILE : (block + 1) * TILE]
        after, before = (block + 1) % blocks, (block - 1) % blocks
        rim = jnp.where(lane < HALF, value[:, after * TILE : (after + 1) * TILE], value[:, before * TILE : (before + 1) * TILE])
        return [main, rim]

    for block in range(blocks):
        one, two = windows(high, block), windows(low, block)
        left = jnp.concatenate(one + two + one, axis=1)
        right = jnp.concatenate([wide_ref[block, :PAIR], wide_ref[block, :PAIR], wide_ref[block, PAIR:]], axis=0)
        spread = product(left, right)
        real = jnp.zeros((rows_all, PAIR), F32)
        imag = jnp.zeros((rows_all, PAIR), F32)
        for octant in range(OCTANTS):
            cosine = cos_ref[octant, :, block * PAIR : (block + 1) * PAIR]
            sine = sin_ref[octant, :, block * PAIR : (block + 1) * PAIR]
            a = spread[octant * rows_all : (octant + 1) * rows_all]
            b = spread[tall + octant * rows_all : tall + (octant + 1) * rows_all]
            real += a * cosine - b * sine
            imag += a * sine + b * cosine
        first = block * PAIR // columns
        for place, piece in enumerate(packed_pieces(real, imag, columns)):
            out[first + place] = piece


def translate_kernel(rows, hot_ref, table_ref, arrived_ref, out):
    width = arrived_ref.shape[1]
    clusters = arrived_ref.shape[0] // rows
    partners = hot_ref.shape[0] // clusters
    hot_cluster = hot_ref[:, : 3 * clusters]
    hot_vector = hot_ref[:, 3 * clusters :]
    step = 2 if rows % 2 == 0 else 1
    for first in range(0, rows, step):
        source = jnp.concatenate(
            [arrived_ref[pl.ds(row, clusters, stride=rows), :] for row in range(first, first + step)], axis=1
        )
        gathered = product(hot_cluster, jnp.concatenate(split_three(source), axis=0))
        for row in range(first, first + step):
            factors = product(hot_vector, table_ref[row])
            direct = jnp.zeros((clusters, width), F32)
            crossed = jnp.zeros((clusters, width), F32)
            for partner in range(partners):
                part = slice(partner * clusters, (partner + 1) * clusters)
                value = gathered[part, (row - first) * width : (row - first + 1) * width]
                direct += value * factors[part, :width]
                crossed += value * factors[part, width:]
            out[pl.ds(row, clusters, stride=rows), :] = direct + jnp.roll(crossed, width // 2, axis=1)


def lower_kernel(groups, sources, own, devices, arrived_ref, cos_ref, sin_ref, wide_ref, down_ref, parent_ref, *outs):
    blocks = wide_ref.shape[0]
    rows_all = cos_ref.shape[1]
    azimuth = cos_ref.shape[2]
    columns = azimuth // devices
    long, tall = groups * OCTANTS * own, OCTANTS * rows_all
    real, imag = unpacked_pieces(lambda device: arrived_ref[device], devices, columns)
    tiles = azimuth // TILE
    for tile in range(tiles):
        for part, value in enumerate((real, imag)):
            parent_ref[pl.ds(2 * tile + part, rows_all, stride=2 * tiles), :] = value[:, tile * TILE : (tile + 1) * TILE]
    mains, rims = [], []
    for block in range(blocks):
        part = slice(block * PAIR, (block + 1) * PAIR)
        a, b = real[:, part], imag[:, part]
        low_real, low_imag = [], []
        for octant in range(OCTANTS):
            cosine, sine = cos_ref[octant, :, part], sin_ref[octant, :, part]
            low_real.append(a * cosine + b * sine)
            low_imag.append(b * cosine - a * sine)
        high, low = split_two(jnp.concatenate(low_real + low_imag, axis=0))
        left = jnp.concatenate([high, low, high], axis=1)
        right = jnp.concatenate([wide_ref[block, :PAIR], wide_ref[block, :PAIR], wide_ref[block, PAIR:]], axis=1)
        both = product(left, right, 1, 1)
        mains.append(both[:, :TILE])
        rims.append(both[:, TILE:])
    lane = iota((2 * tall, TILE), 1)
    coarse = jnp.concatenate(
        [
            mains[block] + jnp.where(lane < HALF, rims[(block - 1) % blocks], rims[(block + 1) % blocks])
            for block in range(blocks)
        ],
        axis=1,
    )
    high, low = split_two(coarse)
    for place, out in enumerate(outs):
        up, fine = down_ref[place, 0], down_ref[place, 1]
        for part in range(2):
            rows = slice(part * tall, (part + 1) * tall)
            value = product(up, high[rows]) + (product(fine, high[rows]) + product(up, low[rows]))
            for block in range(blocks):
                out[pl.ds(2 * block + part, long, stride=2 * blocks), :] = value[:, block * TILE : (block + 1) * TILE]


def call(kernel, outs, args, flops, scratch=(), name=None, space=pltpu.VMEM):
    held = sum(4 * leaf.size for leaf in outs) + sum(4 * arg.size for arg in args)
    return pl.pallas_call(
        kernel,
        out_shape=outs,
        in_specs=[pl.BlockSpec(memory_space=space)] * len(args),
        out_specs=[pl.BlockSpec(memory_space=pltpu.VMEM)] * len(outs),
        scratch_shapes=list(scratch),
        compiler_params=pltpu.CompilerParams(vmem_limit_bytes=VMEM_BYTES),
        cost_estimate=pl.CostEstimate(flops=flops, bytes_accessed=held, transcendentals=0),
        name=name,
    )(*args)


def bind(kernel, *settings):
    return lambda *refs: kernel(*settings, *refs)


def exchange(blocks):
    return lax.all_to_all(blocks, "clus", split_axis=0, concat_axis=0, tiled=True)


def per_device(child_patterns, theta_weights, phi_stencil, phi_weights, shift_phase, translation_table, far_list, far_vector):
    devices, halves = lax.axis_size("clus"), lax.axis_size("samp")
    children, _, own, columns = child_patterns.shape
    groups = children // OCTANTS
    rows, azimuth = theta_weights.shape[0], phi_stencil.shape[0]
    clusters, partners = far_list.shape
    vectors, width = translation_table.shape[0], 2 * translation_table.shape[3]
    blocks, rows_all = columns // TILE, groups * rows
    long, tall = children * own, OCTANTS * rows_all
    sources = 2 if halves == 2 else 3
    struct = jax.ShapeDtypeStruct
    forward = [(i, (i + 1) % halves) for i in range(halves)]
    backward = [((i + 1) % halves, i) for i in range(halves)]

    field = child_patterns.reshape(children, 2, own, blocks, TILE).transpose(0, 2, 3, 1, 4).reshape(long * blocks * 2, TILE)
    neighbours = [lax.ppermute(field, "samp", forward)]
    if sources == 3:
        neighbours.append(lax.ppermute(field, "samp", backward))

    phase = shift_phase.transpose(1, 0, 2).reshape(rows * OCTANTS, azimuth)
    table = translation_table.transpose(0, 2, 1, 3).reshape(vectors * rows * 2, width // 2)
    given = [theta_weights, phase, phi_stencil.T, phi_weights.T, far_list.T, far_vector.T, table, field]
    given = [pltpu.with_memory_space_constraint(arg, pltpu.HBM) for arg in given]
    spread = pltpu.VMEM((azimuth // TILE, rows * OCTANTS, TILE), F32)
    cosine, sine, wide, up, down, hot, factors, partial = call(
        bind(prepare_kernel, groups, sources, own),
        [
            struct((OCTANTS, rows_all, azimuth), F32),
            struct((OCTANTS, rows_all, azimuth), F32),
            struct((blocks, 2 * PAIR, PAIR), BF16),
            struct((sources, 2, tall, long), BF16),
            struct((sources, 2, long, tall), BF16),
            struct((partners * clusters, 3 * clusters + 3 * vectors), BF16),
            struct((rows, 3 * vectors, 2 * width), BF16),
            struct((2 * tall, columns), F32),
        ],
        given,
        400_000_000,
        [pltpu.VMEM(arg.shape, arg.dtype) for arg in given] + [spread, spread, pltpu.SemaphoreType.DMA((len(given),))],
        "prepare",
        pltpu.HBM,
    )
    (outgoing,) = call(
        bind(aggregate_kernel, groups, sources, own, devices),
        [struct((devices, rows_all, width), F32)],
        [*neighbours, partial, cosine, sine, wide, up],
        1_500_000_000,
        (),
        "aggregate",
    )
    arrived = exchange(outgoing)
    (translated,) = call(
        bind(translate_kernel, rows),
        [struct((clusters * rows, width), F32)],
        [hot, factors, arrived.reshape(clusters * rows, width)],
        600_000_000,
        (),
        "translate",
    )
    returned = exchange(translated.reshape(devices, rows_all, width))
    parent, *children_parts = call(
        bind(lower_kernel, groups, sources, own, devices),
        [struct((rows_all * 2 * azimuth // TILE, TILE), F32)] + [struct((long * blocks * 2, TILE), F32)] * sources,
        [returned, cosine, sine, wide, down],
        1_500_000_000,
        (),
        "lower",
    )
    total = children_parts[0] + lax.ppermute(children_parts[1], "samp", backward)
    if sources == 3:
        total = total + lax.ppermute(children_parts[2], "samp", forward)
    child_incoming = total.reshape(children, own, blocks, 2, TILE).transpose(0, 3, 1, 2, 4).reshape(children, 2, own, columns)
    parent_incoming = (
        parent.reshape(groups, rows, azimuth // TILE, 2, TILE).transpose(0, 3, 1, 2, 4).reshape(groups, 2, rows, azimuth)
    )
    return (parent_incoming, child_incoming)


def solution(mesh):
    placed = (
        P("clus", None, "samp", None),
        P(),
        P(),
        P(),
        P(None, "samp", None),
        P(None, None, "samp", "clus"),
        P(),
        P(),
    )
    return jax.shard_map(
        per_device,
        mesh=mesh,
        in_specs=placed,
        out_specs=(P("clus", None, "samp", None), P("clus", None, "samp", None)),
        check_vma=False,
    )
```

time: 49 us -> 41 us (0.84)
  blocking collectives: 11.6 us -> 28.6 us
  local copies, waits for them, and re-layouts: 11.9 us -> 0 us
  starting transfers between devices: 8.47 us -> 0.59 us
  waiting for transfers between devices: 7.73 us -> 1.71 us
  Pallas kernels: 6.95 us -> 8.43 us
    all_to_all x1 -> x2, blocking collectives: 11.6 us -> 28.6 us  [exchange(): lax.all_to_all(blocks, 'clus', split_axis=0, concat_axis=0, tiled=True)]
    unnamed x29 -> x0, local copies, waits for them, and re-layouts: 10.8 us -> none
    all_to_all x1 -> x0, starting transfers between devices: 7.88 us -> none  [exchange(): lax.all_to_all(blocks[0], 'clus', split_axis=0, concat_axis=0, tiled=True)]
    all_to_all x1 -> x0, waiting for transfers between devices: 6.93 us -> none  [exchange(): lax.all_to_all(blocks[0], 'clus', split_axis=0, concat_axis=0, tiled=True)]
    pallas_call x5 -> x4, Pallas kernels: 6.95 us -> 8.43 us  [call(): pl.pallas_call(kernel, out_shape=outs, in_specs=[pl.BlockSpec(memory_spac...]
    slice x1 -> x0, local copies, waits for them, and re-layouts: 1.05 us -> none  [per_device(): real, imag = (translation_table[:, 0], translation_table[:, 1])]
    ppermute x2, waiting for transfers between devices: 0.8 us -> 1.71 us  [the longest x1 1.71 us: per_device(): lax.ppermute(children_parts[1], 'samp', backward)]
  transfers between devices with their start and end apart: 3 -> 2, of which waited for: 2 -> 1; matrix products, arithmetic and copies ran while one was open for 8% -> 0% of each run, Pallas kernels for 5% -> 11%
where the time goes in v2:
time: 41 us; the launch traced here: 40.8 us
  blocking collectives  28.6 us (70%)
  Pallas kernels  8.43 us (21%)
  waiting for transfers between devices  1.71 us (4%)
  other arithmetic  0.8 us (2%)
  between operations  0.68 us (2%)
  starting transfers between devices  0.59 us (1%)
    all_to_all x2, blocking collectives, exchange(): lax.all_to_all(blocks, 'clus', split_axis=0, concat_axis=0, tiled=True)  28.6 us
    pallas_call x4, Pallas kernels, call(): pl.pallas_call(kernel, out_shape=outs, in_specs=[pl.BlockSpec(memory_spac...  8.43 us
    ppermute x1, waiting for transfers between devices, per_device(): lax.ppermute(children_parts[1], 'samp', backward)  1.71 us
  transfers between devices with their start and end apart: 2, of which 1 were waited for; matrix products, arithmetic and copies ran while one was open for 0% of the time, Pallas kernels for 11%

profile of v2, /device:TPU:0, one launch (start us, length us, event | category | flops | bytes accessed | tf_op | source)
XLA Modules:
  0.0 40.8 jit_solution(15582560117719432371)
XLA Ops:
  0.6 0.5 %collective-permute-start = (f32[768,128]{1,0:T(8,128)}, f32[768,128]{1,0:T(8,128)S(1)}, u32[]{:S(2)}, u32[]{:S(2)}) collective-permute-start(f32[768,128]{1,0:T(8,128)} %bitcast.30), channel_id=1, source_target_pairs={{0,1},{1,0},{2,3},{3,2},{4,5},{5,4},{6,7},{7,6},{8,9},{9,8},{10,11... | collective-permute-start | bytes 1179656 | tf_op jit(solution)/shard_map/ppermute | solution.py:362
  1.2 4.5 %prepare.1 = (f32[8,24,1024]{2,1,0:T(8,128)S(1)}, f32[8,24,1024]{2,1,0:T(8,128)S(1)}, bf16[4,512,256]{2,1,0:T(8,128)(2,1)S(1)}, bf16[2,2,192,96]{3,2,1,0:T(8,128...) custom-call(f32[6,9]{1,0:T(8,128)} %refs_0_.1, ...), custom_call_target="tpu_custom_call" | custom-call | flops 400000000 | bytes 6772952 | tf_op jit(solution)/shard_map/prepare/pallas_call | solution.py:327
  5.7 0.0 collective-permute-done.refs_0_
  5.7 1.4 %aggregate.1 = f32[16,24,128]{2,1,0:T(8,128)S(1)} custom-call(f32[768,128]{1,0:T(8,128)S(1)} %collective-permute-done.refs_0_, f32[384,512]{1,0:T(8,128)S(1)} %get-tuple-element.15.refs_1_, f32[8,24,1024]{2,1,0:T(8,128)S(1)} %get-tuple-element.16.refs_2_.refs_1_, f32[8,24,1024]{2,1,0:T(8,128)S(1)} %get-tuple-element.17.refs_3_.refs_2_, ...), custom_call_target="tpu_custom_call" | custom-call | flops 1500000000 | bytes 5341184 | tf_op jit(solution)/shard_map/aggregate/pallas_call | solution.py:327
  7.1 17.0 %all_to_all.10 = f32[16,24,128]{2,1,0:T(8,128)S(1)} all-to-all(f32[16,24,128]{2,1,0:T(8,128)S(1)} %aggregate.1), channel_id=1, replica_groups=mesh['clus'=16,'samp'=2] {'clus'}, dimensions={0} | all-to-all | bytes 393216 | tf_op jit(solution)/shard_map/all_to_all | solution.py:344
  24.1 1.2 %translate.1 = f32[384,128]{1,0:T(8,128)S(1)} custom-call(bf16[768,240]{1,0:T(8,128)(2,1)S(1)} %get-tuple-element.13.refs_0_, bf16[6,48,256]{2,1,0:T(8,128)(2,1)S(1)} %get-tuple-element.14.refs_1_, f32[384,128]{1,0:T(8,128)S(1)} %bitcast.27), custom_call_target="tpu_custom_call" | custom-call | flops 600000000 | bytes 1425408 | tf_op jit(solution)/shard_map/translate/pallas_call | solution.py:327
  25.3 11.6 %all_to_all.11.refs_0_ = f32[16,24,128]{2,1,0:T(8,128)S(1)} all-to-all(f32[16,24,128]{2,1,0:T(8,128)S(1)} %bitcast.28), channel_id=1, replica_groups=mesh['clus'=16,'samp'=2] {'clus'}, dimensions={0} | all-to-all | bytes 393216 | tf_op jit(solution)/shard_map/all_to_all | solution.py:344
  36.9 1.3 %lower.1 = (f32[384,128]{1,0:T(8,128)}, f32[768,128]{1,0:T(8,128)S(1)}, f32[768,128]{1,0:T(8,128)S(1)}) custom-call(f32[16,24,128]{2,1,0:T(8,128)S(1)} %all_to_all.11.refs_0_, f32[8,24,1024]{2,1,0:T(8,128)S(1)} %get-tuple-element.16.refs_2_.refs_1_, f32[8,24,1024]{2,1,0:T(8,128)S(1)} %get-tuple-element.17.refs_3_.refs_2_, ...), custom_call_target="tpu_custom_call" | custom-call | flops 1500000000 | bytes 5144576 | tf_op jit(solution)/shard_map/lower/pallas_call | solution.py:327
  38.2 0.1 collective-permute-start.1
  38.3 1.7 %collective-permute-done.1 = f32[768,128]{1,0:T(8,128)S(1)} collective-permute-done((f32[768,128]{1,0:T(8,128)S(1)}, f32[768,128]{1,0:T(8,128)S(1)}, u32[]{:S(2)}, u32[]{:S(2)}) %collective-permute-start.1) | collective-permute-done | bytes 393248 | tf_op jit(solution)/shard_map/ppermute | solution.py:415
  40.0 0.8 %add.3 = f32[768,128]{1,0:T(8,128)} add(f32[768,128]{1,0:T(8,128)S(1)} %get-tuple-element.22, f32[768,128]{1,0:T(8,128)S(1)} %collective-permute-done.1) | non-fusion elementwise | flops 98304 | bytes 1179648 | tf_op jit(solution)/shard_map/add | solution.py:415
Async XLA Ops:
  0.6 5.1 %collective-permute-start = (f32[768,128]{1,0:T(8,128)}, f32[768,128]{1,0:T(8,128)S(1)}, u32[]{:S(2)}, u32[]{:S(2)}) collective-permute-start(f32[768,128]{1,0:T(8,128)} %bitcast.30), channel_id=1, source_target_pairs={{0,1},{1,0},{2,3},{3,2},{4,5},{5,4},{6,7},{7,6},{8,9},{9,8},{10,11... | collective-permute-start | bytes 1179656 | tf_op jit(solution)/shard_map/ppermute | solution.py:362
  38.2 1.8 %collective-permute-start.1 = (f32[768,128]{1,0:T(8,128)S(1)}, f32[768,128]{1,0:T(8,128)S(1)}, u32[]{:S(2)}, u32[]{:S(2)}) collective-permute-start(f32[768,128]{1,0:T(8,128)S(1)} %get-tuple-element.23), channel_id=1, source_target_pairs={{1,0},{0,1},{3,2},{2,3},{5,4},{4,5},{7,6},{6,7},{9,8},{8,9},{11,10... | collective-permute-start | bytes 1179656 | tf_op jit(solution)/shard_map/ppermute | solution.py:415

commit v3 on v2

--- a/solution.py
+++ b/solution.py
@@ -64,53 +64,56 @@
     return (middle, below + above) if sources == 2 else (middle, below, above)
 
 
-def prepare_kernel(groups, sources, own, *refs):
-    names = 8
-    remote, outs, rest = refs[:names], refs[names : names + 8], refs[names + 8 :]
-    local, cos_s, sin_s, sems = rest[:names], rest[names], rest[names + 1], rest[names + 2]
+def started(remote, local, sems):
     copies = [pltpu.make_async_copy(source, target, sems.at[place]) for place, (source, target) in enumerate(zip(remote, local))]
     for copy in copies:
         copy.start()
-    theta_ref, phase_ref, stencil_ref, weight_ref, listed_ref, vector_ref, table_ref, field_ref = local
-    cos_ref, sin_ref, wide_ref, up_ref, down_ref, hot_ref, table_out, partial_ref = outs
+    return copies
+
+
+def one_hot(flags):
+    return flags.astype(F32).astype(BF16)
+
+
+def halves_of(theta, sources, own):
+    high, low = split_two(jnp.concatenate(folded(theta, sources, own), axis=1))
+    return jnp.concatenate([high, low], axis=1)
+
+
+def prepare_kernel(groups, sources, own, *refs):
+    count = 5
+    remote, outs, rest = refs[:count], refs[count : count + 5], refs[count + 5 :]
+    local, sems = rest[:count], rest[count]
+    theta_ref, phase_ref, stencil_ref, weight_ref, field_ref = local
+    cos_ref, sin_ref, wide_ref, up_ref, partial_ref = outs
+    copies = started(remote, local, sems)
     rows = theta_ref.shape[0]
-    azimuth = phase_ref.shape[1]
     blocks = wide_ref.shape[0]
     tall, long = OCTANTS * groups * rows, groups * OCTANTS * own
 
+    lengths = 2 * sources * long
+    at_row = one_hot(iota((tall, rows), 0) % rows == iota((tall, rows), 1))
+    column = iota((2 * sources * own, lengths), 1)
+    at_own = one_hot(column // long * own + column % own == iota((2 * sources * own, lengths), 0))
+    tall_id = iota((tall, long), 0)
+    same = iota((tall, long), 1) // own == (tall_id // rows) % groups * OCTANTS + tall_id // (groups * rows)
+    shape = (tall, 3 * OCTANTS * rows)
+    place, phase_id = iota(shape, 0), iota(shape, 1) % (OCTANTS * rows)
+    repeat = one_hot(place % rows * OCTANTS + place // (groups * rows) == phase_id)
+
     copies[0].wait()
-    theta = theta_ref[...]
-    for place, weights in enumerate(folded(theta, sources, own)):
-        at_row = iota((tall, rows), 0) % rows == iota((tall, rows), 1)
-        at_own = iota((own, long), 1) % own == iota((own, long), 0)
-        spread = product_exact(product_exact(at_row.astype(F32), weights), at_own.astype(F32))
-        tall_id = iota((tall, long), 0)
-        same = iota((tall, long), 1) // own == (tall_id // rows) % groups * OCTANTS + tall_id // (groups * rows)
-        high, low = split_two(jnp.where(same, spread, 0.0))
-        up_ref[place, 0] = high
-        up_ref[place, 1] = low
-        at_row = iota((rows, tall), 1) % rows == iota((rows, tall), 0)
-        at_own = iota((long, own), 0) % own == iota((long, own), 1)
-        spread = product_exact(product_exact(at_own.astype(F32), weights, 1, 1), at_row.astype(F32))
-        tall_id = iota((long, tall), 1)
-        same = iota((long, tall), 0) // own == (tall_id // rows) % groups * OCTANTS + tall_id // (groups * rows)
-        high, low = split_two(jnp.where(same, spread, 0.0))
-        down_ref[place, 0] = high
-        down_ref[place, 1] = low
+    tall_theta = product(at_row, halves_of(theta_ref[...], sources, own)).astype(BF16)
+    spread = product(tall_theta, at_own)
+    for place in range(2 * sources):
+        up_ref[place % sources, place // sources] = jnp.where(same, spread[:, place * long : (place + 1) * long], 0.0).astype(BF16)
 
     copies[1].wait()
     half = 0.5 * phase_ref[...]
     square = half * half
     sine = half + half * square * series(square, SIN_TERMS)
     cosine = 1.0 + square * series(square, COS_TERMS)
-    for value, held, target in ((1.0 - 2.0 * sine * sine, cos_s, cos_ref), (2.0 * sine * cosine, sin_s, sin_ref)):
-        for tile in range(azimuth // TILE):
-            lanes = slice(tile * TILE, (tile + 1) * TILE)
-            held[tile] = value[:, lanes]
-            for octant in range(OCTANTS):
-                part = held[tile, pl.ds(octant, rows, stride=OCTANTS), :]
-                for group in range(groups):
-                    target[octant, group * rows : (group + 1) * rows, lanes] = part
+    cos_ref[...] = product(repeat, jnp.concatenate(split_three(1.0 - 2.0 * sine * sine), axis=0))
+    sin_ref[...] = product(repeat, jnp.concatenate(split_three(2.0 * sine * cosine), axis=0))
 
     copies[2].wait()
     copies[3].wait()
@@ -136,25 +139,37 @@
         wide_ref[block, PAIR + TILE + 16 : 2 * PAIR - 16, :] = empty
 
     copies[4].wait()
-    copies[5].wait()
-    partners, clusters = listed_ref.shape
-    vectors = table_out.shape[1] // 3
-    unit = (iota((clusters, clusters), 0) == iota((clusters, clusters), 1)).astype(F32)
-    listed = product_exact(unit, listed_ref[...].astype(F32), 1, 1)
-    chosen = product_exact(unit, vector_ref[...].astype(F32), 1, 1)
-    cluster = (iota((clusters, 3 * clusters), 1) % clusters).astype(F32)
-    vector = (iota((clusters, 3 * vectors), 1) % vectors).astype(F32)
-    for partner in range(partners):
-        part = slice(partner * clusters, (partner + 1) * clusters)
-        hot_ref[part, : 3 * clusters] = (cluster == listed[:, partner : partner + 1]).astype(F32).astype(BF16)
-        hot_ref[part, 3 * clusters :] = (vector == chosen[:, partner : partner + 1]).astype(F32).astype(BF16)
-
-    copies[6].wait()
+    for part in range(2):
+        partial_ref[part * tall : (part + 1) * tall, :] = polar(up_ref[0, 0], up_ref[0, 1], field_rows(field_ref, part, blocks, long))
+
+
+def tables_kernel(groups, sources, own, *refs):
+    count = 4
+    remote, outs, rest = refs[:count], refs[count + 1 : count + 5], refs[count + 5 :]
+    local, sems = rest[:count], rest[count]
+    theta_ref, listed_ref, vector_ref, table_ref = local
+    down_ref, hot_ref, even_ref, odd_ref = outs
+    copies = started(remote, local, sems)
+    rows = theta_ref.shape[0]
+    tall, long = OCTANTS * groups * rows, groups * OCTANTS * own
+
+    copies[0].wait()
+    lengths = 2 * sources * long
+    at_row = one_hot(iota((rows, tall), 1) % rows == iota((rows, tall), 0))
+    column = iota((lengths, 2 * sources * own), 0)
+    at_own = one_hot(column // long * own + column % own == iota((lengths, 2 * sources * own), 1))
+    tall_id = iota((long, tall), 1)
+    same = iota((long, tall), 0) // own == (tall_id // rows) % groups * OCTANTS + tall_id // (groups * rows)
+    own_theta = product(at_own, halves_of(theta_ref[...], sources, own), 1, 1).astype(BF16)
+    spread = product(own_theta, at_row)
+    for place in range(2 * sources):
+        down_ref[place % sources, place // sources] = jnp.where(same, spread[place * long : (place + 1) * long], 0.0).astype(BF16)
+
+    copies[3].wait()
     raw = table_ref[...]
-    width = raw.shape[1]
-    many = raw.shape[0]
-    at = iota((many, many), 1)
-    row = iota((many, many), 0)
+    many, width = raw.shape
+    vectors = many // (2 * rows)
+    at, row = iota((many, many), 1), iota((many, many), 0)
     order = at == row % vectors * (2 * rows) + row // (2 * vectors) * 2 + row // vectors % 2
     sorted_rows = product_exact(order.astype(F32), raw)
     lane = iota((width, 2 * width), 1)
@@ -162,16 +177,25 @@
     signed = jnp.where(lane < width, twice, -twice)
     even = product_exact(sorted_rows, twice)
     odd = product_exact(sorted_rows, signed)
+
+    copies[1].wait()
+    copies[2].wait()
+    partners, clusters = listed_ref.shape
+    unit = (iota((clusters, clusters), 0) == iota((clusters, clusters), 1)).astype(F32)
+    listed = product_exact(unit, listed_ref[...].astype(F32), 1, 1)
+    chosen = product_exact(unit, vector_ref[...].astype(F32), 1, 1)
+    cluster = (iota((clusters, 3 * clusters), 1) % clusters).astype(F32)
+    vector = (iota((clusters, 3 * vectors), 1) % vectors).astype(F32)
+    hot_vector = []
+    for partner in range(partners):
+        hot_ref[partner * clusters : (partner + 1) * clusters, :] = one_hot(cluster == listed[:, partner : partner + 1])
+        hot_vector.append(one_hot(vector == chosen[:, partner : partner + 1]))
+    hot_vector = jnp.concatenate(hot_vector, axis=0)
     for row in range(rows):
         start = 2 * row * vectors
-        for place, piece in enumerate(split_three(even[start : start + vectors])):
-            table_out[row, place * vectors : (place + 1) * vectors, : 2 * width] = piece
-        for place, piece in enumerate(split_three(odd[start + vectors : start + 2 * vectors])):
-            table_out[row, place * vectors : (place + 1) * vectors, 2 * width :] = piece
-
-    copies[7].wait()
-    for part in range(2):
-        partial_ref[part * tall : (part + 1) * tall, :] = polar(up_ref[0, 0], up_ref[0, 1], field_rows(field_ref, part, blocks, long))
+        columns = slice(row * 2 * width, (row + 1) * 2 * width)
+        even_ref[:, columns] = product(hot_vector, jnp.concatenate(split_three(even[start : start + vectors]), axis=0))
+        odd_ref[:, columns] = product(hot_vector, jnp.concatenate(split_three(odd[start + vectors : start + 2 * vectors]), axis=0))
 
 
 def field_rows(field, part, blocks, long):
@@ -217,8 +241,8 @@
     fields = refs[: sources - 1]
     partial_ref, cos_ref, sin_ref, wide_ref, up_ref, out = refs[sources - 1 :]
     blocks = wide_ref.shape[0]
-    rows_all = cos_ref.shape[1]
-    columns = cos_ref.shape[2] // devices
+    rows_all = cos_ref.shape[0] // OCTANTS
+    columns = cos_ref.shape[1] // devices
     long, tall = groups * OCTANTS * own, OCTANTS * rows_all
     refined = []
     for part in range(2):
@@ -243,9 +267,10 @@
         real = jnp.zeros((rows_all, PAIR), F32)
         imag = jnp.zeros((rows_all, PAIR), F32)
         for octant in range(OCTANTS):
-            cosine = cos_ref[octant, :, block * PAIR : (block + 1) * PAIR]
-            sine = sin_ref[octant, :, block * PAIR : (block + 1) * PAIR]
-            a = spread[octant * rows_all : (octant + 1) * rows_all]
+            rows = slice(octant * rows_all, (octant + 1) * rows_all)
+            cosine = cos_ref[rows, block * PAIR : (block + 1) * PAIR]
+            sine = sin_ref[rows, block * PAIR : (block + 1) * PAIR]
+            a = spread[rows]
             b = spread[tall + octant * rows_all : tall + (octant + 1) * rows_all]
             real += a * cosine - b * sine
             imag += a * sine + b * cosine
@@ -254,34 +279,32 @@
             out[first + place] = piece
 
 
-def translate_kernel(rows, hot_ref, table_ref, arrived_ref, out):
+def translate_kernel(rows, hot_ref, even_ref, odd_ref, arrived_ref, out):
     width = arrived_ref.shape[1]
     clusters = arrived_ref.shape[0] // rows
     partners = hot_ref.shape[0] // clusters
-    hot_cluster = hot_ref[:, : 3 * clusters]
-    hot_vector = hot_ref[:, 3 * clusters :]
     step = 2 if rows % 2 == 0 else 1
     for first in range(0, rows, step):
         source = jnp.concatenate(
             [arrived_ref[pl.ds(row, clusters, stride=rows), :] for row in range(first, first + step)], axis=1
         )
-        gathered = product(hot_cluster, jnp.concatenate(split_three(source), axis=0))
-        for row in range(first, first + step):
-            factors = product(hot_vector, table_ref[row])
-            direct = jnp.zeros((clusters, width), F32)
-            crossed = jnp.zeros((clusters, width), F32)
-            for partner in range(partners):
-                part = slice(partner * clusters, (partner + 1) * clusters)
-                value = gathered[part, (row - first) * width : (row - first + 1) * width]
-                direct += value * factors[part, :width]
-                crossed += value * factors[part, width:]
-            out[pl.ds(row, clusters, stride=rows), :] = direct + jnp.roll(crossed, width // 2, axis=1)
+        gathered = product(hot_ref[...], jnp.concatenate(split_three(source), axis=0))
+        columns = slice(first * width, (first + step) * width)
+        direct = jnp.zeros((clusters, step * width), F32)
+        crossed = jnp.zeros((clusters, step * width), F32)
+        for partner in range(partners):
+            part = slice(partner * clusters, (partner + 1) * clusters)
+            direct += gathered[part] * even_ref[part, columns]
+            crossed += gathered[part] * odd_ref[part, columns]
+        for row in range(step):
+            own = slice(row * width, (row + 1) * width)
+            out[pl.ds(first + row, clusters, stride=rows), :] = direct[:, own] + jnp.roll(crossed[:, own], width // 2, axis=1)
 
 
 def lower_kernel(groups, sources, own, devices, arrived_ref, cos_ref, sin_ref, wide_ref, down_ref, parent_ref, *outs):
     blocks = wide_ref.shape[0]
-    rows_all = cos_ref.shape[1]
-    azimuth = cos_ref.shape[2]
+    rows_all = cos_ref.shape[0] // OCTANTS
+    azimuth = cos_ref.shape[1]
     columns = azimuth // devices
     long, tall = groups * OCTANTS * own, OCTANTS * rows_all
     real, imag = unpacked_pieces(lambda device: arrived_ref[device], devices, columns)
@@ -295,7 +318,8 @@
         a, b = real[:, part], imag[:, part]
         low_real, low_imag = [], []
         for octant in range(OCTANTS):
-            cosine, sine = cos_ref[octant, :, part], sin_ref[octant, :, part]
+            rows = slice(octant * rows_all, (octant + 1) * rows_all)
+            cosine, sine = cos_ref[rows, part], sin_ref[rows, part]
             low_real.append(a * cosine + b * sine)
             low_imag.append(b * cosine - a * sine)
         high, low = split_two(jnp.concatenate(low_real + low_imag, axis=0))
@@ -322,18 +346,22 @@
                 out[pl.ds(2 * block + part, long, stride=2 * blocks), :] = value[:, block * TILE : (block + 1) * TILE]
 
 
-def call(kernel, outs, args, flops, scratch=(), name=None, space=pltpu.VMEM):
-    held = sum(4 * leaf.size for leaf in outs) + sum(4 * arg.size for arg in args)
+def call(kernel, outs, args, flops, name, remote=()):
+    held = sum(4 * leaf.size for leaf in outs) + sum(4 * arg.size for arg in (*remote, *args))
+    remote = [pltpu.with_memory_space_constraint(arg, pltpu.HBM) for arg in remote]
+    scratch = [pltpu.VMEM(arg.shape, arg.dtype) for arg in remote]
+    if remote:
+        scratch.append(pltpu.SemaphoreType.DMA((len(remote),)))
     return pl.pallas_call(
         kernel,
         out_shape=outs,
-        in_specs=[pl.BlockSpec(memory_space=space)] * len(args),
+        in_specs=[pl.BlockSpec(memory_space=pltpu.HBM)] * len(remote) + [pl.BlockSpec(memory_space=pltpu.VMEM)] * len(args),
         out_specs=[pl.BlockSpec(memory_space=pltpu.VMEM)] * len(outs),
-        scratch_shapes=list(scratch),
+        scratch_shapes=scratch,
         compiler_params=pltpu.CompilerParams(vmem_limit_bytes=VMEM_BYTES),
         cost_estimate=pl.CostEstimate(flops=flops, bytes_accessed=held, transcendentals=0),
         name=name,
-    )(*args)
+    )(*remote, *args)
 
 
 def bind(kernel, *settings):
@@ -365,42 +393,46 @@
 
     phase = shift_phase.transpose(1, 0, 2).reshape(rows * OCTANTS, azimuth)
     table = translation_table.transpose(0, 2, 1, 3).reshape(vectors * rows * 2, width // 2)
-    given = [theta_weights, phase, phi_stencil.T, phi_weights.T, far_list.T, far_vector.T, table, field]
-    given = [pltpu.with_memory_space_constraint(arg, pltpu.HBM) for arg in given]
-    spread = pltpu.VMEM((azimuth // TILE, rows * OCTANTS, TILE), F32)
-    cosine, sine, wide, up, down, hot, factors, partial = call(
+    cosine, sine, wide, up, partial = call(
         bind(prepare_kernel, groups, sources, own),
         [
-            struct((OCTANTS, rows_all, azimuth), F32),
-            struct((OCTANTS, rows_all, azimuth), F32),
+            struct((tall, azimuth), F32),
+            struct((tall, azimuth), F32),
             struct((blocks, 2 * PAIR, PAIR), BF16),
             struct((sources, 2, tall, long), BF16),
-            struct((sources, 2, long, tall), BF16),
-            struct((partners * clusters, 3 * clusters + 3 * vectors), BF16),
-            struct((rows, 3 * vectors, 2 * width), BF16),
             struct((2 * tall, columns), F32),
         ],
-        given,
+        [],
         400_000_000,
-        [pltpu.VMEM(arg.shape, arg.dtype) for arg in given] + [spread, spread, pltpu.SemaphoreType.DMA((len(given),))],
         "prepare",
-        pltpu.HBM,
+        [theta_weights, phase, phi_stencil.T, phi_weights.T, field],
     )
     (outgoing,) = call(
         bind(aggregate_kernel, groups, sources, own, devices),
         [struct((devices, rows_all, width), F32)],
         [*neighbours, partial, cosine, sine, wide, up],
         1_500_000_000,
-        (),
         "aggregate",
     )
     arrived = exchange(outgoing)
+    down, hot, even, odd = call(
+        bind(tables_kernel, groups, sources, own),
+        [
+            struct((sources, 2, long, tall), BF16),
+            struct((partners * clusters, 3 * clusters), BF16),
+            struct((partners * clusters, rows * width), F32),
+            struct((partners * clusters, rows * width), F32),
+        ],
+        [outgoing],
+        600_000_000,
+        "tables",
+        [theta_weights, far_list.T, far_vector.T, table],
+    )
     (translated,) = call(
         bind(translate_kernel, rows),
         [struct((clusters * rows, width), F32)],
-        [hot, factors, arrived.reshape(clusters * rows, width)],
+        [hot, even, odd, arrived.reshape(clusters * rows, width)],
         600_000_000,
-        (),
         "translate",
     )
     returned = exchange(translated.reshape(devices, rows_all, width))
@@ -409,7 +441,6 @@
         [struct((rows_all * 2 * azimuth // TILE, TILE), F32)] + [struct((long * blocks * 2, TILE), F32)] * sources,
         [returned, cosine, sine, wide, down],
         1_500_000_000,
-        (),
         "lower",
     )
     total = children_parts[0] + lax.ppermute(children_parts[1], "samp", backward)

time: 41 us -> 44.4 us (1.083)
  blocking collectives: 28.6 us -> 11.9 us
  starting transfers between devices: 0.59 us -> 8.46 us
  local copies, waits for them, and re-layouts: 0 us -> 5.86 us
  waiting for transfers between devices: 1.71 us -> 5.47 us
  Pallas kernels: 8.43 us -> 10.9 us
    all_to_all x2 -> x1, blocking collectives: 28.6 us -> 11.9 us  [exchange(): lax.all_to_all(blocks, 'clus', split_axis=0, concat_axis=0, tiled=True)]
    all_to_all x0 -> x1, starting transfers between devices: none -> 7.87 us  [exchange(): lax.all_to_all(blocks, 'clus', split_axis=0, concat_axis=0, tiled=True)]
    unnamed x0 -> x16, local copies, waits for them, and re-layouts: none -> 5.86 us
    all_to_all x0 -> x1, waiting for transfers between devices: none -> 3.75 us  [exchange(): lax.all_to_all(blocks, 'clus', split_axis=0, concat_axis=0, tiled=True)]
    pallas_call x4 -> x5, Pallas kernels: 8.43 us -> 10.9 us  [call(): pl.pallas_call(kernel, out_shape=outs, in_specs=[pl.BlockSpec(memory_spac...]
  transfers between devices with their start and end apart: 2 -> 3, of which waited for: 1 -> 2; matrix products, arithmetic and copies ran while one was open for 0% -> 0% of each run, Pallas kernels for 11% -> 15%
where the time goes in v3:
time: 44.4 us; the launch traced here: 44.1 us
  blocking collectives  11.9 us (27%)
  Pallas kernels  10.9 us (25%)
  starting transfers between devices  8.46 us (19%)
  local copies, waits for them, and re-layouts  5.86 us (13%)
  waiting for transfers between devices  5.47 us (12%)
  other arithmetic  0.8 us (2%)
  between operations  0.71 us (2%)
    all_to_all x1, blocking collectives, exchange(): lax.all_to_all(blocks, 'clus', split_axis=0, concat_axis=0, tiled=True)  11.9 us
    pallas_call x5, Pallas kernels, call(): pl.pallas_call(kernel, out_shape=outs, in_specs=[pl.BlockSpec(memory_spac...  10.9 us
    all_to_all x1, starting transfers between devices, exchange(): lax.all_to_all(blocks, 'clus', split_axis=0, concat_axis=0, tiled=True)  7.87 us
    unnamed x16, local copies, waits for them, and re-layouts  5.86 us
    all_to_all x1, waiting for transfers between devices, exchange(): lax.all_to_all(blocks, 'clus', split_axis=0, concat_axis=0, tiled=True)  3.75 us
    ppermute x1, waiting for transfers between devices, per_device(): lax.ppermute(children_parts[1], 'samp', backward)  1.71 us
  transfers between devices with their start and end apart: 3, of which 2 were waited for; matrix products, arithmetic and copies ran while one was open for 0% of the time, Pallas kernels for 15%

profile of v3, /device:TPU:0, one launch (start us, length us, event | category | flops | bytes accessed | tf_op | source)
XLA Modules:
  0.0 44.1 jit_solution(733588482658973197)
XLA Ops:
  0.6 0.5 %collective-permute-start = (f32[768,128]{1,0:T(8,128)}, f32[768,128]{1,0:T(8,128)S(1)}, u32[]{:S(2)}, u32[]{:S(2)}) collective-permute-start(f32[768,128]{1,0:T(8,128)} %bitcast.30), channel_id=1, source_target_pairs={{0,1},{1,0},{2,3},{3,2},{4,5},{5,4},{6,7},{7,6},{8,9},{9,8},{10,11... | collective-permute-start | bytes 1179656 | tf_op jit(solution)/shard_map/ppermute | solution.py:390
  1.1 2.7 %prepare.1 = (f32[192,1024]{1,0:T(8,128)S(1)}, f32[192,1024]{1,0:T(8,128)S(1)}, bf16[4,512,256]{2,1,0:T(8,128)(2,1)S(1)}, bf16[2,2,192,96]{3,2,1,0:T(8,128)(2,1)S(1)}, f32[384,512]{1,0:T(8,128)S(1)}) custom-call(f32[6,9]{1,0:T(8,128)} %refs_0_.3, f32[48,1024]{1,0:T(8,128)} %bitcast.32, s32[6,1024]{1,0:T(8,128)} %bitcast.34, f32[6,1024]{1,0:T(8,128)} %bitcast.35, ...), custom_call_target="tpu_custom_call" | custom-call | flops 400000000 | bytes 5390552 | tf_op jit(solution)/shard_map/prepare/pallas_call | solution.py:355
  3.9 0.0 collective-permute-done.refs_0_
  3.9 2.0 %aggregate.1.refs_4_ = f32[16,24,128]{2,1,0:T(8,128)} custom-call(f32[768,128]{1,0:T(8,128)S(1)} %collective-permute-done.refs_0_, f32[384,512]{1,0:T(8,128)S(1)} %get-tuple-element.14.refs_1_, f32[192,1024]{1,0:T(8,128)S(1)} %get-tuple-element.15.refs_2_.refs_1_, f32[192,1024]{1,0:T(8,128)S(1)} %get-tuple-element.16.refs_3_.refs_2_, ...), custom_call_target="tpu_custom_call" | custom-call | flops 1500000000 | bytes 5341184 | tf_op jit(solution)/shard_map/aggregate/pallas_call | solution.py:355
  5.9 0.0 copy-start.2
  5.9 1.0 %copy-done.2 = bf16[4,512,256]{2,1,0:T(8,128)(2,1)} copy-done((bf16[4,512,256]{2,1,0:T(8,128)(2,1)}, bf16[4,512,256]{2,1,0:T(8,128)(2,1)S(1)}, u32[]{:S(2)}) %copy-start.2) | copy-done | bytes 1048600
  6.9 0.0 copy-start.4
  6.9 0.9 %copy-done.4 = f32[192,1024]{1,0:T(8,128)} copy-done((f32[192,1024]{1,0:T(8,128)}, f32[192,1024]{1,0:T(8,128)S(1)}, u32[]{:S(2)}) %copy-start.4) | copy-done | bytes 786456
  7.8 0.0 copy-start.6
  7.8 0.9 %copy-done.6 = f32[192,1024]{1,0:T(8,128)} copy-done((f32[192,1024]{1,0:T(8,128)}, f32[192,1024]{1,0:T(8,128)S(1)}, u32[]{:S(2)}) %copy-start.6) | copy-done | bytes 786456
  8.7 7.9 %all-to-all-start = ((f32[16,24,128]{2,1,0:T(8,128)}), f32[16,24,128]{2,1,0:T(8,128)S(1)}, u32[]{:S(2)}, u32[]{:S(2)}) async-start(f32[16,24,128]{2,1,0:T(8,128)} %aggregate.1.refs_4_), calls=%async_computation | async-start | bytes 393216 | tf_op jit(solution)/shard_map/all_to_all | solution.py:372
  16.6 4.1 %tables.1 = (bf16[2,2,96,192]{3,2,1,0:T(8,128)(2,1)S(1)}, bf16[768,192]{1,0:T(8,128)(2,1)S(1)}, f32[768,768]{1,0:T(8,128)S(1)}, f32[768,768]{1,0:T(8,128)S(1)}) custom-call(f32[6,9]{1,0:T(8,128)} %refs_0_.3, s32[12,64]{1,0:T(8,128)} %bitcast.36, s32[12,64]{1,0:T(8,128)} %bitcast.37, f32[192,64]{1,0:T(8,128)} %bitcast.33, f32[16,24,128]{2,1,0:T(8,128)} %aggregate.1.refs_4_), custom_call_target="tpu_custom_call" | custom-call | flops 600000000 | bytes 5855448 | tf_op jit(solution)/shard_map/tables/pallas_call | solution.py:355
  20.7 0.0 copy-start
  20.7 1.4 %copy-done = f32[768,768]{1,0:T(8,128)} copy-done((f32[768,768]{1,0:T(8,128)}, f32[768,768]{1,0:T(8,128)S(1)}, u32[]{:S(2)}) %copy-start) | copy-done | bytes 2359320
  22.1 3.8 %all-to-all-done = f32[16,24,128]{2,1,0:T(8,128)S(1)} async-done(((f32[16,24,128]{2,1,0:T(8,128)}), f32[16,24,128]{2,1,0:T(8,128)S(1)}, u32[]{:S(2)}, u32[]{:S(2)}) %all-to-all-start) | async-done | bytes 196640 | tf_op jit(solution)/shard_map/all_to_all | solution.py:372
  25.9 0.0 copy-start.1
  25.9 1.7 %copy-done.1 = f32[768,768]{1,0:T(8,128)S(1)} copy-done((f32[768,768]{1,0:T(8,128)S(1)}, f32[768,768]{1,0:T(8,128)}, u32[]{:S(2)}) %copy-start.1) | copy-done | bytes 2359320
  27.5 0.0 copy-start.3
  27.5 0.0 copy-start.5
  27.5 0.0 copy-start.7
  27.5 0.7 %translate.1 = f32[384,128]{1,0:T(8,128)S(1)} custom-call(bf16[768,192]{1,0:T(8,128)(2,1)S(1)} %get-tuple-element.19.refs_0_, f32[768,768]{1,0:T(8,128)S(1)} %get-tuple-element.20.refs_1_, f32[768,768]{1,0:T(8,128)S(1)} %copy-done.1, f32[384,128]{1,0:T(8,128)S(1)} %bitcast.27), custom_call_target="tpu_custom_call" | custom-call | flops 600000000 | bytes 5701632 | tf_op jit(solution)/shard_map/translate/pallas_call | solution.py:355
  28.2 11.9 %all_to_all.10.refs_0_ = f32[16,24,128]{2,1,0:T(8,128)S(1)} all-to-all(f32[16,24,128]{2,1,0:T(8,128)S(1)} %bitcast.28), channel_id=1, replica_groups=mesh['clus'=16,'samp'=2] {'clus'}, dimensions={0} | all-to-all | bytes 393216 | tf_op jit(solution)/shard_map/all_to_all | solution.py:372
  40.1 0.0 copy-done.3
  40.1 0.0 copy-done.5
  40.1 0.0 copy-done.7
  40.1 1.3 %lower.1 = (f32[384,128]{1,0:T(8,128)}, f32[768,128]{1,0:T(8,128)S(1)}, f32[768,128]{1,0:T(8,128)S(1)}) custom-call(f32[16,24,128]{2,1,0:T(8,128)S(1)} %all_to_all.10.refs_0_, f32[192,1024]{1,0:T(8,128)S(1)} %copy-done.5, f32[192,1024]{1,0:T(8,128)S(1)} %copy-done.7, bf16[4,512,256]{2,1,0:T(8,128)(2,1)S(1)} %copy-done.3, ...), custom_call_target="tpu_custom_call" | custom-call | flops 1500000000 | bytes 5144576 | tf_op jit(solution)/shard_map/lower/pallas_call | solution.py:355
  41.5 0.1 collective-permute-start.1
  41.6 1.7 %collective-permute-done.1 = f32[768,128]{1,0:T(8,128)S(1)} collective-permute-done((f32[768,128]{1,0:T(8,128)S(1)}, f32[768,128]{1,0:T(8,128)S(1)}, u32[]{:S(2)}, u32[]{:S(2)}) %collective-permute-start.1) | collective-permute-done | bytes 393248 | tf_op jit(solution)/shard_map/ppermute | solution.py:446
  43.3 0.8 %add.3 = f32[768,128]{1,0:T(8,128)} add(f32[768,128]{1,0:T(8,128)S(1)} %get-tuple-element.24, f32[768,128]{1,0:T(8,128)S(1)} %collective-permute-done.1) | non-fusion elementwise | flops 98304 | bytes 1179648 | tf_op jit(solution)/shard_map/add | solution.py:446
Async XLA Ops:
  0.6 3.2 %collective-permute-start = (f32[768,128]{1,0:T(8,128)}, f32[768,128]{1,0:T(8,128)S(1)}, u32[]{:S(2)}, u32[]{:S(2)}) collective-permute-start(f32[768,128]{1,0:T(8,128)} %bitcast.30), channel_id=1, source_target_pairs={{0,1},{1,0},{2,3},{3,2},{4,5},{5,4},{6,7},{7,6},{8,9},{9,8},{10,11... | collective-permute-start | bytes 1179656 | tf_op jit(solution)/shard_map/ppermute | solution.py:390
  5.9 1.0 %copy-start.2 = (bf16[4,512,256]{2,1,0:T(8,128)(2,1)}, bf16[4,512,256]{2,1,0:T(8,128)(2,1)S(1)}, u32[]{:S(2)}) copy-start(bf16[4,512,256]{2,1,0:T(8,128)(2,1)S(1)} %get-tuple-element.17.refs_4_.refs_3_) | copy-start | bytes 3145732
  6.9 0.9 %copy-start.4 = (f32[192,1024]{1,0:T(8,128)}, f32[192,1024]{1,0:T(8,128)S(1)}, u32[]{:S(2)}) copy-start(f32[192,1024]{1,0:T(8,128)S(1)} %get-tuple-element.15.refs_2_.refs_1_) | copy-start | bytes 2359300
  7.8 0.9 %copy-start.6 = (f32[192,1024]{1,0:T(8,128)}, f32[192,1024]{1,0:T(8,128)S(1)}, u32[]{:S(2)}) copy-start(f32[192,1024]{1,0:T(8,128)S(1)} %get-tuple-element.16.refs_3_.refs_2_) | copy-start | bytes 2359300
  8.7 17.2 %all-to-all-start = ((f32[16,24,128]{2,1,0:T(8,128)}), f32[16,24,128]{2,1,0:T(8,128)S(1)}, u32[]{:S(2)}, u32[]{:S(2)}) async-start(f32[16,24,128]{2,1,0:T(8,128)} %aggregate.1.refs_4_), calls=%async_computation | async-start | bytes 393216 | tf_op jit(solution)/shard_map/all_to_all | solution.py:372
  20.7 1.4 %copy-start = (f32[768,768]{1,0:T(8,128)}, f32[768,768]{1,0:T(8,128)S(1)}, u32[]{:S(2)}) copy-start(f32[768,768]{1,0:T(8,128)S(1)} %get-tuple-element.21.refs_2_) | copy-start | bytes 7077892
  25.9 1.7 %copy-start.1 = (f32[768,768]{1,0:T(8,128)S(1)}, f32[768,768]{1,0:T(8,128)}, u32[]{:S(2)}) copy-start(f32[768,768]{1,0:T(8,128)} %copy-done) | copy-start | bytes 7077892
  27.5 12.6 %copy-start.3 = (bf16[4,512,256]{2,1,0:T(8,128)(2,1)S(1)}, bf16[4,512,256]{2,1,0:T(8,128)(2,1)}, u32[]{:S(2)}) copy-start(bf16[4,512,256]{2,1,0:T(8,128)(2,1)} %copy-done.2) | copy-start | bytes 3145732
  27.5 12.6 %copy-start.5 = (f32[192,1024]{1,0:T(8,128)S(1)}, f32[192,1024]{1,0:T(8,128)}, u32[]{:S(2)}) copy-start(f32[192,1024]{1,0:T(8,128)} %copy-done.4) | copy-start | bytes 2359300
  27.5 12.6 %copy-start.7 = (f32[192,1024]{1,0:T(8,128)S(1)}, f32[192,1024]{1,0:T(8,128)}, u32[]{:S(2)}) copy-start(f32[192,1024]{1,0:T(8,128)} %copy-done.6) | copy-start | bytes 2359300
  41.5 1.8 %collective-permute-start.1 = (f32[768,128]{1,0:T(8,128)S(1)}, f32[768,128]{1,0:T(8,128)S(1)}, u32[]{:S(2)}, u32[]{:S(2)}) collective-permute-start(f32[768,128]{1,0:T(8,128)S(1)} %get-tuple-element.25), channel_id=1, source_target_pairs={{1,0},{0,1},{3,2},{2,3},{5,4},{4,5},{7,6},{6,7},{9,8},{8,9},{11,10... | collective-permute-start | bytes 1179656 | tf_op jit(solution)/shard_map/ppermute | solution.py:446

commit v4 on v3

--- a/solution.py
+++ b/solution.py
@@ -10,7 +10,7 @@
 TILE = 128
 PAIR = 2 * TILE
 HALF = TILE // 2
-VMEM_BYTES = 24 * 1024 * 1024
+VMEM_BYTES = 8 * 1024 * 1024
 F32 = jnp.float32
 BF16 = jnp.bfloat16
 
@@ -32,16 +32,6 @@
 
 def product(left, right, left_dim=1, right_dim=0):
     return lax.dot_general(left, right, (((left_dim,), (right_dim,)), ((), ())), preferred_element_type=F32)
-
-
-def product_exact(left, right, left_dim=1, right_dim=0):
-    return lax.dot_general(
-        left,
-        right,
-        (((left_dim,), (right_dim,)), ((), ())),
-        preferred_element_type=F32,
-        precision=lax.Precision.HIGHEST,
-    )
 
 
 def series(square, terms):
@@ -145,10 +135,10 @@
 
 def tables_kernel(groups, sources, own, *refs):
     count = 4
-    remote, outs, rest = refs[:count], refs[count + 1 : count + 5], refs[count + 5 :]
+    remote, outs, rest = refs[:count], refs[count + 1 : count + 4], refs[count + 4 :]
     local, sems = rest[:count], rest[count]
     theta_ref, listed_ref, vector_ref, table_ref = local
-    down_ref, hot_ref, even_ref, odd_ref = outs
+    down_ref, hot_ref, table_out = outs
     copies = started(remote, local, sems)
     rows = theta_ref.shape[0]
     tall, long = OCTANTS * groups * rows, groups * OCTANTS * own
@@ -169,33 +159,30 @@
     raw = table_ref[...]
     many, width = raw.shape
     vectors = many // (2 * rows)
-    at, row = iota((many, many), 1), iota((many, many), 0)
-    order = at == row % vectors * (2 * rows) + row // (2 * vectors) * 2 + row // vectors % 2
-    sorted_rows = product_exact(order.astype(F32), raw)
-    lane = iota((width, 2 * width), 1)
-    twice = (lane % width == iota((width, 2 * width), 0)).astype(F32)
-    signed = jnp.where(lane < width, twice, -twice)
-    even = product_exact(sorted_rows, twice)
-    odd = product_exact(sorted_rows, signed)
+    at, place = iota((many, many), 1), iota((many, many), 0)
+    order = one_hot(at == place % vectors * (2 * rows) + place // (2 * vectors) * 2 + place // vectors % 2)
+    lane, source = iota((width, 4 * width), 1), iota((width, 4 * width), 0)
+    twice = jnp.where(lane % width == source, jnp.where(lane < 3 * width, 1.0, -1.0), 0.0).astype(BF16)
+    for piece, part in enumerate(split_three(raw)):
+        wide = product(product(order, part).astype(BF16), twice).astype(BF16)
+        for row in range(rows):
+            start = 2 * row * vectors
+            target = slice(piece * vectors, (piece + 1) * vectors)
+            table_out[row, target, : 2 * width] = wide[start : start + vectors, : 2 * width]
+            table_out[row, target, 2 * width :] = wide[start + vectors : start + 2 * vectors, 2 * width :]
 
     copies[1].wait()
     copies[2].wait()
     partners, clusters = listed_ref.shape
-    unit = (iota((clusters, clusters), 0) == iota((clusters, clusters), 1)).astype(F32)
-    listed = product_exact(unit, listed_ref[...].astype(F32), 1, 1)
-    chosen = product_exact(unit, vector_ref[...].astype(F32), 1, 1)
+    unit = one_hot(iota((clusters, clusters), 0) == iota((clusters, clusters), 1))
+    listed = sum(product(unit, half, 1, 1) for half in split_two(listed_ref[...].astype(F32)))
+    chosen = sum(product(unit, half, 1, 1) for half in split_two(vector_ref[...].astype(F32)))
     cluster = (iota((clusters, 3 * clusters), 1) % clusters).astype(F32)
     vector = (iota((clusters, 3 * vectors), 1) % vectors).astype(F32)
-    hot_vector = []
     for partner in range(partners):
-        hot_ref[partner * clusters : (partner + 1) * clusters, :] = one_hot(cluster == listed[:, partner : partner + 1])
-        hot_vector.append(one_hot(vector == chosen[:, partner : partner + 1]))
-    hot_vector = jnp.concatenate(hot_vector, axis=0)
-    for row in range(rows):
-        start = 2 * row * vectors
-        columns = slice(row * 2 * width, (row + 1) * 2 * width)
-        even_ref[:, columns] = product(hot_vector, jnp.concatenate(split_three(even[start : start + vectors]), axis=0))
-        odd_ref[:, columns] = product(hot_vector, jnp.concatenate(split_three(odd[start + vectors : start + 2 * vectors]), axis=0))
+        part = slice(partner * clusters, (partner + 1) * clusters)
+        hot_ref[part, : 3 * clusters] = one_hot(cluster == listed[:, partner : partner + 1])
+        hot_ref[part, 3 * clusters :] = one_hot(vector == chosen[:, partner : partner + 1])
 
 
 def field_rows(field, part, blocks, long):
@@ -279,26 +266,28 @@
             out[first + place] = piece
 
 
-def translate_kernel(rows, hot_ref, even_ref, odd_ref, arrived_ref, out):
+def translate_kernel(rows, hot_ref, table_ref, arrived_ref, out):
     width = arrived_ref.shape[1]
     clusters = arrived_ref.shape[0] // rows
     partners = hot_ref.shape[0] // clusters
+    hot_cluster = hot_ref[:, : 3 * clusters]
+    hot_vector = hot_ref[:, 3 * clusters :]
     step = 2 if rows % 2 == 0 else 1
     for first in range(0, rows, step):
         source = jnp.concatenate(
             [arrived_ref[pl.ds(row, clusters, stride=rows), :] for row in range(first, first + step)], axis=1
         )
-        gathered = product(hot_ref[...], jnp.concatenate(split_three(source), axis=0))
-        columns = slice(first * width, (first + step) * width)
-        direct = jnp.zeros((clusters, step * width), F32)
-        crossed = jnp.zeros((clusters, step * width), F32)
-        for partner in range(partners):
-            part = slice(partner * clusters, (partner + 1) * clusters)
-            direct += gathered[part] * even_ref[part, columns]
-            crossed += gathered[part] * odd_ref[part, columns]
-        for row in range(step):
-            own = slice(row * width, (row + 1) * width)
-            out[pl.ds(first + row, clusters, stride=rows), :] = direct[:, own] + jnp.roll(crossed[:, own], width // 2, axis=1)
+        gathered = product(hot_cluster, jnp.concatenate(split_three(source), axis=0))
+        for row in range(first, first + step):
+            factors = product(hot_vector, table_ref[row])
+            direct = jnp.zeros((clusters, width), F32)
+            crossed = jnp.zeros((clusters, width), F32)
+            for partner in range(partners):
+                part = slice(partner * clusters, (partner + 1) * clusters)
+                value = gathered[part, (row - first) * width : (row - first + 1) * width]
+                direct += value * factors[part, :width]
+                crossed += value * factors[part, width:]
+            out[pl.ds(row, clusters, stride=rows), :] = direct + jnp.roll(crossed, width // 2, axis=1)
 
 
 def lower_kernel(groups, sources, own, devices, arrived_ref, cos_ref, sin_ref, wide_ref, down_ref, parent_ref, *outs):
@@ -358,7 +347,7 @@
         in_specs=[pl.BlockSpec(memory_space=pltpu.HBM)] * len(remote) + [pl.BlockSpec(memory_space=pltpu.VMEM)] * len(args),
         out_specs=[pl.BlockSpec(memory_space=pltpu.VMEM)] * len(outs),
         scratch_shapes=scratch,
-        compiler_params=pltpu.CompilerParams(vmem_limit_bytes=VMEM_BYTES),
+        compiler_params=pltpu.CompilerParams(vmem_limit_bytes=max(VMEM_BYTES, 8 * max(arg.size for arg in (*remote, *args)))),
         cost_estimate=pl.CostEstimate(flops=flops, bytes_accessed=held, transcendentals=0),
         name=name,
     )(*remote, *args)
@@ -415,13 +404,12 @@
         "aggregate",
     )
     arrived = exchange(outgoing)
-    down, hot, even, odd = call(
+    down, hot, factors = call(
         bind(tables_kernel, groups, sources, own),
         [
             struct((sources, 2, long, tall), BF16),
-            struct((partners * clusters, 3 * clusters), BF16),
-            struct((partners * clusters, rows * width), F32),
-            struct((partners * clusters, rows * width), F32),
+            struct((partners * clusters, 3 * clusters + 3 * vectors), BF16),
+            struct((rows, 3 * vectors, 2 * width), BF16),
         ],
         [outgoing],
         600_000_000,
@@ -431,7 +419,7 @@
     (translated,) = call(
         bind(translate_kernel, rows),
         [struct((clusters * rows, width), F32)],
-        [hot, even, odd, arrived.reshape(clusters * rows, width)],
+        [hot, factors, arrived.reshape(clusters * rows, width)],
         600_000_000,
         "translate",
     )

time: 44.4 us -> 39.9 us (0.90)
  local copies, waits for them, and re-layouts: 5.86 us -> 0 us
  waiting for transfers between devices: 5.47 us -> 7.69 us
  blocking collectives: 11.9 us -> 11.4 us
    unnamed x16 -> x0, local copies, waits for them, and re-layouts: 5.86 us -> none
    all_to_all x1, waiting for transfers between devices: 3.75 us -> 5.98 us  [exchange(): lax.all_to_all(blocks, 'clus', split_axis=0, concat_axis=0, tiled=True)]
    all_to_all x1, blocking collectives: 11.9 us -> 11.4 us  [exchange(): lax.all_to_all(blocks, 'clus', split_axis=0, concat_axis=0, tiled=True)]
where the time goes in v4:
time: 39.9 us; the launch traced here: 39.6 us
  blocking collectives  11.4 us (29%)
  Pallas kernels  10.6 us (27%)
  starting transfers between devices  8.46 us (21%)
  waiting for transfers between devices  7.69 us (19%)
  other arithmetic  0.79 us (2%)
  between operations  0.68 us (2%)
    all_to_all x1, blocking collectives, exchange(): lax.all_to_all(blocks, 'clus', split_axis=0, concat_axis=0, tiled=True)  11.4 us
    pallas_call x5, Pallas kernels, call(): pl.pallas_call(kernel, out_shape=outs, in_specs=[pl.BlockSpec(memory_spac...  10.6 us
    all_to_all x1, starting transfers between devices, exchange(): lax.all_to_all(blocks, 'clus', split_axis=0, concat_axis=0, tiled=True)  7.87 us
    all_to_all x1, waiting for transfers between devices, exchange(): lax.all_to_all(blocks, 'clus', split_axis=0, concat_axis=0, tiled=True)  5.98 us
    ppermute x1, waiting for transfers between devices, per_device(): lax.ppermute(children_parts[1], 'samp', backward)  1.71 us
  transfers between devices with their start and end apart: 3, of which 2 were waited for; matrix products, arithmetic and copies ran while one was open for 0% of the time, Pallas kernels for 15%

profile of v4, /device:TPU:0, one launch (start us, length us, event | category | flops | bytes accessed | tf_op | source)
XLA Modules:
  0.0 39.6 jit_solution(2313406358245582996)
XLA Ops:
  0.6 0.5 %collective-permute-start = (f32[768,128]{1,0:T(8,128)}, f32[768,128]{1,0:T(8,128)S(1)}, u32[]{:S(2)}, u32[]{:S(2)}) collective-permute-start(f32[768,128]{1,0:T(8,128)} %bitcast.30), channel_id=1, source_target_pairs={{0,1},{1,0},{2,3},{3,2},{4,5},{5,4},{6,7},{7,6},{8,9},{9,8},{10,11... | collective-permute-start | bytes 1179656 | tf_op jit(solution)/shard_map/ppermute | solution.py:379
  1.1 2.7 %prepare.1 = (f32[192,1024]{1,0:T(8,128)S(1)}, f32[192,1024]{1,0:T(8,128)S(1)}, bf16[4,512,256]{2,1,0:T(8,128)(2,1)S(1)}, bf16[2,2,192,96]{3,2,1,0:T(8,128)(2,1)S(1)}, f32[384,512]{1,0:T(8,128)S(1)}) custom-call(f32[6,9]{1,0:T(8,128)} %refs_0_.3, f32[48,1024]{1,0:T(8,128)} %bitcast.32, s32[6,1024]{1,0:T(8,128)} %bitcast.34, f32[6,1024]{1,0:T(8,128)} %bitcast.35, ...), custom_call_target="tpu_custom_call" | custom-call | flops 400000000 | bytes 5390552 | tf_op jit(solution)/shard_map/prepare/pallas_call | solution.py:344
  3.9 0.0 collective-permute-done.refs_0_
  3.9 2.0 %aggregate.1.refs_4_ = f32[16,24,128]{2,1,0:T(8,128)} custom-call(f32[768,128]{1,0:T(8,128)S(1)} %collective-permute-done.refs_0_, f32[384,512]{1,0:T(8,128)S(1)} %get-tuple-element.13.refs_1_, f32[192,1024]{1,0:T(8,128)S(1)} %get-tuple-element.14.refs_2_.refs_1_, f32[192,1024]{1,0:T(8,128)S(1)} %get-tuple-element.15.refs_3_.refs_2_, ...), custom_call_target="tpu_custom_call" | custom-call | flops 1500000000 | bytes 5341184 | tf_op jit(solution)/shard_map/aggregate/pallas_call | solution.py:344
  5.9 7.9 %all-to-all-start = ((f32[16,24,128]{2,1,0:T(8,128)}), f32[16,24,128]{2,1,0:T(8,128)S(1)}, u32[]{:S(2)}, u32[]{:S(2)}) async-start(f32[16,24,128]{2,1,0:T(8,128)} %aggregate.1.refs_4_), calls=%async_computation | async-start | bytes 393216 | tf_op jit(solution)/shard_map/all_to_all | solution.py:361
  13.8 3.3 %tables.1 = (bf16[2,2,96,192]{3,2,1,0:T(8,128)(2,1)S(1)}, bf16[768,240]{1,0:T(8,128)(2,1)S(1)}, bf16[6,48,256]{2,1,0:T(8,128)(2,1)S(1)}) custom-call(f32[6,9]{1,0:T(8,128)} %refs_0_.3, s32[12,64]{1,0:T(8,128)} %bitcast.36, s32[12,64]{1,0:T(8,128)} %bitcast.37, f32[192,64]{1,0:T(8,128)} %bitcast.33, f32[16,24,128]{2,1,0:T(8,128)} %aggregate.1.refs_4_), custom_call_target="tpu_custom_call" | custom-call | flops 600000000 | bytes 1579224 | tf_op jit(solution)/shard_map/tables/pallas_call | solution.py:344
  17.1 6.0 %all-to-all-done = f32[16,24,128]{2,1,0:T(8,128)S(1)} async-done(((f32[16,24,128]{2,1,0:T(8,128)}), f32[16,24,128]{2,1,0:T(8,128)S(1)}, u32[]{:S(2)}, u32[]{:S(2)}) %all-to-all-start) | async-done | bytes 196640 | tf_op jit(solution)/shard_map/all_to_all | solution.py:361
  23.1 1.2 %translate.1 = f32[384,128]{1,0:T(8,128)S(1)} custom-call(bf16[768,240]{1,0:T(8,128)(2,1)S(1)} %get-tuple-element.18.refs_0_, bf16[6,48,256]{2,1,0:T(8,128)(2,1)S(1)} %get-tuple-element.19.refs_1_, f32[384,128]{1,0:T(8,128)S(1)} %bitcast.27), custom_call_target="tpu_custom_call" | custom-call | flops 600000000 | bytes 1425408 | tf_op jit(solution)/shard_map/translate/pallas_call | solution.py:344
  24.3 11.4 %all_to_all.10.refs_0_ = f32[16,24,128]{2,1,0:T(8,128)S(1)} all-to-all(f32[16,24,128]{2,1,0:T(8,128)S(1)} %bitcast.28), channel_id=1, replica_groups=mesh['clus'=16,'samp'=2] {'clus'}, dimensions={0} | all-to-all | bytes 393216 | tf_op jit(solution)/shard_map/all_to_all | solution.py:361
  35.7 1.3 %lower.1 = (f32[384,128]{1,0:T(8,128)}, f32[768,128]{1,0:T(8,128)S(1)}, f32[768,128]{1,0:T(8,128)S(1)}) custom-call(f32[16,24,128]{2,1,0:T(8,128)S(1)} %all_to_all.10.refs_0_, f32[192,1024]{1,0:T(8,128)S(1)} %get-tuple-element.14.refs_2_.refs_1_, f32[192,1024]{1,0:T(8,128)S(1)} %get-tuple-element.15.refs_3_.refs_2_, ...), custom_call_target="tpu_custom_call" | custom-call | flops 1500000000 | bytes 5144576 | tf_op jit(solution)/shard_map/lower/pallas_call | solution.py:344
  37.0 0.1 collective-permute-start.1
  37.1 1.7 %collective-permute-done.1 = f32[768,128]{1,0:T(8,128)S(1)} collective-permute-done((f32[768,128]{1,0:T(8,128)S(1)}, f32[768,128]{1,0:T(8,128)S(1)}, u32[]{:S(2)}, u32[]{:S(2)}) %collective-permute-start.1) | collective-permute-done | bytes 393248 | tf_op jit(solution)/shard_map/ppermute | solution.py:434
  38.8 0.8 %add.3 = f32[768,128]{1,0:T(8,128)} add(f32[768,128]{1,0:T(8,128)S(1)} %get-tuple-element.22, f32[768,128]{1,0:T(8,128)S(1)} %collective-permute-done.1) | non-fusion elementwise | flops 98304 | bytes 1179648 | tf_op jit(solution)/shard_map/add | solution.py:434
Async XLA Ops:
  0.6 3.2 %collective-permute-start = (f32[768,128]{1,0:T(8,128)}, f32[768,128]{1,0:T(8,128)S(1)}, u32[]{:S(2)}, u32[]{:S(2)}) collective-permute-start(f32[768,128]{1,0:T(8,128)} %bitcast.30), channel_id=1, source_target_pairs={{0,1},{1,0},{2,3},{3,2},{4,5},{5,4},{6,7},{7,6},{8,9},{9,8},{10,11... | collective-permute-start | bytes 1179656 | tf_op jit(solution)/shard_map/ppermute | solution.py:379
  5.9 17.2 %all-to-all-start = ((f32[16,24,128]{2,1,0:T(8,128)}), f32[16,24,128]{2,1,0:T(8,128)S(1)}, u32[]{:S(2)}, u32[]{:S(2)}) async-start(f32[16,24,128]{2,1,0:T(8,128)} %aggregate.1.refs_4_), calls=%async_computation | async-start | bytes 393216 | tf_op jit(solution)/shard_map/all_to_all | solution.py:361
  37.0 1.8 %collective-permute-start.1 = (f32[768,128]{1,0:T(8,128)S(1)}, f32[768,128]{1,0:T(8,128)S(1)}, u32[]{:S(2)}, u32[]{:S(2)}) collective-permute-start(f32[768,128]{1,0:T(8,128)S(1)} %get-tuple-element.23), channel_id=1, source_target_pairs={{1,0},{0,1},{3,2},{2,3},{5,4},{4,5},{7,6},{6,7},{9,8},{8,9},{11,10... | collective-permute-start | bytes 1179656 | tf_op jit(solution)/shard_map/ppermute | solution.py:434

commit v5 on v4

--- a/solution.py
+++ b/solution.py
@@ -68,6 +68,20 @@
 def halves_of(theta, sources, own):
     high, low = split_two(jnp.concatenate(folded(theta, sources, own), axis=1))
     return jnp.concatenate([high, low], axis=1)
+
+
+def turns(phase, groups, rows):
+    tall = OCTANTS * groups * rows
+    shape = (tall, 3 * OCTANTS * rows)
+    place, phase_id = iota(shape, 0), iota(shape, 1) % (OCTANTS * rows)
+    repeat = one_hot(place % rows * OCTANTS + place // (groups * rows) == phase_id)
+    half = 0.5 * phase
+    square = half * half
+    sine = half + half * square * series(square, SIN_TERMS)
+    cosine = 1.0 + square * series(square, COS_TERMS)
+    return [
+        product(repeat, jnp.concatenate(split_three(value), axis=0)) for value in (1.0 - 2.0 * sine * sine, 2.0 * sine * cosine)
+    ]
 
 
 def prepare_kernel(groups, sources, own, *refs):
@@ -87,9 +101,6 @@
     at_own = one_hot(column // long * own + column % own == iota((2 * sources * own, lengths), 0))
     tall_id = iota((tall, long), 0)
     same = iota((tall, long), 1) // own == (tall_id // rows) % groups * OCTANTS + tall_id // (groups * rows)
-    shape = (tall, 3 * OCTANTS * rows)
-    place, phase_id = iota(shape, 0), iota(shape, 1) % (OCTANTS * rows)
-    repeat = one_hot(place % rows * OCTANTS + place // (groups * rows) == phase_id)
 
     copies[0].wait()
     tall_theta = product(at_row, halves_of(theta_ref[...], sources, own)).astype(BF16)
@@ -98,12 +109,7 @@
         up_ref[place % sources, place // sources] = jnp.where(same, spread[:, place * long : (place + 1) * long], 0.0).astype(BF16)
 
     copies[1].wait()
-    half = 0.5 * phase_ref[...]
-    square = half * half
-    sine = half + half * square * series(square, SIN_TERMS)
-    cosine = 1.0 + square * series(square, COS_TERMS)
-    cos_ref[...] = product(repeat, jnp.concatenate(split_three(1.0 - 2.0 * sine * sine), axis=0))
-    sin_ref[...] = product(repeat, jnp.concatenate(split_three(2.0 * sine * cosine), axis=0))
+    cos_ref[...], sin_ref[...] = turns(phase_ref[...], groups, rows)
 
     copies[2].wait()
     copies[3].wait()
@@ -135,10 +141,11 @@
 
 def tables_kernel(groups, sources, own, *refs):
     count = 4
-    remote, outs, rest = refs[:count], refs[count + 1 : count + 4], refs[count + 4 :]
-    local, sems = rest[:count], rest[count]
+    remote, phases = refs[:count], refs[count : count + sources - 1]
+    outs = refs[count + sources : -count - 1]
+    local, sems = refs[-count - 1 : -1], refs[-1]
     theta_ref, listed_ref, vector_ref, table_ref = local
-    down_ref, hot_ref, table_out = outs
+    down_ref, hot_ref, table_out, *turned_refs = outs
     copies = started(remote, local, sems)
     rows = theta_ref.shape[0]
     tall, long = OCTANTS * groups * rows, groups * OCTANTS * own
@@ -184,6 +191,9 @@
         hot_ref[part, : 3 * clusters] = one_hot(cluster == listed[:, partner : partner + 1])
         hot_ref[part, 3 * clusters :] = one_hot(vector == chosen[:, partner : partner + 1])
 
+    for place, phase in enumerate(phases):
+        turned_refs[2 * place][...], turned_refs[2 * place + 1][...] = turns(phase[...], groups, rows)
+
 
 def field_rows(field, part, blocks, long):
     return jnp.concatenate([field[pl.ds(2 * block + part, long, stride=2 * blocks), :] for block in range(blocks)], axis=1)
@@ -226,7 +236,7 @@
 
 def aggregate_kernel(groups, sources, own, devices, *refs):
     fields = refs[: sources - 1]
-    partial_ref, cos_ref, sin_ref, wide_ref, up_ref, out = refs[sources - 1 :]
+    partial_ref, cos_ref, sin_ref, wide_ref, up_ref, out, ready, sems = refs[sources - 1 :]
     blocks = wide_ref.shape[0]
     rows_all = cos_ref.shape[0] // OCTANTS
     columns = cos_ref.shape[1] // devices
@@ -246,6 +256,7 @@
         rim = jnp.where(lane < HALF, value[:, after * TILE : (after + 1) * TILE], value[:, before * TILE : (before + 1) * TILE])
         return [main, rim]
 
+    copies = []
     for block in range(blocks):
         one, two = windows(high, block), windows(low, block)
         left = jnp.concatenate(one + two + one, axis=1)
@@ -261,9 +272,13 @@
             b = spread[tall + octant * rows_all : tall + (octant + 1) * rows_all]
             real += a * cosine - b * sine
             imag += a * sine + b * cosine
-        first = block * PAIR // columns
+        first, many = block * PAIR // columns, PAIR // columns
         for place, piece in enumerate(packed_pieces(real, imag, columns)):
-            out[first + place] = piece
+            ready[first + place] = piece
+        copies.append(pltpu.make_async_copy(ready.at[first : first + many], out.at[first : first + many], sems.at[block]))
+        copies[-1].start()
+    for copy in copies:
+        copy.wait()
 
 
 def translate_kernel(rows, hot_ref, table_ref, arrived_ref, out):
@@ -290,17 +305,9 @@
             out[pl.ds(row, clusters, stride=rows), :] = direct + jnp.roll(crossed, width // 2, axis=1)
 
 
-def lower_kernel(groups, sources, own, devices, arrived_ref, cos_ref, sin_ref, wide_ref, down_ref, parent_ref, *outs):
+def coarse_columns(real, imag, cos_ref, sin_ref, wide_ref):
     blocks = wide_ref.shape[0]
     rows_all = cos_ref.shape[0] // OCTANTS
-    azimuth = cos_ref.shape[1]
-    columns = azimuth // devices
-    long, tall = groups * OCTANTS * own, OCTANTS * rows_all
-    real, imag = unpacked_pieces(lambda device: arrived_ref[device], devices, columns)
-    tiles = azimuth // TILE
-    for tile in range(tiles):
-        for part, value in enumerate((real, imag)):
-            parent_ref[pl.ds(2 * tile + part, rows_all, stride=2 * tiles), :] = value[:, tile * TILE : (tile + 1) * TILE]
     mains, rims = [], []
     for block in range(blocks):
         part = slice(block * PAIR, (block + 1) * PAIR)
@@ -317,40 +324,81 @@
         both = product(left, right, 1, 1)
         mains.append(both[:, :TILE])
         rims.append(both[:, TILE:])
-    lane = iota((2 * tall, TILE), 1)
-    coarse = jnp.concatenate(
+    lane = iota((2 * OCTANTS * rows_all, TILE), 1)
+    return jnp.concatenate(
         [
             mains[block] + jnp.where(lane < HALF, rims[(block - 1) % blocks], rims[(block + 1) % blocks])
             for block in range(blocks)
         ],
         axis=1,
     )
-    high, low = split_two(coarse)
-    for place, out in enumerate(outs):
-        up, fine = down_ref[place, 0], down_ref[place, 1]
+
+
+def lower_kernel(devices, arrived_ref, cos_ref, sin_ref, wide_ref, down_ref, parent_out, partial_ref, parent_ref, sem):
+    rows_all = cos_ref.shape[0] // OCTANTS
+    azimuth = cos_ref.shape[1]
+    long, tall = down_ref.shape[2:]
+    real, imag = unpacked_pieces(lambda device: arrived_ref[device], devices, azimuth // devices)
+    tiles = azimuth // TILE
+    for tile in range(tiles):
+        for part, value in enumerate((real, imag)):
+            parent_ref[pl.ds(2 * tile + part, rows_all, stride=2 * tiles), :] = value[:, tile * TILE : (tile + 1) * TILE]
+    copy = pltpu.make_async_copy(parent_ref, parent_out, sem)
+    copy.start()
+    coarse = coarse_columns(real, imag, cos_ref, sin_ref, wide_ref)
+    for part in range(2):
+        partial_ref[part * long : (part + 1) * long, :] = polar(down_ref[0, 0], down_ref[0, 1], coarse[part * tall : (part + 1) * tall])
+    copy.wait()
+
+
+def finish_kernel(devices, sources, *refs):
+    arrived = refs[: sources - 1]
+    turned_refs = refs[sources - 1 : 3 * (sources - 1)]
+    wide_ref, down_ref, partial_ref, out, ready, sems = refs[3 * (sources - 1) :]
+    blocks = wide_ref.shape[0]
+    azimuth = turned_refs[0].shape[1]
+    long, tall = down_ref.shape[2:]
+    coarse = []
+    for place, field in enumerate(arrived):
+        real, imag = unpacked_pieces(lambda device: field[device], devices, azimuth // devices)
+        coarse.append(split_two(coarse_columns(real, imag, turned_refs[2 * place], turned_refs[2 * place + 1], wide_ref)))
+    copies = []
+    size = long // 2
+    for first in range(0, long, size):
+        rows = slice(first, first + size)
         for part in range(2):
-            rows = slice(part * tall, (part + 1) * tall)
-            value = product(up, high[rows]) + (product(fine, high[rows]) + product(up, low[rows]))
+            value = partial_ref[part * long + first : part * long + first + size, :]
+            for place, (high, low) in enumerate(coarse):
+                source = slice(part * tall, (part + 1) * tall)
+                up, fine = down_ref[place + 1, 0, rows], down_ref[place + 1, 1, rows]
+                value += product(up, high[source]) + (product(fine, high[source]) + product(up, low[source]))
             for block in range(blocks):
-                out[pl.ds(2 * block + part, long, stride=2 * blocks), :] = value[:, block * TILE : (block + 1) * TILE]
-
-
-def call(kernel, outs, args, flops, name, remote=()):
+                start = 2 * blocks * first + 2 * block + part
+                ready[pl.ds(start, size, stride=2 * blocks), :] = value[:, block * TILE : (block + 1) * TILE]
+        whole = slice(2 * blocks * first, 2 * blocks * (first + size))
+        copies.append(pltpu.make_async_copy(ready.at[whole], out.at[whole], sems.at[len(copies)]))
+        copies[-1].start()
+    for copy in copies:
+        copy.wait()
+
+
+def call(kernel, outs, args, flops, name, remote=(), after=(), far=(), scratch=()):
     held = sum(4 * leaf.size for leaf in outs) + sum(4 * arg.size for arg in (*remote, *args))
     remote = [pltpu.with_memory_space_constraint(arg, pltpu.HBM) for arg in remote]
-    scratch = [pltpu.VMEM(arg.shape, arg.dtype) for arg in remote]
+    scratch = [*scratch, *(pltpu.VMEM(arg.shape, arg.dtype) for arg in remote)]
     if remote:
         scratch.append(pltpu.SemaphoreType.DMA((len(remote),)))
+    near, away, free = (pl.BlockSpec(memory_space=space) for space in (pltpu.VMEM, pltpu.HBM, pl.ANY))
     return pl.pallas_call(
         kernel,
         out_shape=outs,
-        in_specs=[pl.BlockSpec(memory_space=pltpu.HBM)] * len(remote) + [pl.BlockSpec(memory_space=pltpu.VMEM)] * len(args),
-        out_specs=[pl.BlockSpec(memory_space=pltpu.VMEM)] * len(outs),
+        in_specs=[away] * len(remote) + [near] * len(args) + [free] * len(after),
+        out_specs=[free if place in far else near for place in range(len(outs))],
         scratch_shapes=scratch,
         compiler_params=pltpu.CompilerParams(vmem_limit_bytes=max(VMEM_BYTES, 8 * max(arg.size for arg in (*remote, *args)))),
         cost_estimate=pl.CostEstimate(flops=flops, bytes_accessed=held, transcendentals=0),
         name=name,
-    )(*remote, *args)
+    )(*remote, *args, *after)
 
 
 def bind(kernel, *settings):
@@ -381,6 +429,8 @@
         neighbours.append(lax.ppermute(field, "samp", backward))
 
     phase = shift_phase.transpose(1, 0, 2).reshape(rows * OCTANTS, azimuth)
+    ways = [backward] if sources == 2 else [backward, forward]
+    phases = [lax.ppermute(phase, "samp", way) for way in ways]
     table = translation_table.transpose(0, 2, 1, 3).reshape(vectors * rows * 2, width // 2)
     cosine, sine, wide, up, partial = call(
         bind(prepare_kernel, groups, sources, own),
@@ -402,19 +452,23 @@
         [*neighbours, partial, cosine, sine, wide, up],
         1_500_000_000,
         "aggregate",
+        far=(0,),
+        scratch=[pltpu.VMEM((devices, rows_all, width), F32), pltpu.SemaphoreType.DMA((blocks,))],
     )
     arrived = exchange(outgoing)
-    down, hot, factors = call(
+    down, hot, factors, *turned_parts = call(
         bind(tables_kernel, groups, sources, own),
         [
             struct((sources, 2, long, tall), BF16),
             struct((partners * clusters, 3 * clusters + 3 * vectors), BF16),
             struct((rows, 3 * vectors, 2 * width), BF16),
-        ],
-        [outgoing],
+        ]
+        + [struct((tall, azimuth), F32)] * (2 * sources - 2),
+        phases,
         600_000_000,
         "tables",
         [theta_weights, far_list.T, far_vector.T, table],
+        [outgoing],
     )
     (translated,) = call(
         bind(translate_kernel, rows),
@@ -424,16 +478,26 @@
         "translate",
     )
     returned = exchange(translated.reshape(devices, rows_all, width))
-    parent, *children_parts = call(
-        bind(lower_kernel, groups, sources, own, devices),
-        [struct((rows_all * 2 * azimuth // TILE, TILE), F32)] + [struct((long * blocks * 2, TILE), F32)] * sources,
+    size = rows_all * 2 * azimuth // TILE
+    parent, partial = call(
+        bind(lower_kernel, devices),
+        [struct((size, TILE), F32), struct((2 * long, columns), F32)],
         [returned, cosine, sine, wide, down],
         1_500_000_000,
         "lower",
-    )
-    total = children_parts[0] + lax.ppermute(children_parts[1], "samp", backward)
-    if sources == 3:
-        total = total + lax.ppermute(children_parts[2], "samp", forward)
+        far=(0,),
+        scratch=[pltpu.VMEM((size, TILE), F32), pltpu.SemaphoreType.DMA],
+    )
+    returned_parts = [lax.ppermute(returned, "samp", way) for way in ways]
+    (total,) = call(
+        bind(finish_kernel, devices, sources),
+        [struct((long * blocks * 2, TILE), F32)],
+        [*returned_parts, *turned_parts, wide, down, partial],
+        1_500_000_000,
+        "finish",
+        far=(0,),
+        scratch=[pltpu.VMEM((long * blocks * 2, TILE), F32), pltpu.SemaphoreType.DMA((2,))],
+    )
     child_incoming = total.reshape(children, own, blocks, 2, TILE).transpose(0, 3, 1, 2, 4).reshape(children, 2, own, columns)
     parent_incoming = (
         parent.reshape(groups, rows, azimuth // TILE, 2, TILE).transpose(0, 3, 1, 2, 4).reshape(groups, 2, rows, azimuth)

time: 39.9 us -> 40.6 us (1.018)
  waiting for transfers between devices: 7.69 us -> 4.88 us
  local copies, waits for them, and re-layouts: 0 us -> 1.79 us
  Pallas kernels: 10.6 us -> 11.7 us
  blocking collectives: 11.4 us -> 12.2 us
  other arithmetic: 0.79 us -> 0 us
    all_to_all x1, waiting for transfers between devices: 5.98 us -> 3.41 us  [exchange(): lax.all_to_all(blocks, 'clus', split_axis=0, concat_axis=0, tiled=True)]
    unnamed x0 -> x10, local copies, waits for them, and re-layouts: none -> 1.79 us
    pallas_call x5 -> x6, Pallas kernels: 10.6 us -> 11.7 us  [call(): pl.pallas_call(kernel, out_shape=outs, in_specs=[away] * len(remote) + [n...]
    all_to_all x1, blocking collectives: 11.4 us -> 12.2 us  [exchange(): lax.all_to_all(blocks, 'clus', split_axis=0, concat_axis=0, tiled=True)]
    add x1 -> x0, other arithmetic: 0.79 us -> none  [per_device(): children_parts[0] + lax.ppermute(children_parts[1], 'samp', backward)]
    ppermute x1 -> x2, waiting for transfers between devices: 1.71 us -> 1.47 us  [the longest x1 1.23 us: per_device(): phases = [lax.ppermute(phase, 'samp', way) for way in ways]]
  transfers between devices with their start and end apart: 3 -> 4, of which waited for: 2 -> 3; matrix products, arithmetic and copies ran while one was open for 0% -> 0% of each run, Pallas kernels for 15% -> 16%
where the time goes in v5:
time: 40.6 us; the launch traced here: 40.2 us
  blocking collectives  12.2 us (30%)
  Pallas kernels  11.7 us (29%)
  starting transfers between devices  8.83 us (22%)
  waiting for transfers between devices  4.88 us (12%)
  local copies, waits for them, and re-layouts  1.79 us (4%)
  between operations  0.71 us (2%)
    all_to_all x1, blocking collectives, exchange(): lax.all_to_all(blocks, 'clus', split_axis=0, concat_axis=0, tiled=True)  12.2 us
    pallas_call x6, Pallas kernels, call(): pl.pallas_call(kernel, out_shape=outs, in_specs=[away] * len(remote) + [n...  11.7 us
    all_to_all x1, starting transfers between devices, exchange(): lax.all_to_all(blocks, 'clus', split_axis=0, concat_axis=0, tiled=True)  8.03 us
    all_to_all x1, waiting for transfers between devices, exchange(): lax.all_to_all(blocks, 'clus', split_axis=0, concat_axis=0, tiled=True)  3.41 us
    unnamed x10, local copies, waits for them, and re-layouts  1.79 us
    ppermute x1, waiting for transfers between devices, per_device(): phases = [lax.ppermute(phase, 'samp', way) for way in ways]  1.23 us
  transfers between devices with their start and end apart: 4, of which 3 were waited for; matrix products, arithmetic and copies ran while one was open for 0% of the time, Pallas kernels for 16%

profile of v5, /device:TPU:0, one launch (start us, length us, event | category | flops | bytes accessed | tf_op | source)
XLA Modules:
  0.0 40.2 jit_solution(3350573416936538861)
XLA Ops:
  0.6 0.5 %collective-permute-start.1 = (f32[768,128]{1,0:T(8,128)}, f32[768,128]{1,0:T(8,128)S(1)}, u32[]{:S(2)}, u32[]{:S(2)}) collective-permute-start(f32[768,128]{1,0:T(8,128)} %bitcast.29), channel_id=1, source_target_pairs={{0,1},{1,0},{2,3},{3,2},{4,5},{5,4},{6,7},{7,6},{8,9},{9,8},{10,11... | collective-permute-start | bytes 1179656 | tf_op jit(solution)/shard_map/ppermute | solution.py:427
  1.1 2.7 %prepare.1 = (f32[192,1024]{1,0:T(8,128)S(1)}, f32[192,1024]{1,0:T(8,128)S(1)}, bf16[4,512,256]{2,1,0:T(8,128)(2,1)S(1)}, bf16[2,2,192,96]{3,2,1,0:T(8,128)(2,1)S(1)}, f32[384,512]{1,0:T(8,128)S(1)}) custom-call(f32[6,9]{1,0:T(8,128)} %refs_0_.3, f32[48,1024]{1,0:T(8,128)} %bitcast.31, s32[6,1024]{1,0:T(8,128)} %bitcast.34, f32[6,1024]{1,0:T(8,128)} %bitcast.35, ...), custom_call_target="tpu_custom_call" | custom-call | flops 400000000 | bytes 5390552 | tf_op jit(solution)/shard_map/prepare/pallas_call | solution.py:392
  3.9 0.0 collective-permute-done.1.refs_0_
  3.9 2.0 %aggregate.1.refs_5_ = f32[16,24,128]{2,1,0:T(8,128)} custom-call(f32[768,128]{1,0:T(8,128)S(1)} %collective-permute-done.1.refs_0_, f32[384,512]{1,0:T(8,128)S(1)} %get-tuple-element.14.refs_1_, f32[192,1024]{1,0:T(8,128)S(1)} %get-tuple-element.15.refs_2_.refs_1_, f32[192,1024]{1,0:T(8,128)S(1)} %get-tuple-element.16.refs_3_.refs_2_, ...), custom_call_target="tpu_custom_call" | custom-call | flops 1500000000 | bytes 5341184 | tf_op jit(solution)/shard_map/aggregate/pallas_call | solution.py:392
  5.9 0.0 copy-start.4
  5.9 8.0 %all-to-all-start = ((f32[16,24,128]{2,1,0:T(8,128)}), f32[16,24,128]{2,1,0:T(8,128)S(1)}, u32[]{:S(2)}, u32[]{:S(2)}) async-start(f32[16,24,128]{2,1,0:T(8,128)} %aggregate.1.refs_5_), calls=%async_computation | async-start | bytes 393216 | tf_op jit(solution)/shard_map/all_to_all | solution.py:409
  14.0 0.0 copy-done.4
  14.0 0.3 collective-permute-start
  14.2 1.2 %collective-permute-done.refs_4_ = f32[48,1024]{1,0:T(8,128)S(1)} collective-permute-done((f32[48,1024]{1,0:T(8,128)S(1)}, f32[48,1024]{1,0:T(8,128)S(1)}, u32[]{:S(2)}, u32[]{:S(2)}) %collective-permute-start) | collective-permute-done | bytes 196640 | tf_op jit(solution)/shard_map/ppermute | solution.py:433
  15.5 2.6 %tables.1 = (bf16[2,2,96,192]{3,2,1,0:T(8,128)(2,1)S(1)}, bf16[768,240]{1,0:T(8,128)(2,1)S(1)}, bf16[6,48,256]{2,1,0:T(8,128)(2,1)S(1)}, f32[192,1024]{1,0:T(8,128)S(1)}, f32[192,1024]{1,0:T(8,128)S(1)}) custom-call(f32[6,9]{1,0:T(8,128)} %refs_0_.3, s32[12,64]{1,0:T(8,128)} %bitcast.36, s32[12,64]{1,0:T(8,128)} %bitcast.37, f32[192,64]{1,0:T(8,128)} %bitcast.33, ...), custom_call_target="tpu_custom_call" | custom-call | flops 600000000 | bytes 3152088 | tf_op jit(solution)/shard_map/tables/pallas_call | solution.py:392
  18.1 0.0 copy-start
  18.1 0.9 %copy-done = f32[192,1024]{1,0:T(8,128)} copy-done((f32[192,1024]{1,0:T(8,128)}, f32[192,1024]{1,0:T(8,128)S(1)}, u32[]{:S(2)}) %copy-start) | copy-done | bytes 786456
  18.9 0.0 copy-start.2
  18.9 0.9 %copy-done.2 = f32[192,1024]{1,0:T(8,128)} copy-done((f32[192,1024]{1,0:T(8,128)}, f32[192,1024]{1,0:T(8,128)S(1)}, u32[]{:S(2)}) %copy-start.2) | copy-done | bytes 786456
  19.8 3.4 %all-to-all-done = f32[16,24,128]{2,1,0:T(8,128)S(1)} async-done(((f32[16,24,128]{2,1,0:T(8,128)}), f32[16,24,128]{2,1,0:T(8,128)S(1)}, u32[]{:S(2)}, u32[]{:S(2)}) %all-to-all-start) | async-done | bytes 196640 | tf_op jit(solution)/shard_map/all_to_all | solution.py:409
  23.3 1.2 %translate.1 = f32[384,128]{1,0:T(8,128)S(1)} custom-call(bf16[768,240]{1,0:T(8,128)(2,1)S(1)} %get-tuple-element.19.refs_0_, bf16[6,48,256]{2,1,0:T(8,128)(2,1)S(1)} %get-tuple-element.20.refs_1_, f32[384,128]{1,0:T(8,128)S(1)} %bitcast.27), custom_call_target="tpu_custom_call" | custom-call | flops 600000000 | bytes 1425408 | tf_op jit(solution)/shard_map/translate/pallas_call | solution.py:392
  24.5 12.2 %all_to_all.10.refs_0_ = f32[16,24,128]{2,1,0:T(8,128)S(1)} all-to-all(f32[16,24,128]{2,1,0:T(8,128)S(1)} %bitcast.28), channel_id=1, replica_groups=mesh['clus'=16,'samp'=2] {'clus'}, dimensions={0} | all-to-all | bytes 393216 | tf_op jit(solution)/shard_map/all_to_all | solution.py:409
  36.7 0.0 collective-permute-start.2
  36.7 0.0 copy-start.1
  36.7 0.0 copy-start.3
  36.7 1.2 %lower.1 = (f32[384,128]{1,0:T(8,128)}, f32[192,512]{1,0:T(8,128)S(1)}) custom-call(f32[16,24,128]{2,1,0:T(8,128)S(1)} %all_to_all.10.refs_0_, f32[192,1024]{1,0:T(8,128)S(1)} %get-tuple-element.15.refs_2_.refs_1_, f32[192,1024]{1,0:T(8,128)S(1)} %get-tuple-element.16.refs_3_.refs_2_, bf16[4,512,256]{2,1,0:T(8,128)(2,1)S(1)} %get-tuple-element.17.refs_4_.refs_3_, ...), custom_call_target="tpu_custom_call" | custom-call | flops 1500000000 | bytes 4751360 | tf_op jit(solution)/shard_map/lower/pallas_call | solution.py:392
  37.9 0.2 collective-permute-done.2.refs_0_
  38.1 0.0 copy-done.1
  38.1 0.0 copy-done.3
  38.1 2.0 %finish.1 = f32[768,128]{1,0:T(8,128)} custom-call(f32[16,24,128]{2,1,0:T(8,128)S(1)} %collective-permute-done.2.refs_0_, f32[192,1024]{1,0:T(8,128)S(1)} %copy-done.1, f32[192,1024]{1,0:T(8,128)S(1)} %copy-done.3, bf16[4,512,256]{2,1,0:T(8,128)(2,1)S(1)} %get-tuple-element.17.refs_4_.refs_3_, bf16[2,2,96,192]{3,2,1,0:T(8,128)(2,1)S(1)} %get-tuple-element.21.refs_4_, ...), custom_call_target="tpu_custom_call" | custom-call | flops 1500000000 | bytes 4947968 | tf_op jit(solution)/shard_map/finish/pallas_call | solution.py:392
Async XLA Ops:
  0.6 3.2 %collective-permute-start.1 = (f32[768,128]{1,0:T(8,128)}, f32[768,128]{1,0:T(8,128)S(1)}, u32[]{:S(2)}, u32[]{:S(2)}) collective-permute-start(f32[768,128]{1,0:T(8,128)} %bitcast.29), channel_id=1, source_target_pairs={{0,1},{1,0},{2,3},{3,2},{4,5},{5,4},{6,7},{7,6},{8,9},{9,8},{10,11... | collective-permute-start | bytes 1179656 | tf_op jit(solution)/shard_map/ppermute | solution.py:427
  5.9 8.0 %copy-start.4 = (f32[8,6,1024]{2,0,1:T(8,128)S(1)}, f32[8,6,1024]{2,0,1:T(8,128)}, u32[]{:S(2)}) copy-start(f32[8,6,1024]{2,0,1:T(8,128)} %param.12) | copy-start | bytes 589828
  5.9 17.3 %all-to-all-start = ((f32[16,24,128]{2,1,0:T(8,128)}), f32[16,24,128]{2,1,0:T(8,128)S(1)}, u32[]{:S(2)}, u32[]{:S(2)}) async-start(f32[16,24,128]{2,1,0:T(8,128)} %aggregate.1.refs_5_), calls=%async_computation | async-start | bytes 393216 | tf_op jit(solution)/shard_map/all_to_all | solution.py:409
  14.0 1.5 %collective-permute-start = (f32[48,1024]{1,0:T(8,128)S(1)}, f32[48,1024]{1,0:T(8,128)S(1)}, u32[]{:S(2)}, u32[]{:S(2)}) collective-permute-start(f32[48,1024]{1,0:T(8,128)S(1)} %bitcast.32), channel_id=1, source_target_pairs={{1,0},{0,1},{3,2},{2,3},{5,4},{4,5},{7,6},{6,7},{9,8},{8,9},{11,10... | collective-permute-start | bytes 589832 | tf_op jit(solution)/shard_map/ppermute | solution.py:433
  18.1 0.9 %copy-start = (f32[192,1024]{1,0:T(8,128)}, f32[192,1024]{1,0:T(8,128)S(1)}, u32[]{:S(2)}) copy-start(f32[192,1024]{1,0:T(8,128)S(1)} %get-tuple-element.23.refs_1_) | copy-start | bytes 2359300
  18.9 0.9 %copy-start.2 = (f32[192,1024]{1,0:T(8,128)}, f32[192,1024]{1,0:T(8,128)S(1)}, u32[]{:S(2)}) copy-start(f32[192,1024]{1,0:T(8,128)S(1)} %get-tuple-element.24.refs_2_) | copy-start | bytes 2359300
  36.7 1.4 %collective-permute-start.2 = (f32[16,24,128]{2,1,0:T(8,128)S(1)}, f32[16,24,128]{2,1,0:T(8,128)S(1)}, u32[]{:S(2)}, u32[]{:S(2)}) collective-permute-start(f32[16,24,128]{2,1,0:T(8,128)S(1)} %all_to_all.10.refs_0_), channel_id=1, source_target_pairs={{1,0},{0,1},{3,2},{2,3},{5,4},{4,5},{7,6},{6,7},{9,8},{8,9},{11,10... | collective-permute-start | bytes 589832 | tf_op jit(solution)/shard_map/ppermute | solution.py:491
  36.7 1.4 %copy-start.1 = (f32[192,1024]{1,0:T(8,128)S(1)}, f32[192,1024]{1,0:T(8,128)}, u32[]{:S(2)}) copy-start(f32[192,1024]{1,0:T(8,128)} %copy-done) | copy-start | bytes 2359300
  36.7 1.4 %copy-start.3 = (f32[192,1024]{1,0:T(8,128)S(1)}, f32[192,1024]{1,0:T(8,128)}, u32[]{:S(2)}) copy-start(f32[192,1024]{1,0:T(8,128)} %copy-done.2) | copy-start | bytes 2359300

commit v6 on v5

--- a/solution.py
+++ b/solution.py
@@ -145,7 +145,7 @@
     outs = refs[count + sources : -count - 1]
     local, sems = refs[-count - 1 : -1], refs[-1]
     theta_ref, listed_ref, vector_ref, table_ref = local
-    down_ref, hot_ref, table_out, *turned_refs = outs
+    down_ref, hot_ref, even_ref, odd_ref, *turned_refs = outs
     copies = started(remote, local, sems)
     rows = theta_ref.shape[0]
     tall, long = OCTANTS * groups * rows, groups * OCTANTS * own
@@ -170,13 +170,7 @@
     order = one_hot(at == place % vectors * (2 * rows) + place // (2 * vectors) * 2 + place // vectors % 2)
     lane, source = iota((width, 4 * width), 1), iota((width, 4 * width), 0)
     twice = jnp.where(lane % width == source, jnp.where(lane < 3 * width, 1.0, -1.0), 0.0).astype(BF16)
-    for piece, part in enumerate(split_three(raw)):
-        wide = product(product(order, part).astype(BF16), twice).astype(BF16)
-        for row in range(rows):
-            start = 2 * row * vectors
-            target = slice(piece * vectors, (piece + 1) * vectors)
-            table_out[row, target, : 2 * width] = wide[start : start + vectors, : 2 * width]
-            table_out[row, target, 2 * width :] = wide[start + vectors : start + 2 * vectors, 2 * width :]
+    pieces = [product(product(order, part).astype(BF16), twice).astype(BF16) for part in split_three(raw)]
 
     copies[1].wait()
     copies[2].wait()
@@ -186,10 +180,19 @@
     chosen = sum(product(unit, half, 1, 1) for half in split_two(vector_ref[...].astype(F32)))
     cluster = (iota((clusters, 3 * clusters), 1) % clusters).astype(F32)
     vector = (iota((clusters, 3 * vectors), 1) % vectors).astype(F32)
+    hot_vector = []
     for partner in range(partners):
-        part = slice(partner * clusters, (partner + 1) * clusters)
-        hot_ref[part, : 3 * clusters] = one_hot(cluster == listed[:, partner : partner + 1])
-        hot_ref[part, 3 * clusters :] = one_hot(vector == chosen[:, partner : partner + 1])
+        hot_ref[partner * clusters : (partner + 1) * clusters, :] = one_hot(cluster == listed[:, partner : partner + 1])
+        hot_vector.append(one_hot(vector == chosen[:, partner : partner + 1]))
+    hot_vector = jnp.concatenate(hot_vector, axis=0)
+    for row in range(rows):
+        real, imag = 2 * row * vectors, (2 * row + 1) * vectors
+        columns = slice(row * 2 * width, (row + 1) * 2 * width)
+        even = jnp.concatenate([piece[real : real + vectors, : 2 * width] for piece in pieces], axis=0)
+        odd = jnp.concatenate([piece[imag : imag + vectors, 2 * width :] for piece in pieces], axis=0)
+        both = product(hot_vector, jnp.concatenate([even, odd], axis=1))
+        even_ref[:, columns] = both[:, : 2 * width]
+        odd_ref[:, columns] = both[:, 2 * width :]
 
     for place, phase in enumerate(phases):
         turned_refs[2 * place][...], turned_refs[2 * place + 1][...] = turns(phase[...], groups, rows)
@@ -236,7 +239,8 @@
 
 def aggregate_kernel(groups, sources, own, devices, *refs):
     fields = refs[: sources - 1]
-    partial_ref, cos_ref, sin_ref, wide_ref, up_ref, out, ready, sems = refs[sources - 1 :]
+    partial_ref, cos_ref, sin_ref, wide_ref, up_ref = refs[sources - 1 : sources + 4]
+    out = refs[-1]
     blocks = wide_ref.shape[0]
     rows_all = cos_ref.shape[0] // OCTANTS
     columns = cos_ref.shape[1] // devices
@@ -256,7 +260,6 @@
         rim = jnp.where(lane < HALF, value[:, after * TILE : (after + 1) * TILE], value[:, before * TILE : (before + 1) * TILE])
         return [main, rim]
 
-    copies = []
     for block in range(blocks):
         one, two = windows(high, block), windows(low, block)
         left = jnp.concatenate(one + two + one, axis=1)
@@ -272,37 +275,31 @@
             b = spread[tall + octant * rows_all : tall + (octant + 1) * rows_all]
             real += a * cosine - b * sine
             imag += a * sine + b * cosine
-        first, many = block * PAIR // columns, PAIR // columns
+        first = block * PAIR // columns
         for place, piece in enumerate(packed_pieces(real, imag, columns)):
-            ready[first + place] = piece
-        copies.append(pltpu.make_async_copy(ready.at[first : first + many], out.at[first : first + many], sems.at[block]))
-        copies[-1].start()
-    for copy in copies:
-        copy.wait()
-
-
-def translate_kernel(rows, hot_ref, table_ref, arrived_ref, out):
+            out[first + place] = piece
+
+
+def translate_kernel(rows, hot_ref, even_ref, odd_ref, arrived_ref, out):
     width = arrived_ref.shape[1]
     clusters = arrived_ref.shape[0] // rows
     partners = hot_ref.shape[0] // clusters
-    hot_cluster = hot_ref[:, : 3 * clusters]
-    hot_vector = hot_ref[:, 3 * clusters :]
     step = 2 if rows % 2 == 0 else 1
     for first in range(0, rows, step):
         source = jnp.concatenate(
             [arrived_ref[pl.ds(row, clusters, stride=rows), :] for row in range(first, first + step)], axis=1
         )
-        gathered = product(hot_cluster, jnp.concatenate(split_three(source), axis=0))
-        for row in range(first, first + step):
-            factors = product(hot_vector, table_ref[row])
-            direct = jnp.zeros((clusters, width), F32)
-            crossed = jnp.zeros((clusters, width), F32)
-            for partner in range(partners):
-                part = slice(partner * clusters, (partner + 1) * clusters)
-                value = gathered[part, (row - first) * width : (row - first + 1) * width]
-                direct += value * factors[part, :width]
-                crossed += value * factors[part, width:]
-            out[pl.ds(row, clusters, stride=rows), :] = direct + jnp.roll(crossed, width // 2, axis=1)
+        gathered = product(hot_ref[...], jnp.concatenate(split_three(source), axis=0))
+        columns = slice(first * width, (first + step) * width)
+        direct = jnp.zeros((clusters, step * width), F32)
+        crossed = jnp.zeros((clusters, step * width), F32)
+        for partner in range(partners):
+            part = slice(partner * clusters, (partner + 1) * clusters)
+            direct += gathered[part] * even_ref[part, columns]
+            crossed += gathered[part] * odd_ref[part, columns]
+        for row in range(step):
+            own = slice(row * width, (row + 1) * width)
+            out[pl.ds(first + row, clusters, stride=rows), :] = direct[:, own] + jnp.roll(crossed[:, own], width // 2, axis=1)
 
 
 def coarse_columns(real, imag, cos_ref, sin_ref, wide_ref):
@@ -391,7 +388,7 @@
     near, away, free = (pl.BlockSpec(memory_space=space) for space in (pltpu.VMEM, pltpu.HBM, pl.ANY))
     return pl.pallas_call(
         kernel,
-        out_shape=outs,
+        out_shape=[leaf if place in far else pltpu.VMEM(leaf.shape, leaf.dtype) for place, leaf in enumerate(outs)],
         in_specs=[away] * len(remote) + [near] * len(args) + [free] * len(after),
         out_specs=[free if place in far else near for place in range(len(outs))],
         scratch_shapes=scratch,
@@ -452,16 +449,16 @@
         [*neighbours, partial, cosine, sine, wide, up],
         1_500_000_000,
         "aggregate",
-        far=(0,),
-        scratch=[pltpu.VMEM((devices, rows_all, width), F32), pltpu.SemaphoreType.DMA((blocks,))],
+        after=phases,
     )
     arrived = exchange(outgoing)
-    down, hot, factors, *turned_parts = call(
+    down, hot, even, odd, *turned_parts = call(
         bind(tables_kernel, groups, sources, own),
         [
             struct((sources, 2, long, tall), BF16),
-            struct((partners * clusters, 3 * clusters + 3 * vectors), BF16),
-            struct((rows, 3 * vectors, 2 * width), BF16),
+            struct((partners * clusters, 3 * clusters), BF16),
+            struct((partners * clusters, rows * width), F32),
+            struct((partners * clusters, rows * width), F32),
         ]
         + [struct((tall, azimuth), F32)] * (2 * sources - 2),
         phases,
@@ -473,7 +470,7 @@
     (translated,) = call(
         bind(translate_kernel, rows),
         [struct((clusters * rows, width), F32)],
-        [hot, factors, arrived.reshape(clusters * rows, width)],
+        [hot, even, odd, arrived.reshape(clusters * rows, width)],
         600_000_000,
         "translate",
     )

time: 40.6 us -> 44.5 us (1.096)
  local copies, waits for them, and re-layouts: 1.79 us -> 7.7 us
  waiting for transfers between devices: 4.88 us -> 2.86 us
    unnamed x10 -> x24, local copies, waits for them, and re-layouts: 1.79 us -> 7.7 us
    ppermute x1, waiting for transfers between devices: 1.23 us -> 0.01 us  [per_device(): phases = [lax.ppermute(phase, 'samp', way) for way in ways]]
    all_to_all x1, waiting for transfers between devices: 3.41 us -> 2.65 us  [exchange(): lax.all_to_all(blocks, 'clus', split_axis=0, concat_axis=0, tiled=True)]
  transfers between devices with their start and end apart: 4 -> 4, of which waited for: 3 -> 2; matrix products, arithmetic and copies ran while one was open for 0% -> 0% of each run, Pallas kernels for 16% -> 16%
where the time goes in v6:
time: 44.5 us; the launch traced here: 44.1 us
  blocking collectives  12.3 us (28%)
  Pallas kernels  11.6 us (26%)
  starting transfers between devices  8.89 us (20%)
  local copies, waits for them, and re-layouts  7.7 us (17%)
  waiting for transfers between devices  2.86 us (6%)
  between operations  0.73 us (2%)
    all_to_all x1, blocking collectives, exchange(): lax.all_to_all(blocks, 'clus', split_axis=0, concat_axis=0, tiled=True)  12.3 us
    pallas_call x6, Pallas kernels, call(): pl.pallas_call(kernel, out_shape=[leaf if place in far else pltpu.VMEM(le...  11.6 us
    all_to_all x1, starting transfers between devices, exchange(): lax.all_to_all(blocks, 'clus', split_axis=0, concat_axis=0, tiled=True)  8.29 us
    unnamed x24, local copies, waits for them, and re-layouts  7.7 us
    all_to_all x1, waiting for transfers between devices, exchange(): lax.all_to_all(blocks, 'clus', split_axis=0, concat_axis=0, tiled=True)  2.65 us
  transfers between devices with their start and end apart: 4, of which 2 were waited for; matrix products, arithmetic and copies ran while one was open for 0% of the time, Pallas kernels for 16%

profile of v6, /device:TPU:0, one launch (start us, length us, event | category | flops | bytes accessed | tf_op | source)
XLA Modules:
  0.0 44.1 jit_solution(18352323569220085394)
XLA Ops:
  0.6 0.5 %collective-permute-start.1 = (f32[768,128]{1,0:T(8,128)}, f32[768,128]{1,0:T(8,128)S(1)}, u32[]{:S(2)}, u32[]{:S(2)}) collective-permute-start(f32[768,128]{1,0:T(8,128)} %bitcast.29), channel_id=1, source_target_pairs={{0,1},{1,0},{2,3},{3,2},{4,5},{5,4},{6,7},{7,6},{8,9},{9,8},{10,11... | collective-permute-start | bytes 1179656 | tf_op jit(solution)/shard_map/ppermute | solution.py:424
  1.1 0.1 collective-permute-start
  1.2 2.7 %prepare.1 = (f32[192,1024]{1,0:T(8,128)S(1)}, f32[192,1024]{1,0:T(8,128)S(1)}, bf16[4,512,256]{2,1,0:T(8,128)(2,1)S(1)}, bf16[2,2,192,96]{3,2,1,0:T(8,128)(2,1)S(1)}, f32[384,512]{1,0:T(8,128)S(1)}) custom-call(f32[6,9]{1,0:T(8,128)} %refs_0_.3, f32[48,1024]{1,0:T(8,128)} %bitcast.32, s32[6,1024]{1,0:T(8,128)} %bitcast.34, f32[6,1024]{1,0:T(8,128)} %bitcast.35, ...), custom_call_target="tpu_custom_call" | custom-call | flops 400000000 | bytes 5390552 | tf_op jit(solution)/shard_map/prepare/pallas_call | solution.py:389
  3.9 0.0 collective-permute-done.refs_6_.refs_4_
  4.0 0.0 collective-permute-done.1.refs_0_
  4.0 2.0 %aggregate.1.refs_5_ = f32[16,24,128]{2,1,0:T(8,128)} custom-call(f32[768,128]{1,0:T(8,128)S(1)} %collective-permute-done.1.refs_0_, f32[384,512]{1,0:T(8,128)S(1)} %get-tuple-element.15.refs_1_, f32[192,1024]{1,0:T(8,128)S(1)} %get-tuple-element.16.refs_2_.refs_1_, f32[192,1024]{1,0:T(8,128)S(1)} %get-tuple-element.17.refs_3_.refs_2_, ...), custom_call_target="tpu_custom_call" | custom-call | flops 1500000000 | bytes 5341184 | tf_op jit(solution)/shard_map/aggregate/pallas_call | solution.py:389
  6.0 0.0 copy-start.2
  6.0 1.0 %copy-done.2 = bf16[4,512,256]{2,1,0:T(8,128)(2,1)} copy-done((bf16[4,512,256]{2,1,0:T(8,128)(2,1)}, bf16[4,512,256]{2,1,0:T(8,128)(2,1)S(1)}, u32[]{:S(2)}) %copy-start.2) | copy-done | bytes 1048600
  7.0 0.0 copy-start.4
  7.0 0.9 %copy-done.4 = f32[192,1024]{1,0:T(8,128)} copy-done((f32[192,1024]{1,0:T(8,128)}, f32[192,1024]{1,0:T(8,128)S(1)}, u32[]{:S(2)}) %copy-start.4) | copy-done | bytes 786456
  7.9 0.0 copy-start.6
  7.9 0.9 %copy-done.6 = f32[192,1024]{1,0:T(8,128)} copy-done((f32[192,1024]{1,0:T(8,128)}, f32[192,1024]{1,0:T(8,128)S(1)}, u32[]{:S(2)}) %copy-start.6) | copy-done | bytes 786456
  8.8 8.3 %all-to-all-start = ((f32[16,24,128]{2,1,0:T(8,128)}), f32[16,24,128]{2,1,0:T(8,128)S(1)}, u32[]{:S(2)}, u32[]{:S(2)}) async-start(f32[16,24,128]{2,1,0:T(8,128)} %aggregate.1.refs_5_), calls=%async_computation | async-start | bytes 393216 | tf_op jit(solution)/shard_map/all_to_all | solution.py:406
  17.1 3.0 %tables.1 = (bf16[2,2,96,192]{3,2,1,0:T(8,128)(2,1)S(1)}, bf16[768,192]{1,0:T(8,128)(2,1)S(1)}, f32[768,768]{1,0:T(8,128)S(1)}, f32[768,768]{1,0:T(8,128)S(1)}, ...) custom-call(f32[6,9]{1,0:T(8,128)} %refs_0_.3, s32[12,64]{1,0:T(8,128)} %bitcast.36, s32[12,64]{1,0:T(8,128)} %bitcast.37, ...), custom_call_target="tpu_custom_call" | custom-call | flops 600000000 | bytes 7428312 | tf_op jit(solution)/shard_map/tables/pallas_call | solution.py:389
  20.0 0.0 copy-start
  20.0 1.4 %copy-done = f32[768,768]{1,0:T(8,128)} copy-done((f32[768,768]{1,0:T(8,128)}, f32[768,768]{1,0:T(8,128)S(1)}, u32[]{:S(2)}) %copy-start) | copy-done | bytes 2359320
  21.5 0.0 copy-start.8
  21.5 0.9 %copy-done.8 = f32[192,1024]{1,0:T(8,128)} copy-done((f32[192,1024]{1,0:T(8,128)}, f32[192,1024]{1,0:T(8,128)S(1)}, u32[]{:S(2)}) %copy-start.8) | copy-done | bytes 786456
  22.4 0.0 copy-start.10
  22.4 0.9 %copy-done.10 = f32[192,1024]{1,0:T(8,128)} copy-done((f32[192,1024]{1,0:T(8,128)}, f32[192,1024]{1,0:T(8,128)S(1)}, u32[]{:S(2)}) %copy-start.10) | copy-done | bytes 786456
  23.3 2.7 %all-to-all-done = f32[16,24,128]{2,1,0:T(8,128)S(1)} async-done(((f32[16,24,128]{2,1,0:T(8,128)}), f32[16,24,128]{2,1,0:T(8,128)S(1)}, u32[]{:S(2)}, u32[]{:S(2)}) %all-to-all-start) | async-done | bytes 196640 | tf_op jit(solution)/shard_map/all_to_all | solution.py:406
  25.9 0.0 copy-start.1
  25.9 1.7 %copy-done.1 = f32[768,768]{1,0:T(8,128)S(1)} copy-done((f32[768,768]{1,0:T(8,128)S(1)}, f32[768,768]{1,0:T(8,128)}, u32[]{:S(2)}) %copy-start.1) | copy-done | bytes 2359320
  27.6 0.0 copy-start.3
  27.6 0.0 copy-start.5
  27.6 0.0 copy-start.7
  27.6 0.7 %translate.1 = f32[384,128]{1,0:T(8,128)S(1)} custom-call(bf16[768,192]{1,0:T(8,128)(2,1)S(1)} %get-tuple-element.20.refs_0_, f32[768,768]{1,0:T(8,128)S(1)} %get-tuple-element.21.refs_1_, f32[768,768]{1,0:T(8,128)S(1)} %copy-done.1, f32[384,128]{1,0:T(8,128)S(1)} %bitcast.27), custom_call_target="tpu_custom_call" | custom-call | flops 600000000 | bytes 5701632 | tf_op jit(solution)/shard_map/translate/pallas_call | solution.py:389
  28.3 12.3 %all_to_all.10.refs_0_ = f32[16,24,128]{2,1,0:T(8,128)S(1)} all-to-all(f32[16,24,128]{2,1,0:T(8,128)S(1)} %bitcast.28), channel_id=1, replica_groups=mesh['clus'=16,'samp'=2] {'clus'}, dimensions={0} | all-to-all | bytes 393216 | tf_op jit(solution)/shard_map/all_to_all | solution.py:406
  40.6 0.0 collective-permute-start.2
  40.6 0.0 copy-done.3
  40.6 0.0 copy-done.5
  40.6 0.0 copy-done.7
  40.7 0.0 copy-start.9
  40.7 0.0 copy-start.11
  40.7 1.2 %lower.1 = (f32[384,128]{1,0:T(8,128)}, f32[192,512]{1,0:T(8,128)S(1)}) custom-call(f32[16,24,128]{2,1,0:T(8,128)S(1)} %all_to_all.10.refs_0_, f32[192,1024]{1,0:T(8,128)S(1)} %copy-done.5, f32[192,1024]{1,0:T(8,128)S(1)} %copy-done.7, bf16[4,512,256]{2,1,0:T(8,128)(2,1)S(1)} %copy-done.3, bf16[2,2,96,192]{3,2,1,0:T(8,128)(2,1)S(1)} %get-tuple-element.23.refs_4_), custom_call_target="tpu_custom_call" | custom-call | flops 1500000000 | bytes 4751360 | tf_op jit(solution)/shard_map/lower/pallas_call | solution.py:389
  41.9 0.2 collective-permute-done.2.refs_0_
  42.1 0.0 copy-done.9
  42.1 0.0 copy-done.11
  42.1 2.0 %finish.1 = f32[768,128]{1,0:T(8,128)} custom-call(f32[16,24,128]{2,1,0:T(8,128)S(1)} %collective-permute-done.2.refs_0_, f32[192,1024]{1,0:T(8,128)S(1)} %copy-done.9, f32[192,1024]{1,0:T(8,128)S(1)} %copy-done.11, bf16[4,512,256]{2,1,0:T(8,128)(2,1)S(1)} %copy-done.3, bf16[2,2,96,192]{3,2,1,0:T(8,128)(2,1)S(1)} %get-tuple-element.23.refs_4_, ...), custom_call_target="tpu_custom_call" | custom-call | flops 1500000000 | bytes 4947968 | tf_op jit(solution)/shard_map/finish/pallas_call | solution.py:389
Async XLA Ops:
  0.6 3.3 %collective-permute-start.1 = (f32[768,128]{1,0:T(8,128)}, f32[768,128]{1,0:T(8,128)S(1)}, u32[]{:S(2)}, u32[]{:S(2)}) collective-permute-start(f32[768,128]{1,0:T(8,128)} %bitcast.29), channel_id=1, source_target_pairs={{0,1},{1,0},{2,3},{3,2},{4,5},{5,4},{6,7},{7,6},{8,9},{9,8},{10,11... | collective-permute-start | bytes 1179656 | tf_op jit(solution)/shard_map/ppermute | solution.py:424
  1.1 2.8 %collective-permute-start = (f32[48,1024]{1,0:T(8,128)}, f32[48,1024]{1,0:T(8,128)S(1)}, u32[]{:S(2)}, u32[]{:S(2)}) collective-permute-start(f32[48,1024]{1,0:T(8,128)} %bitcast.31), channel_id=1, source_target_pairs={{1,0},{0,1},{3,2},{2,3},{5,4},{4,5},{7,6},{6,7},{9,8},{8,9},{11,10... | collective-permute-start | bytes 589832 | tf_op jit(solution)/shard_map/ppermute | solution.py:430
  6.0 1.0 %copy-start.2 = (bf16[4,512,256]{2,1,0:T(8,128)(2,1)}, bf16[4,512,256]{2,1,0:T(8,128)(2,1)S(1)}, u32[]{:S(2)}) copy-start(bf16[4,512,256]{2,1,0:T(8,128)(2,1)S(1)} %get-tuple-element.18.refs_4_.refs_3_) | copy-start | bytes 3145732
  7.0 0.9 %copy-start.4 = (f32[192,1024]{1,0:T(8,128)}, f32[192,1024]{1,0:T(8,128)S(1)}, u32[]{:S(2)}) copy-start(f32[192,1024]{1,0:T(8,128)S(1)} %get-tuple-element.16.refs_2_.refs_1_) | copy-start | bytes 2359300
  7.9 0.9 %copy-start.6 = (f32[192,1024]{1,0:T(8,128)}, f32[192,1024]{1,0:T(8,128)S(1)}, u32[]{:S(2)}) copy-start(f32[192,1024]{1,0:T(8,128)S(1)} %get-tuple-element.17.refs_3_.refs_2_) | copy-start | bytes 2359300
  8.8 17.2 %all-to-all-start = ((f32[16,24,128]{2,1,0:T(8,128)}), f32[16,24,128]{2,1,0:T(8,128)S(1)}, u32[]{:S(2)}, u32[]{:S(2)}) async-start(f32[16,24,128]{2,1,0:T(8,128)} %aggregate.1.refs_5_), calls=%async_computation | async-start | bytes 393216 | tf_op jit(solution)/shard_map/all_to_all | solution.py:406
  20.0 1.4 %copy-start = (f32[768,768]{1,0:T(8,128)}, f32[768,768]{1,0:T(8,128)S(1)}, u32[]{:S(2)}) copy-start(f32[768,768]{1,0:T(8,128)S(1)} %get-tuple-element.22.refs_2_) | copy-start | bytes 7077892
  21.5 0.9 %copy-start.8 = (f32[192,1024]{1,0:T(8,128)}, f32[192,1024]{1,0:T(8,128)S(1)}, u32[]{:S(2)}) copy-start(f32[192,1024]{1,0:T(8,128)S(1)} %get-tuple-element.25.refs_1_) | copy-start | bytes 2359300
  22.4 0.9 %copy-start.10 = (f32[192,1024]{1,0:T(8,128)}, f32[192,1024]{1,0:T(8,128)S(1)}, u32[]{:S(2)}) copy-start(f32[192,1024]{1,0:T(8,128)S(1)} %get-tuple-element.26.refs_2_) | copy-start | bytes 2359300
  25.9 1.7 %copy-start.1 = (f32[768,768]{1,0:T(8,128)S(1)}, f32[768,768]{1,0:T(8,128)}, u32[]{:S(2)}) copy-start(f32[768,768]{1,0:T(8,128)} %copy-done) | copy-start | bytes 7077892
  27.6 13.0 %copy-start.3 = (bf16[4,512,256]{2,1,0:T(8,128)(2,1)S(1)}, bf16[4,512,256]{2,1,0:T(8,128)(2,1)}, u32[]{:S(2)}) copy-start(bf16[4,512,256]{2,1,0:T(8,128)(2,1)} %copy-done.2) | copy-start | bytes 3145732
  27.6 13.0 %copy-start.5 = (f32[192,1024]{1,0:T(8,128)S(1)}, f32[192,1024]{1,0:T(8,128)}, u32[]{:S(2)}) copy-start(f32[192,1024]{1,0:T(8,128)} %copy-done.4) | copy-start | bytes 2359300
  27.6 13.0 %copy-start.7 = (f32[192,1024]{1,0:T(8,128)S(1)}, f32[192,1024]{1,0:T(8,128)}, u32[]{:S(2)}) copy-start(f32[192,1024]{1,0:T(8,128)} %copy-done.6) | copy-start | bytes 2359300
  40.6 1.4 %collective-permute-start.2 = (f32[16,24,128]{2,1,0:T(8,128)S(1)}, f32[16,24,128]{2,1,0:T(8,128)S(1)}, u32[]{:S(2)}, u32[]{:S(2)}) collective-permute-start(f32[16,24,128]{2,1,0:T(8,128)S(1)} %all_to_all.10.refs_0_), channel_id=1, source_target_pairs={{1,0},{0,1},{3,2},{2,3},{5,4},{4,5},{7,6},{6,7},{9,8},{8,9},{11,10... | collective-permute-start | bytes 589832 | tf_op jit(solution)/shard_map/ppermute | solution.py:488
  40.7 1.4 %copy-start.9 = (f32[192,1024]{1,0:T(8,128)S(1)}, f32[192,1024]{1,0:T(8,128)}, u32[]{:S(2)}) copy-start(f32[192,1024]{1,0:T(8,128)} %copy-done.8) | copy-start | bytes 2359300
  40.7 1.4 %copy-start.11 = (f32[192,1024]{1,0:T(8,128)S(1)}, f32[192,1024]{1,0:T(8,128)}, u32[]{:S(2)}) copy-start(f32[192,1024]{1,0:T(8,128)} %copy-done.10) | copy-start | bytes 2359300

commit v7 on v6

v7 whole, which is shorter than its diff:
```python
import jax
import jax.numpy as jnp
from jax import lax
from jax.experimental import pallas as pl
from jax.experimental.pallas import tpu as pltpu
from jax.sharding import PartitionSpec as P

P_SIZE = 6
OCTANTS = 8
TILE = 128
PAIR = 2 * TILE
HALF = TILE // 2
VMEM_BYTES = 8 * 1024 * 1024
F32 = jnp.float32
BF16 = jnp.bfloat16

SIN_TERMS = (-1 / 6, 1 / 120, -1 / 5040, 1 / 362880, -1 / 39916800, 1 / 6227020800)
COS_TERMS = (-1 / 2, 1 / 24, -1 / 720, 1 / 40320, -1 / 3628800, 1 / 479001600, -1 / 87178291200)


def split_two(value):
    high = value.astype(BF16)
    return high, (value - high.astype(F32)).astype(BF16)


def split_three(value):
    high = value.astype(BF16)
    rest = value - high.astype(F32)
    middle = rest.astype(BF16)
    return high, middle, (rest - middle.astype(F32)).astype(BF16)


def product(left, right, left_dim=1, right_dim=0):
    return lax.dot_general(left, right, (((left_dim,), (right_dim,)), ((), ())), preferred_element_type=F32)


def series(square, terms):
    total = jnp.full_like(square, terms[-1])
    for term in terms[-2::-1]:
        total = total * square + term
    return total


def iota(shape, dim):
    return lax.broadcasted_iota(jnp.int32, shape, dim)


def one_hot(flags):
    return flags.astype(F32).astype(BF16)


def turned(block):
    return jnp.roll(block, HALF, axis=1)


def folded(theta, sources, own):
    below, middle, above = theta[:, :own], theta[:, own : 2 * own], theta[:, 2 * own :]
    return jnp.concatenate((middle, below + above) if sources == 2 else (middle, below, above), axis=1)


def turns(phase):
    half = 0.5 * phase
    square = half * half
    sine = half + half * square * series(square, SIN_TERMS)
    cosine = 1.0 + square * series(square, COS_TERMS)
    return 1.0 - 2.0 * sine * sine, 2.0 * sine * cosine


def started(remote, local, sems):
    copies = [pltpu.make_async_copy(source, target, sems.at[place]) for place, (source, target) in enumerate(zip(remote, local))]
    for copy in copies:
        copy.start()
    return copies


def prepare_kernel(sources, own, *refs):
    count = 5
    remote, outs, rest = refs[:count], refs[count : count + 5], refs[count + 5 :]
    cos_ref, sin_ref, wide_ref, polar_ref, field_out = outs
    theta_ref, phase_ref, stencil_ref, weight_ref, sems = rest
    copies = started(remote, [theta_ref, phase_ref, stencil_ref, weight_ref, field_out], sems)
    rows = theta_ref.shape[0]
    blocks = wide_ref.shape[0]

    wide = sources * own
    at_row = one_hot(iota((rows * wide, rows), 0) // wide == iota((rows * wide, rows), 1))
    keep = iota((rows * wide, wide), 0) % wide == iota((rows * wide, wide), 1)
    ones = jnp.ones((wide, TILE), BF16)
    copies[0].wait()
    parts = [
        product(jnp.where(keep, product(at_row, part), 0.0).astype(BF16), ones)
        for part in split_three(folded(theta_ref[...], sources, own))
    ]
    polar_ref[...] = parts[0] + (parts[1] + parts[2])

    copies[1].wait()
    cos_ref[...], sin_ref[...] = turns(phase_ref[...])

    copies[2].wait()
    copies[3].wait()
    for block in range(blocks):
        columns = slice(block * PAIR, (block + 1) * PAIR)
        after, before = (block + 1) % blocks, (block - 1) % blocks
        pieces = (
            (0, TILE, block * TILE),
            (TILE, 16, after * TILE),
            (PAIR - 16, 16, before * TILE + TILE - 16),
        )
        for start, size, first in pieces:
            child = iota((size, PAIR), 0) + first
            total = jnp.zeros((size, PAIR), F32)
            for point in range(P_SIZE):
                hit = stencil_ref[point : point + 1, columns] == child
                total = jnp.where(hit, weight_ref[point : point + 1, columns], total)
            high, low = split_two(total)
            wide_ref[block, start : start + size, :] = high
            wide_ref[block, PAIR + start : PAIR + start + size, :] = low
        empty = jnp.zeros((TILE - 32, PAIR), BF16)
        wide_ref[block, TILE + 16 : PAIR - 16, :] = empty
        wide_ref[block, PAIR + TILE + 16 : 2 * PAIR - 16, :] = empty
    copies[4].wait()


def polar_splat(polar_ref, row, width):
    return jnp.concatenate([polar_ref[row : row + 1, :]] * (width // TILE), axis=1)


def aggregate_kernel(groups, sources, own, devices, *refs):
    fields = refs[:sources]
    cos_ref, sin_ref, wide_ref, polar_ref = refs[sources : sources + 4]
    out, high_s, low_s = refs[-3:]
    blocks = wide_ref.shape[0]
    rows = cos_ref.shape[0] // OCTANTS
    columns = cos_ref.shape[1] // devices
    size = 2 * groups
    wide = sources * own
    row_stride = 2 * blocks
    child_stride = OCTANTS * own * row_stride

    for octant in range(OCTANTS):
        given = []
        for field in fields:
            for row in range(own):
                start = (octant * own + row) * row_stride
                given.append(
                    jnp.concatenate(
                        [
                            jnp.concatenate(
                                [field[pl.ds(start + 2 * block + part, groups, stride=child_stride), :] for part in range(2)],
                                axis=0,
                            )
                            for block in range(blocks)
                        ],
                        axis=1,
                    )
                )
        for first in range(0, rows, 2):
            pair = []
            for row in (first, first + 1):
                total = given[0] * polar_splat(polar_ref, row * wide, blocks * TILE)
                for place in range(1, wide):
                    total += given[place] * polar_splat(polar_ref, row * wide + place, blocks * TILE)
                pair.append(total)
            high, low = split_two(jnp.concatenate(pair, axis=0))
            target = slice((octant * rows + first) * size, (octant * rows + first + 2) * size)
            high_s[target, :] = high
            low_s[target, :] = low

    lane = iota((OCTANTS * rows * size, TILE), 1)

    def windows(value, block):
        main = value[:, block * TILE : (block + 1) * TILE]
        after, before = (block + 1) % blocks, (block - 1) % blocks
        rim = jnp.where(lane < HALF, value[:, after * TILE : (after + 1) * TILE], value[:, before * TILE : (before + 1) * TILE])
        return [main, rim]

    for block in range(blocks):
        one, two = windows(high_s, block), windows(low_s, block)
        left = jnp.concatenate(one + two + one, axis=1)
        right = jnp.concatenate([wide_ref[block, :PAIR], wide_ref[block, :PAIR], wide_ref[block, PAIR:]], axis=0)
        spread = product(left, right)
        part = slice(block * PAIR, (block + 1) * PAIR)
        summed = []
        for row in range(rows):
            direct = jnp.zeros((size, PAIR), F32)
            crossed = jnp.zeros((size, PAIR), F32)
            for octant in range(OCTANTS):
                start = (octant * rows + row) * size
                turn = slice(row * OCTANTS + octant, row * OCTANTS + octant + 1)
                direct += spread[start : start + size] * cos_ref[turn, part]
                crossed += spread[start : start + size] * sin_ref[turn, part]
            summed.append(direct + jnp.concatenate([-crossed[groups:], crossed[:groups]], axis=0))
        for first in range(0, rows, 2):
            target = slice(first // 2 * size, (first // 2 + 1) * size)
            for place, piece in enumerate(packed_pieces(summed[first], summed[first + 1], columns)):
                out[block * PAIR // columns + place, target, :] = piece


def packed_pieces(one, two, columns):
    found = []
    if columns == HALF:
        lane = iota((one.shape[0], TILE), 1)
        for start in range(0, one.shape[1], TILE):
            a, b = one[:, start : start + TILE], two[:, start : start + TILE]
            found.append(jnp.where(lane < HALF, a, turned(b)))
            found.append(jnp.where(lane < HALF, turned(a), b))
        return found
    for start in range(0, one.shape[1], columns):
        found.append(jnp.concatenate([one[:, start : start + columns], two[:, start : start + columns]], axis=1))
    return found


def unpacked_pieces(blocks, columns):
    if columns == HALF:
        one, two = [], []
        for a, b in zip(blocks[::2], blocks[1::2]):
            lane = iota(a.shape, 1)
            one.append(jnp.where(lane < HALF, a, turned(b)))
            two.append(jnp.where(lane < HALF, turned(a), b))
        return [jnp.concatenate(one, axis=1), jnp.concatenate(two, axis=1)]
    return [
        jnp.concatenate([block[:, :columns] for block in blocks], axis=1),
        jnp.concatenate([block[:, columns:] for block in blocks], axis=1),
    ]


def tables_kernel(groups, sources, rows, *refs):
    count = 3
    remote, phases = refs[:count], refs[count : count + sources - 1]
    outs = refs[count + sources : -count - 1]
    local, sems = refs[-count - 1 : -1], refs[-1]
    listed_ref, vector_ref, table_ref = local
    hot_ref, chosen_ref, table_out, *turned_refs = outs
    copies = started(remote, local, sems)
    for place, phase in enumerate(phases):
        turned_refs[2 * place][...], turned_refs[2 * place + 1][...] = turns(phase[...])

    copies[2].wait()
    raw = table_ref[...]
    many, width = raw.shape
    vectors = many // (2 * rows)
    at, place = iota((many, many), 1), iota((many, many), 0)
    order = one_hot(at == place % vectors * (2 * rows) + place // (2 * vectors) * 2 + place // vectors % 2)
    twice = one_hot(iota((width, 2 * width), 1) % width == iota((width, 2 * width), 0))
    lane = iota((vectors, 2 * width), 1)
    for piece, part in enumerate(split_three(raw)):
        double = product(product(order, part).astype(BF16), twice)
        target = slice(piece * vectors, (piece + 1) * vectors)
        for kind in range(2):
            for first in range(0, rows, 2):
                one, two = (double[(2 * row + kind) * vectors : (2 * row + kind + 1) * vectors] for row in (first, first + 1))
                start = (kind * rows + first) * width
                table_out[target, start : start + 2 * width] = jnp.where(lane < width, one, two).astype(BF16)

    copies[0].wait()
    copies[1].wait()
    partners, clusters = listed_ref.shape
    unit = one_hot(iota((clusters, clusters), 0) == iota((clusters, clusters), 1))
    listed = listed_ref[...]
    at = (listed // groups * (2 * groups) + listed % groups).astype(F32)
    at = sum(product(unit, half, 1, 1) for half in split_two(at))
    chosen = sum(product(unit, half, 1, 1) for half in split_two(vector_ref[...].astype(F32)))
    arrived = (iota((clusters, 4 * clusters), 1) % (2 * clusters)).astype(F32)
    vector = (iota((clusters, 3 * vectors), 1) % vectors).astype(F32)
    for partner in range(partners):
        for part in range(2):
            start = (part * partners + partner) * clusters
            hot_ref[start : start + clusters, :] = one_hot(arrived == at[:, partner : partner + 1] + float(part * groups))
        start = partner * clusters
        chosen_ref[start : start + clusters, :] = one_hot(vector == chosen[:, partner : partner + 1])


def translate_kernel(groups, hot_ref, chosen_ref, table_ref, arrived_ref, out):
    devices, tall, width = arrived_ref.shape
    clusters = devices * groups
    partners = chosen_ref.shape[0] // clusters
    size = 2 * groups
    steps = tall // size
    count = partners * clusters
    source = jnp.concatenate(
        [arrived_ref[:, step * size : (step + 1) * size, :].reshape(devices * size, width) for step in range(steps)], axis=1
    )
    gathered = product(hot_ref[...], jnp.concatenate(split_two(source), axis=0))
    factors = product(chosen_ref[...], table_ref[...])
    for step in range(steps):
        lanes = slice(step * width, (step + 1) * width)
        other = slice((steps + step) * width, (steps + step + 1) * width)
        real = jnp.zeros((clusters, width), F32)
        imag = jnp.zeros((clusters, width), F32)
        for partner in range(partners):
            part = slice(partner * clusters, (partner + 1) * clusters)
            cross = slice(count + partner * clusters, count + (partner + 1) * clusters)
            a, b = gathered[part, lanes], gathered[cross, lanes]
            real += a * factors[part, lanes] - b * factors[part, other]
            imag += a * factors[part, other] + b * factors[part, lanes]
        for device in range(devices):
            rows = slice(device * groups, (device + 1) * groups)
            out[device, step * size : (step + 1) * size, :] = jnp.concatenate([real[rows], imag[rows]], axis=0)


def unpacked_fields(arrived_ref, size, columns):
    fields = []
    for start in range(0, arrived_ref.shape[1], size):
        fields += unpacked_pieces([arrived_ref[device, start : start + size, :] for device in range(arrived_ref.shape[0])], columns)
    return fields


def coarse_columns(fields, cos_ref, sin_ref, wide_ref):
    blocks = wide_ref.shape[0]
    rows, size = len(fields), fields[0].shape[0]
    groups = size // 2
    crossed = [jnp.concatenate([field[groups:], -field[:groups]], axis=0) for field in fields]
    mains, rims = [], []
    for block in range(blocks):
        part = slice(block * PAIR, (block + 1) * PAIR)
        lowered = []
        for octant in range(OCTANTS):
            for row in range(rows):
                turn = slice(row * OCTANTS + octant, row * OCTANTS + octant + 1)
                lowered.append(fields[row][:, part] * cos_ref[turn, part] + crossed[row][:, part] * sin_ref[turn, part])
        high, low = split_two(jnp.concatenate(lowered, axis=0))
        left = jnp.concatenate([high, low, high], axis=1)
        right = jnp.concatenate([wide_ref[block, :PAIR], wide_ref[block, :PAIR], wide_ref[block, PAIR:]], axis=1)
        both = product(left, right, 1, 1)
        mains.append(both[:, :TILE])
        rims.append(both[:, TILE:])
    lane = iota((OCTANTS * rows * size, TILE), 1)
    return jnp.concatenate(
        [
            mains[block] + jnp.where(lane < HALF, rims[(block - 1) % blocks], rims[(block + 1) % blocks])
            for block in range(blocks)
        ],
        axis=1,
    )


def anterpolated(coarse, polar_ref, octant, place, rows, size, wide):
    total = None
    for row in range(rows):
        start = (octant * rows + row) * size
        term = coarse[start : start + size] * polar_splat(polar_ref, row * wide + place, coarse.shape[1])
        total = term if total is None else total + term
    return total


def lower_kernel(groups, own, arrived_ref, cos_ref, sin_ref, wide_ref, polar_ref, parent_out, partial_ref, parent_ref, sem):
    devices = arrived_ref.shape[0]
    azimuth = cos_ref.shape[1]
    size = 2 * groups
    fields = unpacked_fields(arrived_ref, size, azimuth // devices)
    rows = len(fields)
    wide = polar_ref.shape[0] // rows
    tiles = azimuth // TILE
    for row, field in enumerate(fields):
        for tile in range(tiles):
            for part in range(2):
                start = (row * tiles + tile) * 2 + part
                parent_ref[pl.ds(start, groups, stride=rows * tiles * 2), :] = field[
                    part * groups : (part + 1) * groups, tile * TILE : (tile + 1) * TILE
                ]
    copy = pltpu.make_async_copy(parent_ref, parent_out, sem)
    copy.start()
    coarse = coarse_columns(fields, cos_ref, sin_ref, wide_ref)
    for octant in range(OCTANTS):
        for row in range(own):
            start = (octant * own + row) * size
            partial_ref[start : start + size, :] = anterpolated(coarse, polar_ref, octant, row, rows, size, wide)
    copy.wait()


def finish_kernel(groups, sources, own, *refs):
    arrived = refs[: sources - 1]
    turned_refs = refs[sources - 1 : 3 * (sources - 1)]
    wide_ref, polar_ref, partial_ref, out = refs[3 * (sources - 1) :]
    blocks = wide_ref.shape[0]
    azimuth = turned_refs[0].shape[1]
    size = 2 * groups
    coarse = []
    for place, field in enumerate(arrived):
        fields = unpacked_fields(field, size, azimuth // field.shape[0])
        coarse.append(coarse_columns(fields, turned_refs[2 * place], turned_refs[2 * place + 1], wide_ref))
    rows = len(fields)
    wide = sources * own
    row_stride = 2 * blocks
    for octant in range(OCTANTS):
        for row in range(own):
            start = (octant * own + row) * size
            value = partial_ref[start : start + size, :]
            for place in range(sources - 1):
                value += anterpolated(coarse[place], polar_ref, octant, (place + 1) * own + row, rows, size, wide)
            for block in range(blocks):
                for part in range(2):
                    first = (octant * own + row) * row_stride + 2 * block + part
                    out[pl.ds(first, groups, stride=OCTANTS * own * row_stride), :] = value[
                        part * groups : (part + 1) * groups, block * TILE : (block + 1) * TILE
                    ]


def call(kernel, outs, args, flops, name, remote=(), after=(), far=(), scratch=(), into=0):
    held = sum(4 * leaf.size for leaf in outs) + sum(4 * arg.size for arg in (*remote, *args))
    remote = [pltpu.with_memory_space_constraint(arg, pltpu.HBM) for arg in remote]
    scratch = [*scratch, *(pltpu.VMEM(arg.shape, arg.dtype) for arg in remote[: len(remote) - into])]
    if remote:
        scratch.append(pltpu.SemaphoreType.DMA((len(remote),)))
    near, away, free = (pl.BlockSpec(memory_space=space) for space in (pltpu.VMEM, pltpu.HBM, pl.ANY))
    return pl.pallas_call(
        kernel,
        out_shape=outs,
        in_specs=[away] * len(remote) + [near] * len(args) + [free] * len(after),
        out_specs=[free if place in far else near for place in range(len(outs))],
        scratch_shapes=scratch,
        compiler_params=pltpu.CompilerParams(vmem_limit_bytes=max(VMEM_BYTES, 8 * max(arg.size for arg in (*remote, *args)))),
        cost_estimate=pl.CostEstimate(flops=flops, bytes_accessed=held, transcendentals=0),
        name=name,
    )(*remote, *args, *after)


def bind(kernel, *settings):
    return lambda *refs: kernel(*settings, *refs)


def exchange(blocks):
    return lax.all_to_all(blocks, "clus", split_axis=0, concat_axis=0, tiled=True)


def per_device(child_patterns, theta_weights, phi_stencil, phi_weights, shift_phase, translation_table, far_list, far_vector):
    devices, halves = lax.axis_size("clus"), lax.axis_size("samp")
    children, _, own, columns = child_patterns.shape
    groups = children // OCTANTS
    rows, azimuth = theta_weights.shape[0], phi_stencil.shape[0]
    clusters, partners = far_list.shape
    vectors, width = translation_table.shape[0], 2 * translation_table.shape[3]
    blocks, rows_all = columns // TILE, groups * rows
    long = children * own
    sources = 2 if halves == 2 else 3
    struct = jax.ShapeDtypeStruct
    forward = [(i, (i + 1) % halves) for i in range(halves)]
    backward = [((i + 1) % halves, i) for i in range(halves)]

    field = child_patterns.reshape(children, 2, own, blocks, TILE).transpose(0, 2, 3, 1, 4).reshape(long * blocks * 2, TILE)
    neighbours = [lax.ppermute(field, "samp", forward)]
    if sources == 3:
        neighbours.append(lax.ppermute(field, "samp", backward))
    phase = shift_phase.transpose(1, 0, 2).reshape(rows * OCTANTS, azimuth)
    ways = [backward] if sources == 2 else [backward, forward]
    phases = [lax.ppermute(phase, "samp", way) for way in ways]
    table = translation_table.transpose(0, 2, 1, 3).reshape(vectors * rows * 2, width // 2)
    turn = struct((rows * OCTANTS, azimuth), F32)

    cosine, sine, wide, polar, held = call(
        bind(prepare_kernel, sources, own),
        [
            turn,
            turn,
            struct((blocks, 2 * PAIR, PAIR), BF16),
            struct((rows * sources * own, TILE), F32),
            struct(field.shape, F32),
        ],
        [],
        400_000_000,
        "prepare",
        [theta_weights, phase, phi_stencil.T, phi_weights.T, field],
        into=1,
    )
    (outgoing,) = call(
        bind(aggregate_kernel, groups, sources, own, devices),
        [struct((devices, rows_all, width), F32)],
        [held, *neighbours, cosine, sine, wide, polar],
        1_500_000_000,
        "aggregate",
        after=phases,
        scratch=[pltpu.VMEM((2 * groups * OCTANTS * rows, columns), BF16)] * 2,
    )
    arrived = exchange(outgoing)
    hot, chosen, factors, *turned_parts = call(
        bind(tables_kernel, groups, sources, rows),
        [
            struct((2 * partners * clusters, 4 * clusters), BF16),
            struct((partners * clusters, 3 * vectors), BF16),
            struct((3 * vectors, rows * width), BF16),
        ]
        + [turn] * (2 * sources - 2),
        phases,
        600_000_000,
        "tables",
        [far_list.T, far_vector.T, table],
        [outgoing],
    )
    (translated,) = call(
        bind(translate_kernel, groups),
        [struct((devices, rows_all, width), F32)],
        [hot, chosen, factors, arrived],
        600_000_000,
        "translate",
    )
    returned = exchange(translated)
    size = rows_all * 2 * azimuth // TILE
    parent, partial = call(
        bind(lower_kernel, groups, own),
        [struct((size, TILE), F32), struct((2 * long, columns), F32)],
        [returned, cosine, sine, wide, polar],
        1_500_000_000,
        "lower",
        far=(0,),
        scratch=[pltpu.VMEM((size, TILE), F32), pltpu.SemaphoreType.DMA],
    )
    returned_parts = [lax.ppermute(returned, "samp", way) for way in ways]
    (total,) = call(
        bind(finish_kernel, groups, sources, own),
        [struct((long * blocks * 2, TILE), F32)],
        [*returned_parts, *turned_parts, wide, polar, partial],
        1_500_000_000,
        "finish",
    )
    child_incoming = total.reshape(children, own, blocks, 2, TILE).transpose(0, 3, 1, 2, 4).reshape(children, 2, own, columns)
    parent_incoming = (
        parent.reshape(groups, rows, azimuth // TILE, 2, TILE).transpose(0, 3, 1, 2, 4).reshape(groups, 2, rows, azimuth)
    )
    return (parent_incoming, child_incoming)


def solution(mesh):
    placed = (
        P("clus", None, "samp", None),
        P(),
        P(),
        P(),
        P(None, "samp", None),
        P(None, None, "samp", "clus"),
        P(),
        P(),
    )
    return jax.shard_map(
        per_device,
        mesh=mesh,
        in_specs=placed,
        out_specs=(P("clus", None, "samp", None), P("clus", None, "samp", None)),
        check_vma=False,
    )
```

time: 44.5 us -> 38.5 us (0.87)
  local copies, waits for them, and re-layouts: 7.7 us -> 0 us
  waiting for transfers between devices: 2.86 us -> 7.12 us
  Pallas kernels: 11.6 us -> 10.3 us
  blocking collectives: 12.3 us -> 11.3 us
    unnamed x24 -> x0, local copies, waits for them, and re-layouts: 7.7 us -> none
    all_to_all x1, waiting for transfers between devices: 2.65 us -> 6.82 us  [exchange(): lax.all_to_all(blocks, 'clus', split_axis=0, concat_axis=0, tiled=True)]
    pallas_call x6, Pallas kernels: 11.6 us -> 10.3 us  [call(): pl.pallas_call(kernel, out_shape=outs, in_specs=[away] * len(remote) + [n...]
    all_to_all x1, blocking collectives: 12.3 us -> 11.3 us  [exchange(): lax.all_to_all(blocks, 'clus', split_axis=0, concat_axis=0, tiled=True)]
  transfers between devices with their start and end apart: 4 -> 4, of which waited for: 2 -> 2; matrix products, arithmetic and copies ran while one was open for 0% -> 0% of each run, Pallas kernels for 16% -> 13%
where the time goes in v7:
time: 38.5 us; the launch traced here: 38.2 us
  blocking collectives  11.3 us (29%)
  Pallas kernels  10.3 us (27%)
  starting transfers between devices  8.9 us (23%)
  waiting for transfers between devices  7.12 us (18%)
  between operations  0.69 us (2%)
    all_to_all x1, blocking collectives, exchange(): lax.all_to_all(blocks, 'clus', split_axis=0, concat_axis=0, tiled=True)  11.3 us
    pallas_call x6, Pallas kernels, call(): pl.pallas_call(kernel, out_shape=outs, in_specs=[away] * len(remote) + [n...  10.3 us
    all_to_all x1, starting transfers between devices, exchange(): lax.all_to_all(blocks, 'clus', split_axis=0, concat_axis=0, tiled=True)  8.3 us
    all_to_all x1, waiting for transfers between devices, exchange(): lax.all_to_all(blocks, 'clus', split_axis=0, concat_axis=0, tiled=True)  6.82 us
  transfers between devices with their start and end apart: 4, of which 2 were waited for; matrix products, arithmetic and copies ran while one was open for 0% of the time, Pallas kernels for 13%

profile of v7, /device:TPU:0, one launch (start us, length us, event | category | flops | bytes accessed | tf_op | source)
XLA Modules:
  0.0 38.2 jit_solution(9399335383003736540)
XLA Ops:
  0.6 0.5 %collective-permute-start.1 = (f32[768,128]{1,0:T(8,128)}, f32[768,128]{1,0:T(8,128)S(1)}, u32[]{:S(2)}, u32[]{:S(2)}) collective-permute-start(f32[768,128]{1,0:T(8,128)} %bitcast.25), channel_id=1, source_target_pairs={{0,1},{1,0},{2,3},{3,2},{4,5},{5,4},{6,7},{7,6},{8,9},{9,8},{10,11... | collective-permute-start | bytes 1179656 | tf_op jit(solution)/shard_map/ppermute | solution.py:441
  1.1 0.1 collective-permute-start
  1.2 1.8 %prepare.1 = (f32[48,1024]{1,0:T(8,128)S(1)}, f32[48,1024]{1,0:T(8,128)S(1)}, bf16[4,512,256]{2,1,0:T(8,128)(2,1)S(1)}, f32[36,128]{1,0:T(8,128)S(1)}, f32[768,128]{1,0:T(8,128)S(1)}) custom-call(f32[6,9]{1,0:T(8,128)} %refs_0_.1, f32[48,1024]{1,0:T(8,128)} %bitcast.28, s32[6,1024]{1,0:T(8,128)} %bitcast.30, f32[6,1024]{1,0:T(8,128)} %bitcast.31, ...), custom_call_target="tpu_custom_call" | custom-call | flops 400000000 | bytes 3541208 | tf_op jit(solution)/shard_map/prepare/pallas_call | solution.py:406
  3.0 0.0 collective-permute-done.refs_6_.refs_3_
  3.0 0.0 collective-permute-done.1.refs_1_
  3.0 2.3 %aggregate.1.refs_4_ = f32[16,24,128]{2,1,0:T(8,128)} custom-call(f32[768,128]{1,0:T(8,128)S(1)} %get-tuple-element.14.refs_0_, f32[768,128]{1,0:T(8,128)S(1)} %collective-permute-done.1.refs_1_, f32[48,1024]{1,0:T(8,128)S(1)} %get-tuple-element.15.refs_2_.refs_1_, f32[48,1024]{1,0:T(8,128)S(1)} %get-tuple-element.16.refs_3_.refs_2_, ...), custom_call_target="tpu_custom_call" | custom-call | flops 1500000000 | bytes 3491840 | tf_op jit(solution)/shard_map/aggregate/pallas_call | solution.py:406
  5.4 8.3 %all-to-all-start = ((f32[16,24,128]{2,1,0:T(8,128)}), f32[16,24,128]{2,1,0:T(8,128)S(1)}, u32[]{:S(2)}, u32[]{:S(2)}) async-start(f32[16,24,128]{2,1,0:T(8,128)} %aggregate.1.refs_4_), calls=%async_computation | async-start | bytes 393216 | tf_op jit(solution)/shard_map/all_to_all | solution.py:423
  13.7 2.0 %tables.1 = (bf16[1536,256]{1,0:T(8,128)(2,1)S(1)}, bf16[768,48]{1,0:T(8,128)(2,1)S(1)}, bf16[48,768]{1,0:T(8,128)(2,1)S(1)}, f32[48,1024]{1,0:T(8,128)S(1)}, f32[48,1024]{1,0:T(8,128)S(1)}) custom-call(s32[12,64]{1,0:T(8,128)} %bitcast.32, s32[12,64]{1,0:T(8,128)} %bitcast.33, f32[192,64]{1,0:T(8,128)} %bitcast.29, ...), custom_call_target="tpu_custom_call" | custom-call | flops 600000000 | bytes 2512896 | tf_op jit(solution)/shard_map/tables/pallas_call | solution.py:406
  15.7 6.8 %all-to-all-done.refs_3_ = f32[16,24,128]{2,1,0:T(8,128)S(1)} async-done(((f32[16,24,128]{2,1,0:T(8,128)}), f32[16,24,128]{2,1,0:T(8,128)S(1)}, u32[]{:S(2)}, u32[]{:S(2)}) %all-to-all-start) | async-done | bytes 196640 | tf_op jit(solution)/shard_map/all_to_all | solution.py:423
  22.6 1.0 %translate.1 = f32[16,24,128]{2,1,0:T(8,128)S(1)} custom-call(bf16[1536,256]{1,0:T(8,128)(2,1)S(1)} %get-tuple-element.19.refs_0_, bf16[768,48]{1,0:T(8,128)(2,1)S(1)} %get-tuple-element.20.refs_1_, bf16[48,768]{1,0:T(8,128)(2,1)S(1)} %get-tuple-element.21.refs_2_, f32[16,24,128]{2,1,0:T(8,128)S(1)} %all-to-all-done.refs_3_), custom_call_target="tpu_custom_call" | custom-call | flops 600000000 | bytes 2260992 | tf_op jit(solution)/shard_map/translate/pallas_call | solution.py:406
  23.6 11.3 %all_to_all.10.refs_0_ = f32[16,24,128]{2,1,0:T(8,128)S(1)} all-to-all(f32[16,24,128]{2,1,0:T(8,128)S(1)} %translate.1), channel_id=1, replica_groups=mesh['clus'=16,'samp'=2] {'clus'}, dimensions={0} | all-to-all | bytes 393216 | tf_op jit(solution)/shard_map/all_to_all | solution.py:423
  34.8 0.0 collective-permute-start.2
  34.8 1.1 %lower.1 = (f32[384,128]{1,0:T(8,128)}, f32[192,512]{1,0:T(8,128)S(1)}) custom-call(f32[16,24,128]{2,1,0:T(8,128)S(1)} %all_to_all.10.refs_0_, f32[48,1024]{1,0:T(8,128)S(1)} %get-tuple-element.15.refs_2_.refs_1_, f32[48,1024]{1,0:T(8,128)S(1)} %get-tuple-element.16.refs_3_.refs_2_, bf16[4,512,256]{2,1,0:T(8,128)(2,1)S(1)} %get-tuple-element.17.refs_4_.refs_3_, ...), custom_call_target="tpu_custom_call" | custom-call | flops 1500000000 | bytes 3295232 | tf_op jit(solution)/shard_map/lower/pallas_call | solution.py:406
  36.0 0.3 collective-permute-done.2.refs_0_
  36.3 2.0 %finish.1 = f32[768,128]{1,0:T(8,128)} custom-call(f32[16,24,128]{2,1,0:T(8,128)S(1)} %collective-permute-done.2.refs_0_, f32[48,1024]{1,0:T(8,128)S(1)} %get-tuple-element.23.refs_1_, f32[48,1024]{1,0:T(8,128)S(1)} %get-tuple-element.24.refs_2_, bf16[4,512,256]{2,1,0:T(8,128)(2,1)S(1)} %get-tuple-element.17.refs_4_.refs_3_, ...), custom_call_target="tpu_custom_call" | custom-call | flops 1500000000 | bytes 3491840 | tf_op jit(solution)/shard_map/finish/pallas_call | solution.py:406
Async XLA Ops:
  0.6 2.4 %collective-permute-start.1 = (f32[768,128]{1,0:T(8,128)}, f32[768,128]{1,0:T(8,128)S(1)}, u32[]{:S(2)}, u32[]{:S(2)}) collective-permute-start(f32[768,128]{1,0:T(8,128)} %bitcast.25), channel_id=1, source_target_pairs={{0,1},{1,0},{2,3},{3,2},{4,5},{5,4},{6,7},{7,6},{8,9},{9,8},{10,11... | collective-permute-start | bytes 1179656 | tf_op jit(solution)/shard_map/ppermute | solution.py:441
  1.1 1.9 %collective-permute-start = (f32[48,1024]{1,0:T(8,128)}, f32[48,1024]{1,0:T(8,128)S(1)}, u32[]{:S(2)}, u32[]{:S(2)}) collective-permute-start(f32[48,1024]{1,0:T(8,128)} %bitcast.27), channel_id=1, source_target_pairs={{1,0},{0,1},{3,2},{2,3},{5,4},{4,5},{7,6},{6,7},{9,8},{8,9},{11,10... | collective-permute-start | bytes 589832 | tf_op jit(solution)/shard_map/ppermute | solution.py:446
  5.4 17.2 %all-to-all-start = ((f32[16,24,128]{2,1,0:T(8,128)}), f32[16,24,128]{2,1,0:T(8,128)S(1)}, u32[]{:S(2)}, u32[]{:S(2)}) async-start(f32[16,24,128]{2,1,0:T(8,128)} %aggregate.1.refs_4_), calls=%async_computation | async-start | bytes 393216 | tf_op jit(solution)/shard_map/all_to_all | solution.py:423
  34.8 1.4 %collective-permute-start.2 = (f32[16,24,128]{2,1,0:T(8,128)S(1)}, f32[16,24,128]{2,1,0:T(8,128)S(1)}, u32[]{:S(2)}, u32[]{:S(2)}) collective-permute-start(f32[16,24,128]{2,1,0:T(8,128)S(1)} %all_to_all.10.refs_0_), channel_id=1, source_target_pairs={{1,0},{0,1},{3,2},{2,3},{5,4},{4,5},{7,6},{6,7},{9,8},{8,9},{11,10... | collective-permute-start | bytes 589832 | tf_op jit(solution)/shard_map/ppermute | solution.py:507

commit v8 on v7

--- a/solution.py
+++ b/solution.py
@@ -224,7 +224,7 @@
     ]
 
 
-def tables_kernel(groups, sources, rows, *refs):
+def tables_kernel(sources, rows, *refs):
     count = 3
     remote, phases = refs[:count], refs[count : count + sources - 1]
     outs = refs[count + sources : -count - 1]
@@ -256,18 +256,14 @@
     copies[1].wait()
     partners, clusters = listed_ref.shape
     unit = one_hot(iota((clusters, clusters), 0) == iota((clusters, clusters), 1))
-    listed = listed_ref[...]
-    at = (listed // groups * (2 * groups) + listed % groups).astype(F32)
-    at = sum(product(unit, half, 1, 1) for half in split_two(at))
+    listed = sum(product(unit, half, 1, 1) for half in split_two(listed_ref[...].astype(F32)))
     chosen = sum(product(unit, half, 1, 1) for half in split_two(vector_ref[...].astype(F32)))
-    arrived = (iota((clusters, 4 * clusters), 1) % (2 * clusters)).astype(F32)
+    cluster = (iota((clusters, 2 * clusters), 1) % clusters).astype(F32)
     vector = (iota((clusters, 3 * vectors), 1) % vectors).astype(F32)
     for partner in range(partners):
-        for part in range(2):
-            start = (part * partners + partner) * clusters
-            hot_ref[start : start + clusters, :] = one_hot(arrived == at[:, partner : partner + 1] + float(part * groups))
-        start = partner * clusters
-        chosen_ref[start : start + clusters, :] = one_hot(vector == chosen[:, partner : partner + 1])
+        part = slice(partner * clusters, (partner + 1) * clusters)
+        hot_ref[part, :] = one_hot(cluster == listed[:, partner : partner + 1])
+        chosen_ref[part, :] = one_hot(vector == chosen[:, partner : partner + 1])
 
 
 def translate_kernel(groups, hot_ref, chosen_ref, table_ref, arrived_ref, out):
@@ -276,9 +272,9 @@
     partners = chosen_ref.shape[0] // clusters
     size = 2 * groups
     steps = tall // size
-    count = partners * clusters
+    starts = [step * size + part * groups for part in range(2) for step in range(steps)]
     source = jnp.concatenate(
-        [arrived_ref[:, step * size : (step + 1) * size, :].reshape(devices * size, width) for step in range(steps)], axis=1
+        [arrived_ref[:, start : start + groups, :].reshape(clusters, width) for start in starts], axis=1
     )
     gathered = product(hot_ref[...], jnp.concatenate(split_two(source), axis=0))
     factors = product(chosen_ref[...], table_ref[...])
@@ -289,8 +285,7 @@
         imag = jnp.zeros((clusters, width), F32)
         for partner in range(partners):
             part = slice(partner * clusters, (partner + 1) * clusters)
-            cross = slice(count + partner * clusters, count + (partner + 1) * clusters)
-            a, b = gathered[part, lanes], gathered[cross, lanes]
+            a, b = gathered[part, lanes], gathered[part, other]
             real += a * factors[part, lanes] - b * factors[part, other]
             imag += a * factors[part, other] + b * factors[part, lanes]
         for device in range(devices):
@@ -468,14 +463,13 @@
         [held, *neighbours, cosine, sine, wide, polar],
         1_500_000_000,
         "aggregate",
-        after=phases,
         scratch=[pltpu.VMEM((2 * groups * OCTANTS * rows, columns), BF16)] * 2,
     )
     arrived = exchange(outgoing)
     hot, chosen, factors, *turned_parts = call(
-        bind(tables_kernel, groups, sources, rows),
+        bind(tables_kernel, sources, rows),
         [
-            struct((2 * partners * clusters, 4 * clusters), BF16),
+            struct((partners * clusters, 2 * clusters), BF16),
             struct((partners * clusters, 3 * vectors), BF16),
             struct((3 * vectors, rows * width), BF16),
         ]

time: 38.5 us -> 38.4 us (level)
    ppermute x1, waiting for transfers between devices: 0.01 us -> 1.36 us  [per_device(): phases = [lax.ppermute(phase, 'samp', way) for way in ways]]
    all_to_all x1, waiting for transfers between devices: 6.82 us -> 5.7 us  [exchange(): lax.all_to_all(blocks, 'clus', split_axis=0, concat_axis=0, tiled=True)]
  transfers between devices with their start and end apart: 4 -> 4, of which waited for: 2 -> 3; matrix products, arithmetic and copies ran while one was open for 0% -> 0% of each run, Pallas kernels for 13% -> 13%
where the time goes in v8:
time: 38.4 us; the launch traced here: 38.1 us
  blocking collectives  11.3 us (29%)
  Pallas kernels  9.97 us (26%)
  starting transfers between devices  8.82 us (23%)
  waiting for transfers between devices  7.36 us (19%)
  between operations  0.69 us (2%)
    all_to_all x1, blocking collectives, exchange(): lax.all_to_all(blocks, 'clus', split_axis=0, concat_axis=0, tiled=True)  11.3 us
    pallas_call x6, Pallas kernels, call(): pl.pallas_call(kernel, out_shape=outs, in_specs=[away] * len(remote) + [n...  9.97 us
    all_to_all x1, starting transfers between devices, exchange(): lax.all_to_all(blocks, 'clus', split_axis=0, concat_axis=0, tiled=True)  8.15 us
    all_to_all x1, waiting for transfers between devices, exchange(): lax.all_to_all(blocks, 'clus', split_axis=0, concat_axis=0, tiled=True)  5.7 us
    ppermute x1, waiting for transfers between devices, per_device(): phases = [lax.ppermute(phase, 'samp', way) for way in ways]  1.36 us
  transfers between devices with their start and end apart: 4, of which 3 were waited for; matrix products, arithmetic and copies ran while one was open for 0% of the time, Pallas kernels for 13%

profile of v8, /device:TPU:0, one launch (start us, length us, event | category | flops | bytes accessed | tf_op | source)
XLA Modules:
  0.0 38.1 jit_solution(1184314634056350990)
XLA Ops:
  0.6 0.5 %collective-permute-start.1 = (f32[768,128]{1,0:T(8,128)}, f32[768,128]{1,0:T(8,128)S(1)}, u32[]{:S(2)}, u32[]{:S(2)}) collective-permute-start(f32[768,128]{1,0:T(8,128)} %bitcast.25), channel_id=1, source_target_pairs={{0,1},{1,0},{2,3},{3,2},{4,5},{5,4},{6,7},{7,6},{8,9},{9,8},{10,11... | collective-permute-start | bytes 1179656 | tf_op jit(solution)/shard_map/ppermute | solution.py:436
  1.1 1.8 %prepare.1 = (f32[48,1024]{1,0:T(8,128)S(1)}, f32[48,1024]{1,0:T(8,128)S(1)}, bf16[4,512,256]{2,1,0:T(8,128)(2,1)S(1)}, f32[36,128]{1,0:T(8,128)S(1)}, f32[768,128]{1,0:T(8,128)S(1)}) custom-call(f32[6,9]{1,0:T(8,128)} %refs_0_.1, f32[48,1024]{1,0:T(8,128)} %bitcast.27, s32[6,1024]{1,0:T(8,128)} %bitcast.30, f32[6,1024]{1,0:T(8,128)} %bitcast.31, ...), custom_call_target="tpu_custom_call" | custom-call | flops 400000000 | bytes 3541208 | tf_op jit(solution)/shard_map/prepare/pallas_call | solution.py:401
  2.9 0.0 collective-permute-done.1.refs_1_
  3.0 2.3 %aggregate.1.refs_4_ = f32[16,24,128]{2,1,0:T(8,128)} custom-call(f32[768,128]{1,0:T(8,128)S(1)} %get-tuple-element.14.refs_0_, f32[768,128]{1,0:T(8,128)S(1)} %collective-permute-done.1.refs_1_, f32[48,1024]{1,0:T(8,128)S(1)} %get-tuple-element.15.refs_2_.refs_1_, f32[48,1024]{1,0:T(8,128)S(1)} %get-tuple-element.16.refs_3_.refs_2_, ...), custom_call_target="tpu_custom_call" | custom-call | flops 1500000000 | bytes 3491840 | tf_op jit(solution)/shard_map/aggregate/pallas_call | solution.py:401
  5.3 0.0 copy-start
  5.3 8.1 %all-to-all-start = ((f32[16,24,128]{2,1,0:T(8,128)}), f32[16,24,128]{2,1,0:T(8,128)S(1)}, u32[]{:S(2)}, u32[]{:S(2)}) async-start(f32[16,24,128]{2,1,0:T(8,128)} %aggregate.1.refs_4_), calls=%async_computation | async-start | bytes 393216 | tf_op jit(solution)/shard_map/all_to_all | solution.py:418
  13.4 0.0 copy-done
  13.5 0.1 collective-permute-start
  13.6 1.4 %collective-permute-done.refs_3_ = f32[48,1024]{1,0:T(8,128)S(1)} collective-permute-done((f32[48,1024]{1,0:T(8,128)S(1)}, f32[48,1024]{1,0:T(8,128)S(1)}, u32[]{:S(2)}, u32[]{:S(2)}) %collective-permute-start) | collective-permute-done | bytes 196640 | tf_op jit(solution)/shard_map/ppermute | solution.py:441
  15.0 1.9 %tables.1 = (bf16[768,128]{1,0:T(8,128)(2,1)S(1)}, bf16[768,48]{1,0:T(8,128)(2,1)S(1)}, bf16[48,768]{1,0:T(8,128)(2,1)S(1)}, f32[48,1024]{1,0:T(8,128)S(1)}, f32[48,1024]{1,0:T(8,128)S(1)}) custom-call(s32[12,64]{1,0:T(8,128)} %bitcast.32, s32[12,64]{1,0:T(8,128)} %bitcast.33, f32[192,64]{1,0:T(8,128)} %bitcast.29, ...), custom_call_target="tpu_custom_call" | custom-call | flops 600000000 | bytes 1333248 | tf_op jit(solution)/shard_map/tables/pallas_call | solution.py:401
  16.9 5.7 %all-to-all-done.refs_3_ = f32[16,24,128]{2,1,0:T(8,128)S(1)} async-done(((f32[16,24,128]{2,1,0:T(8,128)}), f32[16,24,128]{2,1,0:T(8,128)S(1)}, u32[]{:S(2)}, u32[]{:S(2)}) %all-to-all-start) | async-done | bytes 196640 | tf_op jit(solution)/shard_map/all_to_all | solution.py:418
  22.6 0.9 %translate.1 = f32[16,24,128]{2,1,0:T(8,128)S(1)} custom-call(bf16[768,128]{1,0:T(8,128)(2,1)S(1)} %get-tuple-element.19.refs_0_, bf16[768,48]{1,0:T(8,128)(2,1)S(1)} %get-tuple-element.20.refs_1_, bf16[48,768]{1,0:T(8,128)(2,1)S(1)} %get-tuple-element.21.refs_2_, f32[16,24,128]{2,1,0:T(8,128)S(1)} %all-to-all-done.refs_3_), custom_call_target="tpu_custom_call" | custom-call | flops 600000000 | bytes 1081344 | tf_op jit(solution)/shard_map/translate/pallas_call | solution.py:401
  23.5 11.3 %all_to_all.10.refs_0_ = f32[16,24,128]{2,1,0:T(8,128)S(1)} all-to-all(f32[16,24,128]{2,1,0:T(8,128)S(1)} %translate.1), channel_id=1, replica_groups=mesh['clus'=16,'samp'=2] {'clus'}, dimensions={0} | all-to-all | bytes 393216 | tf_op jit(solution)/shard_map/all_to_all | solution.py:418
  34.8 0.0 collective-permute-start.2
  34.8 1.1 %lower.1 = (f32[384,128]{1,0:T(8,128)}, f32[192,512]{1,0:T(8,128)S(1)}) custom-call(f32[16,24,128]{2,1,0:T(8,128)S(1)} %all_to_all.10.refs_0_, f32[48,1024]{1,0:T(8,128)S(1)} %get-tuple-element.15.refs_2_.refs_1_, f32[48,1024]{1,0:T(8,128)S(1)} %get-tuple-element.16.refs_3_.refs_2_, bf16[4,512,256]{2,1,0:T(8,128)(2,1)S(1)} %get-tuple-element.17.refs_4_.refs_3_, ...), custom_call_target="tpu_custom_call" | custom-call | flops 1500000000 | bytes 3295232 | tf_op jit(solution)/shard_map/lower/pallas_call | solution.py:401
  35.9 0.3 collective-permute-done.2.refs_0_
  36.2 1.9 %finish.1 = f32[768,128]{1,0:T(8,128)} custom-call(f32[16,24,128]{2,1,0:T(8,128)S(1)} %collective-permute-done.2.refs_0_, f32[48,1024]{1,0:T(8,128)S(1)} %get-tuple-element.23.refs_1_, f32[48,1024]{1,0:T(8,128)S(1)} %get-tuple-element.24.refs_2_, bf16[4,512,256]{2,1,0:T(8,128)(2,1)S(1)} %get-tuple-element.17.refs_4_.refs_3_, ...), custom_call_target="tpu_custom_call" | custom-call | flops 1500000000 | bytes 3491840 | tf_op jit(solution)/shard_map/finish/pallas_call | solution.py:401
Async XLA Ops:
  0.6 2.3 %collective-permute-start.1 = (f32[768,128]{1,0:T(8,128)}, f32[768,128]{1,0:T(8,128)S(1)}, u32[]{:S(2)}, u32[]{:S(2)}) collective-permute-start(f32[768,128]{1,0:T(8,128)} %bitcast.25), channel_id=1, source_target_pairs={{0,1},{1,0},{2,3},{3,2},{4,5},{5,4},{6,7},{7,6},{8,9},{9,8},{10,11... | collective-permute-start | bytes 1179656 | tf_op jit(solution)/shard_map/ppermute | solution.py:436
  5.3 8.2 %copy-start = (f32[8,6,1024]{2,0,1:T(8,128)S(1)}, f32[8,6,1024]{2,0,1:T(8,128)}, u32[]{:S(2)}) copy-start(f32[8,6,1024]{2,0,1:T(8,128)} %param.12) | copy-start | bytes 589828
  5.3 17.3 %all-to-all-start = ((f32[16,24,128]{2,1,0:T(8,128)}), f32[16,24,128]{2,1,0:T(8,128)S(1)}, u32[]{:S(2)}, u32[]{:S(2)}) async-start(f32[16,24,128]{2,1,0:T(8,128)} %aggregate.1.refs_4_), calls=%async_computation | async-start | bytes 393216 | tf_op jit(solution)/shard_map/all_to_all | solution.py:418
  13.5 1.5 %collective-permute-start = (f32[48,1024]{1,0:T(8,128)S(1)}, f32[48,1024]{1,0:T(8,128)S(1)}, u32[]{:S(2)}, u32[]{:S(2)}) collective-permute-start(f32[48,1024]{1,0:T(8,128)S(1)} %bitcast.28), channel_id=1, source_target_pairs={{1,0},{0,1},{3,2},{2,3},{5,4},{4,5},{7,6},{6,7},{9,8},{8,9},{11,10... | collective-permute-start | bytes 589832 | tf_op jit(solution)/shard_map/ppermute | solution.py:441
  34.8 1.4 %collective-permute-start.2 = (f32[16,24,128]{2,1,0:T(8,128)S(1)}, f32[16,24,128]{2,1,0:T(8,128)S(1)}, u32[]{:S(2)}, u32[]{:S(2)}) collective-permute-start(f32[16,24,128]{2,1,0:T(8,128)S(1)} %all_to_all.10.refs_0_), channel_id=1, source_target_pairs={{1,0},{0,1},{3,2},{2,3},{5,4},{4,5},{7,6},{6,7},{9,8},{8,9},{11,10... | collective-permute-start | bytes 589832 | tf_op jit(solution)/shard_map/ppermute | solution.py:501

commit v9 on v8

--- a/solution.py
+++ b/solution.py
@@ -7,6 +7,7 @@
 
 P_SIZE = 6
 OCTANTS = 8
+SUBLANES = 8
 TILE = 128
 PAIR = 2 * TILE
 HALF = TILE // 2
@@ -83,8 +84,9 @@
     blocks = wide_ref.shape[0]
 
     wide = sources * own
-    at_row = one_hot(iota((rows * wide, rows), 0) // wide == iota((rows * wide, rows), 1))
-    keep = iota((rows * wide, wide), 0) % wide == iota((rows * wide, wide), 1)
+    tall = rows * wide * SUBLANES
+    at_row = one_hot(iota((tall, rows), 0) // (wide * SUBLANES) == iota((tall, rows), 1))
+    keep = iota((tall, wide), 0) // SUBLANES % wide == iota((tall, wide), 1)
     ones = jnp.ones((wide, TILE), BF16)
     copies[0].wait()
     parts = [
@@ -94,7 +96,7 @@
     polar_ref[...] = parts[0] + (parts[1] + parts[2])
 
     copies[1].wait()
-    cos_ref[...], sin_ref[...] = turns(phase_ref[...])
+    keep_turns(phase_ref[...], cos_ref, sin_ref)
 
     copies[2].wait()
     copies[3].wait()
@@ -122,7 +124,19 @@
 
 
 def polar_splat(polar_ref, row, width):
-    return jnp.concatenate([polar_ref[row : row + 1, :]] * (width // TILE), axis=1)
+    return jnp.concatenate([polar_ref[row * SUBLANES : (row + 1) * SUBLANES, :]] * (width // TILE), axis=1)
+
+
+def turn_splat(turn_ref, row, block, size):
+    return jnp.concatenate([turn_ref[2 * block + half, pl.ds(row, size, stride=0), :] for half in range(2)], axis=1)
+
+
+def keep_turns(phase, cos_ref, sin_ref):
+    count = phase.shape[0]
+    for value, target in zip(turns(phase), (cos_ref, sin_ref)):
+        for tile in range(target.shape[0]):
+            target[tile, :count, :] = value[:, tile * TILE : (tile + 1) * TILE]
+            target[tile, count:, :] = jnp.zeros((target.shape[1] - count, TILE), F32)
 
 
 def aggregate_kernel(groups, sources, own, devices, *refs):
@@ -130,8 +144,8 @@
     cos_ref, sin_ref, wide_ref, polar_ref = refs[sources : sources + 4]
     out, high_s, low_s = refs[-3:]
     blocks = wide_ref.shape[0]
-    rows = cos_ref.shape[0] // OCTANTS
-    columns = cos_ref.shape[1] // devices
+    rows = cos_ref.shape[1] // OCTANTS - 1
+    columns = cos_ref.shape[0] * TILE // devices
     size = 2 * groups
     wide = sources * own
     row_stride = 2 * blocks
@@ -179,16 +193,15 @@
         left = jnp.concatenate(one + two + one, axis=1)
         right = jnp.concatenate([wide_ref[block, :PAIR], wide_ref[block, :PAIR], wide_ref[block, PAIR:]], axis=0)
         spread = product(left, right)
-        part = slice(block * PAIR, (block + 1) * PAIR)
         summed = []
         for row in range(rows):
             direct = jnp.zeros((size, PAIR), F32)
             crossed = jnp.zeros((size, PAIR), F32)
             for octant in range(OCTANTS):
                 start = (octant * rows + row) * size
-                turn = slice(row * OCTANTS + octant, row * OCTANTS + octant + 1)
-                direct += spread[start : start + size] * cos_ref[turn, part]
-                crossed += spread[start : start + size] * sin_ref[turn, part]
+                turn = row * OCTANTS + octant
+                direct += spread[start : start + size] * turn_splat(cos_ref, turn, block, size)
+                crossed += spread[start : start + size] * turn_splat(sin_ref, turn, block, size)
             summed.append(direct + jnp.concatenate([-crossed[groups:], crossed[:groups]], axis=0))
         for first in range(0, rows, 2):
             target = slice(first // 2 * size, (first // 2 + 1) * size)
@@ -233,7 +246,7 @@
     hot_ref, chosen_ref, table_out, *turned_refs = outs
     copies = started(remote, local, sems)
     for place, phase in enumerate(phases):
-        turned_refs[2 * place][...], turned_refs[2 * place + 1][...] = turns(phase[...])
+        keep_turns(phase[...], turned_refs[2 * place], turned_refs[2 * place + 1])
 
     copies[2].wait()
     raw = table_ref[...]
@@ -311,8 +324,11 @@
         lowered = []
         for octant in range(OCTANTS):
             for row in range(rows):
-                turn = slice(row * OCTANTS + octant, row * OCTANTS + octant + 1)
-                lowered.append(fields[row][:, part] * cos_ref[turn, part] + crossed[row][:, part] * sin_ref[turn, part])
+                turn = row * OCTANTS + octant
+                lowered.append(
+                    fields[row][:, part] * turn_splat(cos_ref, turn, block, size)
+                    + crossed[row][:, part] * turn_splat(sin_ref, turn, block, size)
+                )
         high, low = split_two(jnp.concatenate(lowered, axis=0))
         left = jnp.concatenate([high, low, high], axis=1)
         right = jnp.concatenate([wide_ref[block, :PAIR], wide_ref[block, :PAIR], wide_ref[block, PAIR:]], axis=1)
@@ -340,11 +356,11 @@
 
 def lower_kernel(groups, own, arrived_ref, cos_ref, sin_ref, wide_ref, polar_ref, parent_out, partial_ref, parent_ref, sem):
     devices = arrived_ref.shape[0]
-    azimuth = cos_ref.shape[1]
+    azimuth = cos_ref.shape[0] * TILE
     size = 2 * groups
     fields = unpacked_fields(arrived_ref, size, azimuth // devices)
     rows = len(fields)
-    wide = polar_ref.shape[0] // rows
+    wide = polar_ref.shape[0] // (rows * SUBLANES)
     tiles = azimuth // TILE
     for row, field in enumerate(fields):
         for tile in range(tiles):
@@ -368,7 +384,7 @@
     turned_refs = refs[sources - 1 : 3 * (sources - 1)]
     wide_ref, polar_ref, partial_ref, out = refs[3 * (sources - 1) :]
     blocks = wide_ref.shape[0]
-    azimuth = turned_refs[0].shape[1]
+    azimuth = turned_refs[0].shape[0] * TILE
     size = 2 * groups
     coarse = []
     for place, field in enumerate(arrived):
@@ -440,7 +456,7 @@
     ways = [backward] if sources == 2 else [backward, forward]
     phases = [lax.ppermute(phase, "samp", way) for way in ways]
     table = translation_table.transpose(0, 2, 1, 3).reshape(vectors * rows * 2, width // 2)
-    turn = struct((rows * OCTANTS, azimuth), F32)
+    turn = struct((azimuth // TILE, rows * OCTANTS + OCTANTS, TILE), F32)
 
     cosine, sine, wide, polar, held = call(
         bind(prepare_kernel, sources, own),
@@ -448,7 +464,7 @@
             turn,
             turn,
             struct((blocks, 2 * PAIR, PAIR), BF16),
-            struct((rows * sources * own, TILE), F32),
+            struct((rows * sources * own * SUBLANES, TILE), F32),
             struct(field.shape, F32),
         ],
         [],

time: 38.4 us -> 38.6 us (level)
  no operation moved by 1% of the time
where the time goes in v9:
time: 38.6 us; the launch traced here: 38.3 us
  blocking collectives  11.4 us (30%)
  Pallas kernels  10.1 us (26%)
  starting transfers between devices  8.81 us (23%)
  waiting for transfers between devices  7.37 us (19%)
  between operations  0.69 us (2%)
    all_to_all x1, blocking collectives, exchange(): lax.all_to_all(blocks, 'clus', split_axis=0, concat_axis=0, tiled=True)  11.4 us
    pallas_call x6, Pallas kernels, call(): pl.pallas_call(kernel, out_shape=outs, in_specs=[away] * len(remote) + [n...  10.1 us
    all_to_all x1, starting transfers between devices, exchange(): lax.all_to_all(blocks, 'clus', split_axis=0, concat_axis=0, tiled=True)  8.01 us
    all_to_all x1, waiting for transfers between devices, exchange(): lax.all_to_all(blocks, 'clus', split_axis=0, concat_axis=0, tiled=True)  5.84 us
    ppermute x1, waiting for transfers between devices, per_device(): phases = [lax.ppermute(phase, 'samp', way) for way in ways]  1.23 us
  transfers between devices with their start and end apart: 4, of which 3 were waited for; matrix products, arithmetic and copies ran while one was open for 0% of the time, Pallas kernels for 13%

profile of v9, /device:TPU:0, one launch (start us, length us, event | category | flops | bytes accessed | tf_op | source)
XLA Modules:
  0.0 38.3 jit_solution(18071894263347858935)
XLA Ops:
  0.6 0.5 %collective-permute-start.1 = (f32[768,128]{1,0:T(8,128)}, f32[768,128]{1,0:T(8,128)S(1)}, u32[]{:S(2)}, u32[]{:S(2)}) collective-permute-start(f32[768,128]{1,0:T(8,128)} %bitcast.25), channel_id=1, source_target_pairs={{0,1},{1,0},{2,3},{3,2},{4,5},{5,4},{6,7},{7,6},{8,9},{9,8},{10,11... | collective-permute-start | bytes 1179656 | tf_op jit(solution)/shard_map/ppermute | solution.py:452
  1.1 1.9 %prepare.1 = (f32[8,56,128]{2,1,0:T(8,128)S(1)}, f32[8,56,128]{2,1,0:T(8,128)S(1)}, bf16[4,512,256]{2,1,0:T(8,128)(2,1)S(1)}, f32[288,128]{1,0:T(8,128)S(1)}, f32[768,128]{1,0:T(8,128)S(1)}) custom-call(f32[6,9]{1,0:T(8,128)} %refs_0_.1, f32[48,1024]{1,0:T(8,128)} %bitcast.27, s32[6,1024]{1,0:T(8,128)} %bitcast.30, f32[6,1024]{1,0:T(8,128)} %bitcast.31, ...), custom_call_target="tpu_custom_call" | custom-call | flops 400000000 | bytes 3735768 | tf_op jit(solution)/shard_map/prepare/pallas_call | solution.py:417
  3.1 0.0 collective-permute-done.1.refs_1_
  3.1 2.3 %aggregate.1.refs_4_ = f32[16,24,128]{2,1,0:T(8,128)} custom-call(f32[768,128]{1,0:T(8,128)S(1)} %get-tuple-element.14.refs_0_, f32[768,128]{1,0:T(8,128)S(1)} %collective-permute-done.1.refs_1_, f32[8,56,128]{2,1,0:T(8,128)S(1)} %get-tuple-element.15.refs_2_.refs_1_, f32[8,56,128]{2,1,0:T(8,128)S(1)} %get-tuple-element.16.refs_3_.refs_2_, ...), custom_call_target="tpu_custom_call" | custom-call | flops 1500000000 | bytes 3686400 | tf_op jit(solution)/shard_map/aggregate/pallas_call | solution.py:417
  5.4 0.0 copy-start
  5.4 8.0 %all-to-all-start = ((f32[16,24,128]{2,1,0:T(8,128)}), f32[16,24,128]{2,1,0:T(8,128)S(1)}, u32[]{:S(2)}, u32[]{:S(2)}) async-start(f32[16,24,128]{2,1,0:T(8,128)} %aggregate.1.refs_4_), calls=%async_computation | async-start | bytes 393216 | tf_op jit(solution)/shard_map/all_to_all | solution.py:434
  13.4 0.0 copy-done
  13.4 0.3 collective-permute-start
  13.7 1.2 %collective-permute-done.refs_3_ = f32[48,1024]{1,0:T(8,128)S(1)} collective-permute-done((f32[48,1024]{1,0:T(8,128)S(1)}, f32[48,1024]{1,0:T(8,128)S(1)}, u32[]{:S(2)}, u32[]{:S(2)}) %collective-permute-start) | collective-permute-done | bytes 196640 | tf_op jit(solution)/shard_map/ppermute | solution.py:457
  14.9 1.9 %tables.1 = (bf16[768,128]{1,0:T(8,128)(2,1)S(1)}, bf16[768,48]{1,0:T(8,128)(2,1)S(1)}, bf16[48,768]{1,0:T(8,128)(2,1)S(1)}, f32[8,56,128]{2,1,0:T(8,128)S(1)}, f32[8,56,128]{2,1,0:T(8,128)S(1)}) custom-call(s32[12,64]{1,0:T(8,128)} %bitcast.32, s32[12,64]{1,0:T(8,128)} %bitcast.33, f32[192,64]{1,0:T(8,128)} %bitcast.29, ...), custom_call_target="tpu_custom_call" | custom-call | flops 600000000 | bytes 1398784 | tf_op jit(solution)/shard_map/tables/pallas_call | solution.py:417
  16.9 5.8 %all-to-all-done.refs_3_ = f32[16,24,128]{2,1,0:T(8,128)S(1)} async-done(((f32[16,24,128]{2,1,0:T(8,128)}), f32[16,24,128]{2,1,0:T(8,128)S(1)}, u32[]{:S(2)}, u32[]{:S(2)}) %all-to-all-start) | async-done | bytes 196640 | tf_op jit(solution)/shard_map/all_to_all | solution.py:434
  22.7 0.9 %translate.1 = f32[16,24,128]{2,1,0:T(8,128)S(1)} custom-call(bf16[768,128]{1,0:T(8,128)(2,1)S(1)} %get-tuple-element.19.refs_0_, bf16[768,48]{1,0:T(8,128)(2,1)S(1)} %get-tuple-element.20.refs_1_, bf16[48,768]{1,0:T(8,128)(2,1)S(1)} %get-tuple-element.21.refs_2_, f32[16,24,128]{2,1,0:T(8,128)S(1)} %all-to-all-done.refs_3_), custom_call_target="tpu_custom_call" | custom-call | flops 600000000 | bytes 1081344 | tf_op jit(solution)/shard_map/translate/pallas_call | solution.py:417
  23.6 11.4 %all_to_all.10.refs_0_ = f32[16,24,128]{2,1,0:T(8,128)S(1)} all-to-all(f32[16,24,128]{2,1,0:T(8,128)S(1)} %translate.1), channel_id=1, replica_groups=mesh['clus'=16,'samp'=2] {'clus'}, dimensions={0} | all-to-all | bytes 393216 | tf_op jit(solution)/shard_map/all_to_all | solution.py:434
  35.0 0.0 collective-permute-start.2
  35.0 1.1 %lower.1 = (f32[384,128]{1,0:T(8,128)}, f32[192,512]{1,0:T(8,128)S(1)}) custom-call(f32[16,24,128]{2,1,0:T(8,128)S(1)} %all_to_all.10.refs_0_, f32[8,56,128]{2,1,0:T(8,128)S(1)} %get-tuple-element.15.refs_2_.refs_1_, f32[8,56,128]{2,1,0:T(8,128)S(1)} %get-tuple-element.16.refs_3_.refs_2_, bf16[4,512,256]{2,1,0:T(8,128)(2,1)S(1)} %get-tuple-element.17.refs_4_.refs_3_, ...), custom_call_target="tpu_custom_call" | custom-call | flops 1500000000 | bytes 3489792 | tf_op jit(solution)/shard_map/lower/pallas_call | solution.py:417
  36.1 0.3 collective-permute-done.2.refs_0_
  36.4 1.9 %finish.1 = f32[768,128]{1,0:T(8,128)} custom-call(f32[16,24,128]{2,1,0:T(8,128)S(1)} %collective-permute-done.2.refs_0_, f32[8,56,128]{2,1,0:T(8,128)S(1)} %get-tuple-element.23.refs_1_, f32[8,56,128]{2,1,0:T(8,128)S(1)} %get-tuple-element.24.refs_2_, bf16[4,512,256]{2,1,0:T(8,128)(2,1)S(1)} %get-tuple-element.17.refs_4_.refs_3_, ...), custom_call_target="tpu_custom_call" | custom-call | flops 1500000000 | bytes 3686400 | tf_op jit(solution)/shard_map/finish/pallas_call | solution.py:417
Async XLA Ops:
  0.6 2.5 %collective-permute-start.1 = (f32[768,128]{1,0:T(8,128)}, f32[768,128]{1,0:T(8,128)S(1)}, u32[]{:S(2)}, u32[]{:S(2)}) collective-permute-start(f32[768,128]{1,0:T(8,128)} %bitcast.25), channel_id=1, source_target_pairs={{0,1},{1,0},{2,3},{3,2},{4,5},{5,4},{6,7},{7,6},{8,9},{9,8},{10,11... | collective-permute-start | bytes 1179656 | tf_op jit(solution)/shard_map/ppermute | solution.py:452
  5.4 8.0 %copy-start = (f32[8,6,1024]{2,0,1:T(8,128)S(1)}, f32[8,6,1024]{2,0,1:T(8,128)}, u32[]{:S(2)}) copy-start(f32[8,6,1024]{2,0,1:T(8,128)} %param.12) | copy-start | bytes 589828
  5.4 17.3 %all-to-all-start = ((f32[16,24,128]{2,1,0:T(8,128)}), f32[16,24,128]{2,1,0:T(8,128)S(1)}, u32[]{:S(2)}, u32[]{:S(2)}) async-start(f32[16,24,128]{2,1,0:T(8,128)} %aggregate.1.refs_4_), calls=%async_computation | async-start | bytes 393216 | tf_op jit(solution)/shard_map/all_to_all | solution.py:434
  13.4 1.5 %collective-permute-start = (f32[48,1024]{1,0:T(8,128)S(1)}, f32[48,1024]{1,0:T(8,128)S(1)}, u32[]{:S(2)}, u32[]{:S(2)}) collective-permute-start(f32[48,1024]{1,0:T(8,128)S(1)} %bitcast.28), channel_id=1, source_target_pairs={{1,0},{0,1},{3,2},{2,3},{5,4},{4,5},{7,6},{6,7},{9,8},{8,9},{11,10... | collective-permute-start | bytes 589832 | tf_op jit(solution)/shard_map/ppermute | solution.py:457
  35.0 1.4 %collective-permute-start.2 = (f32[16,24,128]{2,1,0:T(8,128)S(1)}, f32[16,24,128]{2,1,0:T(8,128)S(1)}, u32[]{:S(2)}, u32[]{:S(2)}) collective-permute-start(f32[16,24,128]{2,1,0:T(8,128)S(1)} %all_to_all.10.refs_0_), channel_id=1, source_target_pairs={{1,0},{0,1},{3,2},{2,3},{5,4},{4,5},{7,6},{6,7},{9,8},{8,9},{11,10... | collective-permute-start | bytes 589832 | tf_op jit(solution)/shard_map/ppermute | solution.py:517

commit v10 on v8

--- a/solution.py
+++ b/solution.py
@@ -300,26 +300,33 @@
     return fields
 
 
-def coarse_columns(fields, cos_ref, sin_ref, wide_ref):
+def coarse_columns(fields, cos_ref, sin_ref, wide_ref, polar_ref, first, own):
     blocks = wide_ref.shape[0]
     rows, size = len(fields), fields[0].shape[0]
     groups = size // 2
+    wide = polar_ref.shape[0] // rows
     crossed = [jnp.concatenate([field[groups:], -field[:groups]], axis=0) for field in fields]
     mains, rims = [], []
     for block in range(blocks):
         part = slice(block * PAIR, (block + 1) * PAIR)
-        lowered = []
+        kept = []
         for octant in range(OCTANTS):
+            lowered = []
             for row in range(rows):
                 turn = slice(row * OCTANTS + octant, row * OCTANTS + octant + 1)
                 lowered.append(fields[row][:, part] * cos_ref[turn, part] + crossed[row][:, part] * sin_ref[turn, part])
-        high, low = split_two(jnp.concatenate(lowered, axis=0))
+            for place in range(first, first + own):
+                total = lowered[0] * polar_splat(polar_ref, place, PAIR)
+                for row in range(1, rows):
+                    total += lowered[row] * polar_splat(polar_ref, row * wide + place, PAIR)
+                kept.append(total)
+        high, low = split_two(jnp.concatenate(kept, axis=0))
         left = jnp.concatenate([high, low, high], axis=1)
         right = jnp.concatenate([wide_ref[block, :PAIR], wide_ref[block, :PAIR], wide_ref[block, PAIR:]], axis=1)
         both = product(left, right, 1, 1)
         mains.append(both[:, :TILE])
         rims.append(both[:, TILE:])
-    lane = iota((OCTANTS * rows * size, TILE), 1)
+    lane = iota((OCTANTS * own * size, TILE), 1)
     return jnp.concatenate(
         [
             mains[block] + jnp.where(lane < HALF, rims[(block - 1) % blocks], rims[(block + 1) % blocks])
@@ -329,22 +336,12 @@
     )
 
 
-def anterpolated(coarse, polar_ref, octant, place, rows, size, wide):
-    total = None
-    for row in range(rows):
-        start = (octant * rows + row) * size
-        term = coarse[start : start + size] * polar_splat(polar_ref, row * wide + place, coarse.shape[1])
-        total = term if total is None else total + term
-    return total
-
-
 def lower_kernel(groups, own, arrived_ref, cos_ref, sin_ref, wide_ref, polar_ref, parent_out, partial_ref, parent_ref, sem):
     devices = arrived_ref.shape[0]
     azimuth = cos_ref.shape[1]
     size = 2 * groups
     fields = unpacked_fields(arrived_ref, size, azimuth // devices)
     rows = len(fields)
-    wide = polar_ref.shape[0] // rows
     tiles = azimuth // TILE
     for row, field in enumerate(fields):
         for tile in range(tiles):
@@ -355,11 +352,7 @@
                 ]
     copy = pltpu.make_async_copy(parent_ref, parent_out, sem)
     copy.start()
-    coarse = coarse_columns(fields, cos_ref, sin_ref, wide_ref)
-    for octant in range(OCTANTS):
-        for row in range(own):
-            start = (octant * own + row) * size
-            partial_ref[start : start + size, :] = anterpolated(coarse, polar_ref, octant, row, rows, size, wide)
+    partial_ref[...] = coarse_columns(fields, cos_ref, sin_ref, wide_ref, polar_ref, 0, own)
     copy.wait()
 
 
@@ -370,19 +363,15 @@
     blocks = wide_ref.shape[0]
     azimuth = turned_refs[0].shape[1]
     size = 2 * groups
-    coarse = []
+    total = partial_ref[...]
     for place, field in enumerate(arrived):
         fields = unpacked_fields(field, size, azimuth // field.shape[0])
-        coarse.append(coarse_columns(fields, turned_refs[2 * place], turned_refs[2 * place + 1], wide_ref))
-    rows = len(fields)
-    wide = sources * own
+        turn_refs = turned_refs[2 * place : 2 * place + 2]
+        total += coarse_columns(fields, *turn_refs, wide_ref, polar_ref, (place + 1) * own, own)
     row_stride = 2 * blocks
     for octant in range(OCTANTS):
         for row in range(own):
-            start = (octant * own + row) * size
-            value = partial_ref[start : start + size, :]
-            for place in range(sources - 1):
-                value += anterpolated(coarse[place], polar_ref, octant, (place + 1) * own + row, rows, size, wide)
+            value = total[(octant * own + row) * size : (octant * own + row + 1) * size]
             for block in range(blocks):
                 for part in range(2):
                     first = (octant * own + row) * row_stride + 2 * block + part

time: 38.4 us -> 38.6 us (level)
  Pallas kernels: 9.97 us -> 10.4 us
    pallas_call x6, Pallas kernels: 9.97 us -> 10.4 us  [call(): pl.pallas_call(kernel, out_shape=outs, in_specs=[away] * len(remote) + [n...]
  transfers between devices with their start and end apart: 4 -> 4, of which waited for: 3 -> 2; matrix products, arithmetic and copies ran while one was open for 0% -> 0% of each run, Pallas kernels for 13% -> 14%
where the time goes in v10:
time: 38.6 us; the launch traced here: 38.3 us
  blocking collectives  11.3 us (29%)
  Pallas kernels  10.4 us (27%)
  starting transfers between devices  8.82 us (23%)
  waiting for transfers between devices  7.07 us (18%)
  between operations  0.7 us (2%)
    all_to_all x1, blocking collectives, exchange(): lax.all_to_all(blocks, 'clus', split_axis=0, concat_axis=0, tiled=True)  11.3 us
    pallas_call x6, Pallas kernels, call(): pl.pallas_call(kernel, out_shape=outs, in_specs=[away] * len(remote) + [n...  10.4 us
    all_to_all x1, starting transfers between devices, exchange(): lax.all_to_all(blocks, 'clus', split_axis=0, concat_axis=0, tiled=True)  8.15 us
    all_to_all x1, waiting for transfers between devices, exchange(): lax.all_to_all(blocks, 'clus', split_axis=0, concat_axis=0, tiled=True)  5.7 us
    ppermute x1, waiting for transfers between devices, per_device(): phases = [lax.ppermute(phase, 'samp', way) for way in ways]  1.36 us
  transfers between devices with their start and end apart: 4, of which 2 were waited for; matrix products, arithmetic and copies ran while one was open for 0% of the time, Pallas kernels for 14%

profile of v10, /device:TPU:0, one launch (start us, length us, event | category | flops | bytes accessed | tf_op | source)
XLA Modules:
  0.0 38.3 jit_solution(11129051481001929516)
XLA Ops:
  0.6 0.5 %collective-permute-start.1 = (f32[768,128]{1,0:T(8,128)}, f32[768,128]{1,0:T(8,128)S(1)}, u32[]{:S(2)}, u32[]{:S(2)}) collective-permute-start(f32[768,128]{1,0:T(8,128)} %bitcast.25), channel_id=1, source_target_pairs={{0,1},{1,0},{2,3},{3,2},{4,5},{5,4},{6,7},{7,6},{8,9},{9,8},{10,11... | collective-permute-start | bytes 1179656 | tf_op jit(solution)/shard_map/ppermute | solution.py:425
  1.1 1.8 %prepare.1 = (f32[48,1024]{1,0:T(8,128)S(1)}, f32[48,1024]{1,0:T(8,128)S(1)}, bf16[4,512,256]{2,1,0:T(8,128)(2,1)S(1)}, f32[36,128]{1,0:T(8,128)S(1)}, f32[768,128]{1,0:T(8,128)S(1)}) custom-call(f32[6,9]{1,0:T(8,128)} %refs_0_.1, f32[48,1024]{1,0:T(8,128)} %bitcast.27, s32[6,1024]{1,0:T(8,128)} %bitcast.30, f32[6,1024]{1,0:T(8,128)} %bitcast.31, ...), custom_call_target="tpu_custom_call" | custom-call | flops 400000000 | bytes 3541208 | tf_op jit(solution)/shard_map/prepare/pallas_call | solution.py:390
  2.9 0.0 collective-permute-done.1.refs_1_
  3.0 2.3 %aggregate.1.refs_4_ = f32[16,24,128]{2,1,0:T(8,128)} custom-call(f32[768,128]{1,0:T(8,128)S(1)} %get-tuple-element.14.refs_0_, f32[768,128]{1,0:T(8,128)S(1)} %collective-permute-done.1.refs_1_, f32[48,1024]{1,0:T(8,128)S(1)} %get-tuple-element.15.refs_2_.refs_1_, f32[48,1024]{1,0:T(8,128)S(1)} %get-tuple-element.16.refs_3_.refs_2_, ...), custom_call_target="tpu_custom_call" | custom-call | flops 1500000000 | bytes 3491840 | tf_op jit(solution)/shard_map/aggregate/pallas_call | solution.py:390
  5.3 0.0 copy-start
  5.3 8.1 %all-to-all-start = ((f32[16,24,128]{2,1,0:T(8,128)}), f32[16,24,128]{2,1,0:T(8,128)S(1)}, u32[]{:S(2)}, u32[]{:S(2)}) async-start(f32[16,24,128]{2,1,0:T(8,128)} %aggregate.1.refs_4_), calls=%async_computation | async-start | bytes 393216 | tf_op jit(solution)/shard_map/all_to_all | solution.py:407
  13.4 0.0 copy-done
  13.5 0.1 collective-permute-start
  13.6 1.4 %collective-permute-done.refs_3_ = f32[48,1024]{1,0:T(8,128)S(1)} collective-permute-done((f32[48,1024]{1,0:T(8,128)S(1)}, f32[48,1024]{1,0:T(8,128)S(1)}, u32[]{:S(2)}, u32[]{:S(2)}) %collective-permute-start) | collective-permute-done | bytes 196640 | tf_op jit(solution)/shard_map/ppermute | solution.py:430
  15.0 1.9 %tables.1 = (bf16[768,128]{1,0:T(8,128)(2,1)S(1)}, bf16[768,48]{1,0:T(8,128)(2,1)S(1)}, bf16[48,768]{1,0:T(8,128)(2,1)S(1)}, f32[48,1024]{1,0:T(8,128)S(1)}, f32[48,1024]{1,0:T(8,128)S(1)}) custom-call(s32[12,64]{1,0:T(8,128)} %bitcast.32, s32[12,64]{1,0:T(8,128)} %bitcast.33, f32[192,64]{1,0:T(8,128)} %bitcast.29, ...), custom_call_target="tpu_custom_call" | custom-call | flops 600000000 | bytes 1333248 | tf_op jit(solution)/shard_map/tables/pallas_call | solution.py:390
  16.9 5.7 %all-to-all-done.refs_3_ = f32[16,24,128]{2,1,0:T(8,128)S(1)} async-done(((f32[16,24,128]{2,1,0:T(8,128)}), f32[16,24,128]{2,1,0:T(8,128)S(1)}, u32[]{:S(2)}, u32[]{:S(2)}) %all-to-all-start) | async-done | bytes 196640 | tf_op jit(solution)/shard_map/all_to_all | solution.py:407
  22.6 0.9 %translate.1 = f32[16,24,128]{2,1,0:T(8,128)S(1)} custom-call(bf16[768,128]{1,0:T(8,128)(2,1)S(1)} %get-tuple-element.19.refs_0_, bf16[768,48]{1,0:T(8,128)(2,1)S(1)} %get-tuple-element.20.refs_1_, bf16[48,768]{1,0:T(8,128)(2,1)S(1)} %get-tuple-element.21.refs_2_, f32[16,24,128]{2,1,0:T(8,128)S(1)} %all-to-all-done.refs_3_), custom_call_target="tpu_custom_call" | custom-call | flops 600000000 | bytes 1081344 | tf_op jit(solution)/shard_map/translate/pallas_call | solution.py:390
  23.5 11.3 %all_to_all.10.refs_0_ = f32[16,24,128]{2,1,0:T(8,128)S(1)} all-to-all(f32[16,24,128]{2,1,0:T(8,128)S(1)} %translate.1), channel_id=1, replica_groups=mesh['clus'=16,'samp'=2] {'clus'}, dimensions={0} | all-to-all | bytes 393216 | tf_op jit(solution)/shard_map/all_to_all | solution.py:407
  34.8 0.0 collective-permute-start.2
  34.8 1.6 %lower.1 = (f32[384,128]{1,0:T(8,128)}, f32[192,512]{1,0:T(8,128)S(1)}) custom-call(f32[16,24,128]{2,1,0:T(8,128)S(1)} %all_to_all.10.refs_0_, f32[48,1024]{1,0:T(8,128)S(1)} %get-tuple-element.15.refs_2_.refs_1_, f32[48,1024]{1,0:T(8,128)S(1)} %get-tuple-element.16.refs_3_.refs_2_, bf16[4,512,256]{2,1,0:T(8,128)(2,1)S(1)} %get-tuple-element.17.refs_4_.refs_3_, ...), custom_call_target="tpu_custom_call" | custom-call | flops 1500000000 | bytes 3295232 | tf_op jit(solution)/shard_map/lower/pallas_call | solution.py:390
  36.4 0.0 collective-permute-done.2.refs_0_
  36.4 1.9 %finish.1 = f32[768,128]{1,0:T(8,128)} custom-call(f32[16,24,128]{2,1,0:T(8,128)S(1)} %collective-permute-done.2.refs_0_, f32[48,1024]{1,0:T(8,128)S(1)} %get-tuple-element.23.refs_1_, f32[48,1024]{1,0:T(8,128)S(1)} %get-tuple-element.24.refs_2_, bf16[4,512,256]{2,1,0:T(8,128)(2,1)S(1)} %get-tuple-element.17.refs_4_.refs_3_, ...), custom_call_target="tpu_custom_call" | custom-call | flops 1500000000 | bytes 3491840 | tf_op jit(solution)/shard_map/finish/pallas_call | solution.py:390
Async XLA Ops:
  0.6 2.3 %collective-permute-start.1 = (f32[768,128]{1,0:T(8,128)}, f32[768,128]{1,0:T(8,128)S(1)}, u32[]{:S(2)}, u32[]{:S(2)}) collective-permute-start(f32[768,128]{1,0:T(8,128)} %bitcast.25), channel_id=1, source_target_pairs={{0,1},{1,0},{2,3},{3,2},{4,5},{5,4},{6,7},{7,6},{8,9},{9,8},{10,11... | collective-permute-start | bytes 1179656 | tf_op jit(solution)/shard_map/ppermute | solution.py:425
  5.3 8.2 %copy-start = (f32[8,6,1024]{2,0,1:T(8,128)S(1)}, f32[8,6,1024]{2,0,1:T(8,128)}, u32[]{:S(2)}) copy-start(f32[8,6,1024]{2,0,1:T(8,128)} %param.12) | copy-start | bytes 589828
  5.3 17.3 %all-to-all-start = ((f32[16,24,128]{2,1,0:T(8,128)}), f32[16,24,128]{2,1,0:T(8,128)S(1)}, u32[]{:S(2)}, u32[]{:S(2)}) async-start(f32[16,24,128]{2,1,0:T(8,128)} %aggregate.1.refs_4_), calls=%async_computation | async-start | bytes 393216 | tf_op jit(solution)/shard_map/all_to_all | solution.py:407
  13.5 1.5 %collective-permute-start = (f32[48,1024]{1,0:T(8,128)S(1)}, f32[48,1024]{1,0:T(8,128)S(1)}, u32[]{:S(2)}, u32[]{:S(2)}) collective-permute-start(f32[48,1024]{1,0:T(8,128)S(1)} %bitcast.28), channel_id=1, source_target_pairs={{1,0},{0,1},{3,2},{2,3},{5,4},{4,5},{7,6},{6,7},{9,8},{8,9},{11,10... | collective-permute-start | bytes 589832 | tf_op jit(solution)/shard_map/ppermute | solution.py:430
  34.8 1.6 %collective-permute-start.2 = (f32[16,24,128]{2,1,0:T(8,128)S(1)}, f32[16,24,128]{2,1,0:T(8,128)S(1)}, u32[]{:S(2)}, u32[]{:S(2)}) collective-permute-start(f32[16,24,128]{2,1,0:T(8,128)S(1)} %all_to_all.10.refs_0_), channel_id=1, source_target_pairs={{1,0},{0,1},{3,2},{2,3},{5,4},{4,5},{7,6},{6,7},{9,8},{8,9},{11,10... | collective-permute-start | bytes 589832 | tf_op jit(solution)/shard_map/ppermute | solution.py:490

commit v11 on v8

--- a/solution.py
+++ b/solution.py
@@ -224,7 +224,7 @@
     ]
 
 
-def tables_kernel(sources, rows, *refs):
+def tables_kernel(devices, sources, rows, *refs):
     count = 3
     remote, phases = refs[:count], refs[count : count + sources - 1]
     outs = refs[count + sources : -count - 1]
@@ -256,7 +256,9 @@
     copies[1].wait()
     partners, clusters = listed_ref.shape
     unit = one_hot(iota((clusters, clusters), 0) == iota((clusters, clusters), 1))
-    listed = sum(product(unit, half, 1, 1) for half in split_two(listed_ref[...].astype(F32)))
+    groups = clusters // devices
+    listed = place_of(listed_ref[...] // groups, devices) * groups + listed_ref[...] % groups
+    listed = sum(product(unit, half, 1, 1) for half in split_two(listed.astype(F32)))
     chosen = sum(product(unit, half, 1, 1) for half in split_two(vector_ref[...].astype(F32)))
     cluster = (iota((clusters, 2 * clusters), 1) % clusters).astype(F32)
     vector = (iota((clusters, 3 * vectors), 1) % vectors).astype(F32)
@@ -296,7 +298,9 @@
 def unpacked_fields(arrived_ref, size, columns):
     fields = []
     for start in range(0, arrived_ref.shape[1], size):
-        fields += unpacked_pieces([arrived_ref[device, start : start + size, :] for device in range(arrived_ref.shape[0])], columns)
+        devices = arrived_ref.shape[0]
+        blocks = [arrived_ref[place_of(device, devices), start : start + size, :] for device in range(devices)]
+        fields += unpacked_pieces(blocks, columns)
     return fields
 
 
@@ -414,8 +418,25 @@
     return lambda *refs: kernel(*settings, *refs)
 
 
-def exchange(blocks):
-    return lax.all_to_all(blocks, "clus", split_axis=0, concat_axis=0, tiled=True)
+def factors_of(devices):
+    near = 1
+    while near * near < devices:
+        near *= 2
+    return (devices // near, near) if devices % near == 0 else (1, devices)
+
+
+def place_of(device, devices):
+    far, near = factors_of(devices)
+    return device % near * far + device // near
+
+
+def exchange(blocks, devices):
+    far, near = factors_of(devices)
+    along_far = [[z * near + r for z in range(far)] for r in range(near)]
+    along_near = [[z * near + r for r in range(near)] for z in range(far)]
+    moved = lax.all_to_all(blocks, "clus", split_axis=0, concat_axis=0, tiled=True, axis_index_groups=along_far)
+    moved = moved.reshape(far, near, *blocks.shape[1:]).swapaxes(0, 1).reshape(blocks.shape)
+    return lax.all_to_all(moved, "clus", split_axis=0, concat_axis=0, tiled=True, axis_index_groups=along_near)
 
 
 def per_device(child_patterns, theta_weights, phi_stencil, phi_weights, shift_phase, translation_table, far_list, far_vector):
@@ -465,9 +486,9 @@
         "aggregate",
         scratch=[pltpu.VMEM((2 * groups * OCTANTS * rows, columns), BF16)] * 2,
     )
-    arrived = exchange(outgoing)
+    arrived = exchange(outgoing, devices)
     hot, chosen, factors, *turned_parts = call(
-        bind(tables_kernel, sources, rows),
+        bind(tables_kernel, devices, sources, rows),
         [
             struct((partners * clusters, 2 * clusters), BF16),
             struct((partners * clusters, 3 * vectors), BF16),
@@ -487,7 +508,7 @@
         600_000_000,
         "translate",
     )
-    returned = exchange(translated)
+    returned = exchange(translated, devices)
     size = rows_all * 2 * azimuth // TILE
     parent, partial = call(
         bind(lower_kernel, groups, own),

time: 38.4 us -> 51 us (1.33)
  blocking collectives: 11.3 us -> 17.2 us
  waiting for transfers between devices: 7.36 us -> 11.5 us
  starting transfers between devices: 8.82 us -> 10.5 us
  local copies, waits for them, and re-layouts: 0.01 us -> 0.71 us
    all_to_all x1 -> x2, blocking collectives: 11.3 us -> 17.2 us  [the longest x1 9.33 us: exchange(): lax.all_to_all(blocks, 'clus', split_axis=0, concat_axis=0, tiled=True, a...]
    all_to_all x1 -> x2, waiting for transfers between devices: 5.7 us -> 11.2 us  [the longest x1 7.91 us: exchange(): lax.all_to_all(blocks, 'clus', split_axis=0, concat_axis=0, tiled=True, a...]
    all_to_all x1 -> x2, starting transfers between devices: 8.15 us -> 9.87 us  [the longest x1 6.15 us: exchange(): lax.all_to_all(blocks, 'clus', split_axis=0, concat_axis=0, tiled=True, a...]
    ppermute x1, waiting for transfers between devices: 1.36 us -> 0.01 us  [per_device(): phases = [lax.ppermute(phase, 'samp', way) for way in ways]]
    reshape x0 -> x2, local copies, waits for them, and re-layouts: none -> 0.7 us  [exchange(): moved.reshape(far, near, *blocks.shape[1:]).swapaxes(0, 1)]
  transfers between devices with their start and end apart: 4 -> 5, of which waited for: 3 -> 3; matrix products, arithmetic and copies ran while one was open for 0% -> 1% of each run, Pallas kernels for 13% -> 10%
where the time goes in v11:
time: 51 us; the launch traced here: 50.5 us
  blocking collectives  17.2 us (34%)
  waiting for transfers between devices  11.5 us (23%)
  starting transfers between devices  10.5 us (21%)
  Pallas kernels  9.97 us (20%)
  local copies, waits for them, and re-layouts  0.71 us (1%)
  between operations  0.68 us (1%)
    pallas_call x6, Pallas kernels, call(): pl.pallas_call(kernel, out_shape=outs, in_specs=[away] * len(remote) + [n...  9.97 us
    all_to_all x1, blocking collectives, exchange(): lax.all_to_all(blocks, 'clus', split_axis=0, concat_axis=0, tiled=True, a...  9.33 us
    all_to_all x1, blocking collectives, exchange(): lax.all_to_all(moved, 'clus', split_axis=0, concat_axis=0, tiled=True, ax...  7.92 us
    all_to_all x1, waiting for transfers between devices, exchange(): lax.all_to_all(blocks, 'clus', split_axis=0, concat_axis=0, tiled=True, a...  7.91 us
    all_to_all x1, starting transfers between devices, exchange(): lax.all_to_all(blocks, 'clus', split_axis=0, concat_axis=0, tiled=True, a...  6.15 us
    all_to_all x1, starting transfers between devices, exchange(): lax.all_to_all(moved, 'clus', split_axis=0, concat_axis=0, tiled=True, ax...  3.72 us
    all_to_all x1, waiting for transfers between devices, exchange(): lax.all_to_all(moved, 'clus', split_axis=0, concat_axis=0, tiled=True, ax...  3.25 us
  transfers between devices with their start and end apart: 5, of which 3 were waited for; matrix products, arithmetic and copies ran while one was open for 1% of the time, Pallas kernels for 10%

profile of v11, /device:TPU:0, one launch (start us, length us, event | category | flops | bytes accessed | tf_op | source)
XLA Modules:
  0.0 50.5 jit_solution(11431122253813556312)
XLA Ops:
  0.6 0.5 %collective-permute-start.1 = (f32[768,128]{1,0:T(8,128)}, f32[768,128]{1,0:T(8,128)S(1)}, u32[]{:S(2)}, u32[]{:S(2)}) collective-permute-start(f32[768,128]{1,0:T(8,128)} %bitcast.36), channel_id=1, source_target_pairs={{0,1},{1,0},{2,3},{3,2},{4,5},{5,4},{6,7},{7,6},{8,9},{9,8},{10,11... | collective-permute-start | bytes 1179656 | tf_op jit(solution)/shard_map/ppermute | solution.py:457
  1.1 1.8 %prepare.1 = (f32[48,1024]{1,0:T(8,128)S(1)}, f32[48,1024]{1,0:T(8,128)S(1)}, bf16[4,512,256]{2,1,0:T(8,128)(2,1)S(1)}, f32[36,128]{1,0:T(8,128)S(1)}, f32[768,128]{1,0:T(8,128)S(1)}) custom-call(f32[6,9]{1,0:T(8,128)} %refs_0_.1, f32[48,1024]{1,0:T(8,128)} %bitcast.38, s32[6,1024]{1,0:T(8,128)} %bitcast.41, f32[6,1024]{1,0:T(8,128)} %bitcast.42, ...), custom_call_target="tpu_custom_call" | custom-call | flops 400000000 | bytes 3541208 | tf_op jit(solution)/shard_map/prepare/pallas_call | solution.py:405
  2.9 0.0 collective-permute-done.1.refs_1_
  3.0 2.3 %aggregate.1.refs_4_ = f32[16,24,128]{2,1,0:T(8,128)} custom-call(f32[768,128]{1,0:T(8,128)S(1)} %get-tuple-element.14.refs_0_, f32[768,128]{1,0:T(8,128)S(1)} %collective-permute-done.1.refs_1_, f32[48,1024]{1,0:T(8,128)S(1)} %get-tuple-element.15.refs_2_.refs_1_, f32[48,1024]{1,0:T(8,128)S(1)} %get-tuple-element.16.refs_3_.refs_2_, ...), custom_call_target="tpu_custom_call" | custom-call | flops 1500000000 | bytes 3491840 | tf_op jit(solution)/shard_map/aggregate/pallas_call | solution.py:405
  5.3 0.0 copy-start
  5.3 6.2 %all-to-all-start = ((f32[16,24,128]{2,1,0:T(8,128)}), f32[16,24,128]{2,1,0:T(8,128)S(1)}, u32[]{:S(2)}, u32[]{:S(2)}) async-start(f32[16,24,128]{2,1,0:T(8,128)} %aggregate.1.refs_4_), calls=%async_computation | async-start | bytes 393216 | tf_op jit(solution)/shard_map/all_to_all | solution.py:437
  11.4 0.0 copy-done
  11.4 0.1 collective-permute-start
  11.5 7.9 %all-to-all-done = f32[16,24,128]{2,1,0:T(8,128)S(1)} async-done(((f32[16,24,128]{2,1,0:T(8,128)}), f32[16,24,128]{2,1,0:T(8,128)S(1)}, u32[]{:S(2)}, u32[]{:S(2)}) %all-to-all-start) | async-done | bytes 196640 | tf_op jit(solution)/shard_map/all_to_all | solution.py:437
  19.4 0.7 %copy.11 = f32[4,4,24,128]{3,2,0,1:T(8,128)} copy(f32[4,4,24,128]{3,2,1,0:T(8,128)S(1)} %bitcast.33) | data formatting | bytes 393216 | tf_op jit(solution)/shard_map/reshape | solution.py:438
  20.1 3.7 %all-to-all-start.1 = ((f32[16,24,128]{2,1,0:T(8,128)}), f32[16,24,128]{2,1,0:T(8,128)S(1)}, u32[]{:S(2)}, u32[]{:S(2)}) async-start(f32[16,24,128]{2,1,0:T(8,128)} %bitcast.16), calls=%async_computation.1 | async-start | bytes 393216 | tf_op jit(solution)/shard_map/all_to_all | solution.py:439
  23.9 0.0 collective-permute-done.refs_3_
  23.9 1.9 %tables.1 = (bf16[768,128]{1,0:T(8,128)(2,1)S(1)}, bf16[768,48]{1,0:T(8,128)(2,1)S(1)}, bf16[48,768]{1,0:T(8,128)(2,1)S(1)}, f32[48,1024]{1,0:T(8,128)S(1)}, f32[48,1024]{1,0:T(8,128)S(1)}) custom-call(s32[12,64]{1,0:T(8,128)} %bitcast.43, s32[12,64]{1,0:T(8,128)} %bitcast.44, f32[192,64]{1,0:T(8,128)} %bitcast.40, ...), custom_call_target="tpu_custom_call" | custom-call | flops 600000000 | bytes 1333248 | tf_op jit(solution)/shard_map/tables/pallas_call | solution.py:405
  25.8 3.2 %all-to-all-done.1.refs_3_ = f32[16,24,128]{2,1,0:T(8,128)S(1)} async-done(((f32[16,24,128]{2,1,0:T(8,128)}), f32[16,24,128]{2,1,0:T(8,128)S(1)}, u32[]{:S(2)}, u32[]{:S(2)}) %all-to-all-start.1) | async-done | bytes 196640 | tf_op jit(solution)/shard_map/all_to_all | solution.py:439
  29.0 0.9 %translate.1 = f32[16,24,128]{2,1,0:T(8,128)S(1)} custom-call(bf16[768,128]{1,0:T(8,128)(2,1)S(1)} %get-tuple-element.19.refs_0_, bf16[768,48]{1,0:T(8,128)(2,1)S(1)} %get-tuple-element.20.refs_1_, bf16[48,768]{1,0:T(8,128)(2,1)S(1)} %get-tuple-element.21.refs_2_, f32[16,24,128]{2,1,0:T(8,128)S(1)} %all-to-all-done.1.refs_3_), custom_call_target="tpu_custom_call" | custom-call | flops 600000000 | bytes 1081344 | tf_op jit(solution)/shard_map/translate/pallas_call | solution.py:405
  29.9 9.3 %all_to_all.20 = f32[16,24,128]{2,1,0:T(8,128)S(1)} all-to-all(f32[16,24,128]{2,1,0:T(8,128)S(1)} %translate.1), channel_id=1, replica_groups={{0,8,16,24},{2,10,18,26},{4,12,20,28},{6,14,22,30},{1,9,17,25},{3,11,19..., dimensions={0} | all-to-all | bytes 393216 | tf_op jit(solution)/shard_map/all_to_all | solution.py:437
  39.3 7.9 %all_to_all.21.refs_0_ = f32[16,24,128]{2,1,0:T(8,128)S(1)} all-to-all(f32[16,24,128]{2,1,0:T(8,128)S(1)} %bitcast.35), channel_id=1, replica_groups={{0,2,4,6},{8,10,12,14},{16,18,20,22},{24,26,28,30},{1,3,5,7},{9,11,13,1..., dimensions={0} | all-to-all | bytes 393216 | tf_op jit(solution)/shard_map/all_to_all | solution.py:439
  47.2 0.0 collective-permute-start.2
  47.2 1.1 %lower.1 = (f32[384,128]{1,0:T(8,128)}, f32[192,512]{1,0:T(8,128)S(1)}) custom-call(f32[16,24,128]{2,1,0:T(8,128)S(1)} %all_to_all.21.refs_0_, f32[48,1024]{1,0:T(8,128)S(1)} %get-tuple-element.15.refs_2_.refs_1_, f32[48,1024]{1,0:T(8,128)S(1)} %get-tuple-element.16.refs_3_.refs_2_, bf16[4,512,256]{2,1,0:T(8,128)(2,1)S(1)} %get-tuple-element.17.refs_4_.refs_3_, ...), custom_call_target="tpu_custom_call" | custom-call | flops 1500000000 | bytes 3295232 | tf_op jit(solution)/shard_map/lower/pallas_call | solution.py:405
  48.3 0.3 collective-permute-done.2.refs_0_
  48.6 1.9 %finish.1 = f32[768,128]{1,0:T(8,128)} custom-call(f32[16,24,128]{2,1,0:T(8,128)S(1)} %collective-permute-done.2.refs_0_, f32[48,1024]{1,0:T(8,128)S(1)} %get-tuple-element.23.refs_1_, f32[48,1024]{1,0:T(8,128)S(1)} %get-tuple-element.24.refs_2_, bf16[4,512,256]{2,1,0:T(8,128)(2,1)S(1)} %get-tuple-element.17.refs_4_.refs_3_, ...), custom_call_target="tpu_custom_call" | custom-call | flops 1500000000 | bytes 3491840 | tf_op jit(solution)/shard_map/finish/pallas_call | solution.py:405
  (1 shorter events, 0.0 us)
Async XLA Ops:
  0.6 2.3 %collective-permute-start.1 = (f32[768,128]{1,0:T(8,128)}, f32[768,128]{1,0:T(8,128)S(1)}, u32[]{:S(2)}, u32[]{:S(2)}) collective-permute-start(f32[768,128]{1,0:T(8,128)} %bitcast.36), channel_id=1, source_target_pairs={{0,1},{1,0},{2,3},{3,2},{4,5},{5,4},{6,7},{7,6},{8,9},{9,8},{10,11... | collective-permute-start | bytes 1179656 | tf_op jit(solution)/shard_map/ppermute | solution.py:457
  5.3 6.2 %copy-start = (f32[8,6,1024]{2,0,1:T(8,128)S(1)}, f32[8,6,1024]{2,0,1:T(8,128)}, u32[]{:S(2)}) copy-start(f32[8,6,1024]{2,0,1:T(8,128)} %param.12) | copy-start | bytes 589828
  5.3 14.1 %all-to-all-start = ((f32[16,24,128]{2,1,0:T(8,128)}), f32[16,24,128]{2,1,0:T(8,128)S(1)}, u32[]{:S(2)}, u32[]{:S(2)}) async-start(f32[16,24,128]{2,1,0:T(8,128)} %aggregate.1.refs_4_), calls=%async_computation | async-start | bytes 393216 | tf_op jit(solution)/shard_map/all_to_all | solution.py:437
  11.4 12.4 %collective-permute-start = (f32[48,1024]{1,0:T(8,128)S(1)}, f32[48,1024]{1,0:T(8,128)S(1)}, u32[]{:S(2)}, u32[]{:S(2)}) collective-permute-start(f32[48,1024]{1,0:T(8,128)S(1)} %bitcast.39), channel_id=1, source_target_pairs={{1,0},{0,1},{3,2},{2,3},{5,4},{4,5},{7,6},{6,7},{9,8},{8,9},{11,10... | collective-permute-start | bytes 589832 | tf_op jit(solution)/shard_map/ppermute | solution.py:462
  20.1 8.9 %all-to-all-start.1 = ((f32[16,24,128]{2,1,0:T(8,128)}), f32[16,24,128]{2,1,0:T(8,128)S(1)}, u32[]{:S(2)}, u32[]{:S(2)}) async-start(f32[16,24,128]{2,1,0:T(8,128)} %bitcast.16), calls=%async_computation.1 | async-start | bytes 393216 | tf_op jit(solution)/shard_map/all_to_all | solution.py:439
  47.2 1.4 %collective-permute-start.2 = (f32[16,24,128]{2,1,0:T(8,128)S(1)}, f32[16,24,128]{2,1,0:T(8,128)S(1)}, u32[]{:S(2)}, u32[]{:S(2)}) collective-permute-start(f32[16,24,128]{2,1,0:T(8,128)S(1)} %all_to_all.21.refs_0_), channel_id=1, source_target_pairs={{1,0},{0,1},{3,2},{2,3},{5,4},{4,5},{7,6},{6,7},{9,8},{8,9},{11,10... | collective-permute-start | bytes 589832 | tf_op jit(solution)/shard_map/ppermute | solution.py:522

commit v12 on v8

--- a/solution.py
+++ b/solution.py
@@ -13,6 +13,9 @@
 VMEM_BYTES = 8 * 1024 * 1024
 F32 = jnp.float32
 BF16 = jnp.bfloat16
+
+RIM = 16
+KEPT = TILE + 2 * RIM
 
 SIN_TERMS = (-1 / 6, 1 / 120, -1 / 5040, 1 / 362880, -1 / 39916800, 1 / 6227020800)
 COS_TERMS = (-1 / 2, 1 / 24, -1 / 720, 1 / 40320, -1 / 3628800, 1 / 479001600, -1 / 87178291200)
@@ -103,8 +106,8 @@
         after, before = (block + 1) % blocks, (block - 1) % blocks
         pieces = (
             (0, TILE, block * TILE),
-            (TILE, 16, after * TILE),
-            (PAIR - 16, 16, before * TILE + TILE - 16),
+            (TILE, RIM, after * TILE),
+            (TILE + RIM, RIM, before * TILE + TILE - RIM),
         )
         for start, size, first in pieces:
             child = iota((size, PAIR), 0) + first
@@ -114,11 +117,17 @@
                 total = jnp.where(hit, weight_ref[point : point + 1, columns], total)
             high, low = split_two(total)
             wide_ref[block, start : start + size, :] = high
-            wide_ref[block, PAIR + start : PAIR + start + size, :] = low
-        empty = jnp.zeros((TILE - 32, PAIR), BF16)
-        wide_ref[block, TILE + 16 : PAIR - 16, :] = empty
-        wide_ref[block, PAIR + TILE + 16 : 2 * PAIR - 16, :] = empty
+            wide_ref[block, KEPT + start : KEPT + start + size, :] = low
     copies[4].wait()
+
+
+def azimuthal(wide_ref, block, axis):
+    empty = jnp.zeros((TILE - 2 * RIM, PAIR), BF16)
+    halves = []
+    for start in (0, KEPT):
+        kept = (wide_ref[block, start : start + TILE + RIM], empty, wide_ref[block, start + TILE + RIM : start + KEPT])
+        halves.append(jnp.concatenate(kept, axis=0))
+    return jnp.concatenate([halves[0], halves[0], halves[1]], axis=axis)
 
 
 def polar_splat(polar_ref, row, width):
@@ -177,8 +186,7 @@
     for block in range(blocks):
         one, two = windows(high_s, block), windows(low_s, block)
         left = jnp.concatenate(one + two + one, axis=1)
-        right = jnp.concatenate([wide_ref[block, :PAIR], wide_ref[block, :PAIR], wide_ref[block, PAIR:]], axis=0)
-        spread = product(left, right)
+        spread = product(left, azimuthal(wide_ref, block, 0))
         part = slice(block * PAIR, (block + 1) * PAIR)
         summed = []
         for row in range(rows):
@@ -230,7 +238,7 @@
     outs = refs[count + sources : -count - 1]
     local, sems = refs[-count - 1 : -1], refs[-1]
     listed_ref, vector_ref, table_ref = local
-    hot_ref, chosen_ref, table_out, *turned_refs = outs
+    hot_ref, factors_ref, *turned_refs = outs
     copies = started(remote, local, sems)
     for place, phase in enumerate(phases):
         turned_refs[2 * place][...], turned_refs[2 * place + 1][...] = turns(phase[...])
@@ -243,14 +251,16 @@
     order = one_hot(at == place % vectors * (2 * rows) + place // (2 * vectors) * 2 + place // vectors % 2)
     twice = one_hot(iota((width, 2 * width), 1) % width == iota((width, 2 * width), 0))
     lane = iota((vectors, 2 * width), 1)
-    for piece, part in enumerate(split_three(raw)):
+    pieces = []
+    for part in split_three(raw):
         double = product(product(order, part).astype(BF16), twice)
-        target = slice(piece * vectors, (piece + 1) * vectors)
+        pairs = []
         for kind in range(2):
             for first in range(0, rows, 2):
                 one, two = (double[(2 * row + kind) * vectors : (2 * row + kind + 1) * vectors] for row in (first, first + 1))
-                start = (kind * rows + first) * width
-                table_out[target, start : start + 2 * width] = jnp.where(lane < width, one, two).astype(BF16)
+                pairs.append(jnp.where(lane < width, one, two).astype(BF16))
+        pieces.append(jnp.concatenate(pairs, axis=1))
+    spread = jnp.concatenate(pieces, axis=0)
 
     copies[0].wait()
     copies[1].wait()
@@ -260,16 +270,18 @@
     chosen = sum(product(unit, half, 1, 1) for half in split_two(vector_ref[...].astype(F32)))
     cluster = (iota((clusters, 2 * clusters), 1) % clusters).astype(F32)
     vector = (iota((clusters, 3 * vectors), 1) % vectors).astype(F32)
+    picked = []
     for partner in range(partners):
         part = slice(partner * clusters, (partner + 1) * clusters)
         hot_ref[part, :] = one_hot(cluster == listed[:, partner : partner + 1])
-        chosen_ref[part, :] = one_hot(vector == chosen[:, partner : partner + 1])
-
-
-def translate_kernel(groups, hot_ref, chosen_ref, table_ref, arrived_ref, out):
+        picked.append(one_hot(vector == chosen[:, partner : partner + 1]))
+    factors_ref[...] = product(jnp.concatenate(picked, axis=0), spread)
+
+
+def translate_kernel(groups, hot_ref, factors_ref, arrived_ref, out):
     devices, tall, width = arrived_ref.shape
     clusters = devices * groups
-    partners = chosen_ref.shape[0] // clusters
+    partners = hot_ref.shape[0] // clusters
     size = 2 * groups
     steps = tall // size
     starts = [step * size + part * groups for part in range(2) for step in range(steps)]
@@ -277,7 +289,6 @@
         [arrived_ref[:, start : start + groups, :].reshape(clusters, width) for start in starts], axis=1
     )
     gathered = product(hot_ref[...], jnp.concatenate(split_two(source), axis=0))
-    factors = product(chosen_ref[...], table_ref[...])
     for step in range(steps):
         lanes = slice(step * width, (step + 1) * width)
         other = slice((steps + step) * width, (steps + step + 1) * width)
@@ -286,8 +297,9 @@
         for partner in range(partners):
             part = slice(partner * clusters, (partner + 1) * clusters)
             a, b = gathered[part, lanes], gathered[part, other]
-            real += a * factors[part, lanes] - b * factors[part, other]
-            imag += a * factors[part, other] + b * factors[part, lanes]
+            c, d = factors_ref[part, lanes], factors_ref[part, other]
+            real += a * c - b * d
+            imag += a * d + b * c
         for device in range(devices):
             rows = slice(device * groups, (device + 1) * groups)
             out[device, step * size : (step + 1) * size, :] = jnp.concatenate([real[rows], imag[rows]], axis=0)
@@ -315,8 +327,7 @@
                 lowered.append(fields[row][:, part] * cos_ref[turn, part] + crossed[row][:, part] * sin_ref[turn, part])
         high, low = split_two(jnp.concatenate(lowered, axis=0))
         left = jnp.concatenate([high, low, high], axis=1)
-        right = jnp.concatenate([wide_ref[block, :PAIR], wide_ref[block, :PAIR], wide_ref[block, PAIR:]], axis=1)
-        both = product(left, right, 1, 1)
+        both = product(left, azimuthal(wide_ref, block, 1), 1, 1)
         mains.append(both[:, :TILE])
         rims.append(both[:, TILE:])
     lane = iota((OCTANTS * rows * size, TILE), 1)
@@ -447,7 +458,7 @@
         [
             turn,
             turn,
-            struct((blocks, 2 * PAIR, PAIR), BF16),
+            struct((blocks, 2 * KEPT, PAIR), BF16),
             struct((rows * sources * own, TILE), F32),
             struct(field.shape, F32),
         ],
@@ -466,12 +477,11 @@
         scratch=[pltpu.VMEM((2 * groups * OCTANTS * rows, columns), BF16)] * 2,
     )
     arrived = exchange(outgoing)
-    hot, chosen, factors, *turned_parts = call(
+    hot, factors, *turned_parts = call(
         bind(tables_kernel, sources, rows),
         [
             struct((partners * clusters, 2 * clusters), BF16),
-            struct((partners * clusters, 3 * vectors), BF16),
-            struct((3 * vectors, rows * width), BF16),
+            struct((partners * clusters, rows * width), F32),
         ]
         + [turn] * (2 * sources - 2),
         phases,
@@ -483,7 +493,7 @@
     (translated,) = call(
         bind(translate_kernel, groups),
         [struct((devices, rows_all, width), F32)],
-        [hot, chosen, factors, arrived],
+        [hot, factors, arrived],
         600_000_000,
         "translate",
     )

time: 38.4 us -> 39.9 us (1.039)
  local copies, waits for them, and re-layouts: 0.01 us -> 2.74 us
  waiting for transfers between devices: 7.36 us -> 5.71 us
  blocking collectives: 11.3 us -> 11.7 us
    unnamed x2 -> x18, local copies, waits for them, and re-layouts: 0.01 us -> 2.74 us
    all_to_all x1, waiting for transfers between devices: 5.7 us -> 4.08 us  [exchange(): lax.all_to_all(blocks, 'clus', split_axis=0, concat_axis=0, tiled=True)]
where the time goes in v12:
time: 39.9 us; the launch traced here: 39.5 us
  blocking collectives  11.7 us (29%)
  Pallas kernels  10 us (25%)
  starting transfers between devices  8.68 us (22%)
  waiting for transfers between devices  5.71 us (14%)
  local copies, waits for them, and re-layouts  2.74 us (7%)
  between operations  0.72 us (2%)
    all_to_all x1, blocking collectives, exchange(): lax.all_to_all(blocks, 'clus', split_axis=0, concat_axis=0, tiled=True)  11.7 us
    pallas_call x6, Pallas kernels, call(): pl.pallas_call(kernel, out_shape=outs, in_specs=[away] * len(remote) + [n...  10 us
    all_to_all x1, starting transfers between devices, exchange(): lax.all_to_all(blocks, 'clus', split_axis=0, concat_axis=0, tiled=True)  8.01 us
    all_to_all x1, waiting for transfers between devices, exchange(): lax.all_to_all(blocks, 'clus', split_axis=0, concat_axis=0, tiled=True)  4.08 us
    unnamed x18, local copies, waits for them, and re-layouts  2.74 us
    ppermute x1, waiting for transfers between devices, per_device(): phases = [lax.ppermute(phase, 'samp', way) for way in ways]  1.36 us
  transfers between devices with their start and end apart: 4, of which 3 were waited for; matrix products, arithmetic and copies ran while one was open for 0% of the time, Pallas kernels for 13%

profile of v12, /device:TPU:0, one launch (start us, length us, event | category | flops | bytes accessed | tf_op | source)
XLA Modules:
  0.0 39.5 jit_solution(15495420180232092991)
XLA Ops:
  0.6 0.5 %collective-permute-start.1 = (f32[768,128]{1,0:T(8,128)}, f32[768,128]{1,0:T(8,128)S(1)}, u32[]{:S(2)}, u32[]{:S(2)}) collective-permute-start(f32[768,128]{1,0:T(8,128)} %bitcast.25), channel_id=1, source_target_pairs={{0,1},{1,0},{2,3},{3,2},{4,5},{5,4},{6,7},{7,6},{8,9},{9,8},{10,11... | collective-permute-start | bytes 1179656 | tf_op jit(solution)/shard_map/ppermute | solution.py:447
  1.1 1.8 %prepare.1 = (f32[48,1024]{1,0:T(8,128)S(1)}, f32[48,1024]{1,0:T(8,128)S(1)}, bf16[4,320,256]{2,1,0:T(8,128)(2,1)S(1)}, f32[36,128]{1,0:T(8,128)S(1)}, f32[768,128]{1,0:T(8,128)S(1)}) custom-call(f32[6,9]{1,0:T(8,128)} %refs_0_.1, f32[48,1024]{1,0:T(8,128)} %bitcast.27, s32[6,1024]{1,0:T(8,128)} %bitcast.30, f32[6,1024]{1,0:T(8,128)} %bitcast.31, ...), custom_call_target="tpu_custom_call" | custom-call | flops 400000000 | bytes 2754776 | tf_op jit(solution)/shard_map/prepare/pallas_call | solution.py:412
  2.9 0.0 collective-permute-done.1.refs_1_
  2.9 0.0 copy-start.8
  3.0 2.3 %aggregate.1.refs_4_ = f32[16,24,128]{2,1,0:T(8,128)} custom-call(f32[768,128]{1,0:T(8,128)S(1)} %get-tuple-element.13.refs_0_, f32[768,128]{1,0:T(8,128)S(1)} %collective-permute-done.1.refs_1_, f32[48,1024]{1,0:T(8,128)S(1)} %get-tuple-element.14.refs_2_.refs_1_, f32[48,1024]{1,0:T(8,128)S(1)} %get-tuple-element.15.refs_3_.refs_2_, ...), custom_call_target="tpu_custom_call" | custom-call | flops 1500000000 | bytes 2705408 | tf_op jit(solution)/shard_map/aggregate/pallas_call | solution.py:412
  5.3 0.0 copy-start
  5.3 0.7 %copy-done = f32[48,1024]{1,0:T(8,128)} copy-done((f32[48,1024]{1,0:T(8,128)}, f32[48,1024]{1,0:T(8,128)S(1)}, u32[]{:S(2)}) %copy-start) | copy-done | bytes 196632
  5.9 0.0 copy-start.2
  5.9 0.7 %copy-done.2 = f32[48,1024]{1,0:T(8,128)} copy-done((f32[48,1024]{1,0:T(8,128)}, f32[48,1024]{1,0:T(8,128)S(1)}, u32[]{:S(2)}) %copy-start.2) | copy-done | bytes 196632
  6.6 8.0 %all-to-all-start = ((f32[16,24,128]{2,1,0:T(8,128)}), f32[16,24,128]{2,1,0:T(8,128)S(1)}, u32[]{:S(2)}, u32[]{:S(2)}) async-start(f32[16,24,128]{2,1,0:T(8,128)} %aggregate.1.refs_4_), calls=%async_computation | async-start | bytes 393216 | tf_op jit(solution)/shard_map/all_to_all | solution.py:429
  14.6 0.0 copy-done.8
  14.7 0.1 collective-permute-start
  14.8 1.4 %collective-permute-done.refs_3_ = f32[48,1024]{1,0:T(8,128)S(1)} collective-permute-done((f32[48,1024]{1,0:T(8,128)S(1)}, f32[48,1024]{1,0:T(8,128)S(1)}, u32[]{:S(2)}, u32[]{:S(2)}) %collective-permute-start) | collective-permute-done | bytes 196640 | tf_op jit(solution)/shard_map/ppermute | solution.py:452
  16.2 2.2 %tables.1 = (bf16[768,128]{1,0:T(8,128)(2,1)S(1)}, f32[768,768]{1,0:T(8,128)S(1)}, f32[48,1024]{1,0:T(8,128)S(1)}, f32[48,1024]{1,0:T(8,128)S(1)}) custom-call(s32[12,64]{1,0:T(8,128)} %bitcast.32, s32[12,64]{1,0:T(8,128)} %bitcast.33, f32[192,64]{1,0:T(8,128)} %bitcast.29, f32[48,1024]{1,0:T(8,128)S(1)} %collective-permute-done.refs_3_, ...), custom_call_target="tpu_custom_call" | custom-call | flops 600000000 | bytes 3397632 | tf_op jit(solution)/shard_map/tables/pallas_call | solution.py:412
  18.4 0.0 copy-start.4
  18.4 0.7 %copy-done.4 = f32[48,1024]{1,0:T(8,128)} copy-done((f32[48,1024]{1,0:T(8,128)}, f32[48,1024]{1,0:T(8,128)S(1)}, u32[]{:S(2)}) %copy-start.4) | copy-done | bytes 196632
  19.1 0.0 copy-start.6
  19.1 0.7 %copy-done.6 = f32[48,1024]{1,0:T(8,128)} copy-done((f32[48,1024]{1,0:T(8,128)}, f32[48,1024]{1,0:T(8,128)S(1)}, u32[]{:S(2)}) %copy-start.6) | copy-done | bytes 196632
  19.7 4.1 %all-to-all-done.refs_2_ = f32[16,24,128]{2,1,0:T(8,128)S(1)} async-done(((f32[16,24,128]{2,1,0:T(8,128)}), f32[16,24,128]{2,1,0:T(8,128)S(1)}, u32[]{:S(2)}, u32[]{:S(2)}) %all-to-all-start) | async-done | bytes 196640 | tf_op jit(solution)/shard_map/all_to_all | solution.py:429
  23.8 0.0 copy-start.1
  23.8 0.0 copy-start.3
  23.8 0.6 %translate.1 = f32[16,24,128]{2,1,0:T(8,128)S(1)} custom-call(bf16[768,128]{1,0:T(8,128)(2,1)S(1)} %get-tuple-element.18.refs_0_, f32[768,768]{1,0:T(8,128)S(1)} %get-tuple-element.19.refs_1_, f32[16,24,128]{2,1,0:T(8,128)S(1)} %all-to-all-done.refs_2_), custom_call_target="tpu_custom_call" | custom-call | flops 600000000 | bytes 3145728 | tf_op jit(solution)/shard_map/translate/pallas_call | solution.py:412
  24.5 11.7 %all_to_all.10.refs_0_ = f32[16,24,128]{2,1,0:T(8,128)S(1)} all-to-all(f32[16,24,128]{2,1,0:T(8,128)S(1)} %translate.1), channel_id=1, replica_groups=mesh['clus'=16,'samp'=2] {'clus'}, dimensions={0} | all-to-all | bytes 393216 | tf_op jit(solution)/shard_map/all_to_all | solution.py:429
  36.1 0.0 copy-start.5
  36.1 0.0 copy-start.7
  36.1 0.0 collective-permute-start.2
  36.1 0.0 copy-done.1
  36.1 0.0 copy-done.3
  36.2 1.1 %lower.1 = (f32[384,128]{1,0:T(8,128)}, f32[192,512]{1,0:T(8,128)S(1)}) custom-call(f32[16,24,128]{2,1,0:T(8,128)S(1)} %all_to_all.10.refs_0_, f32[48,1024]{1,0:T(8,128)S(1)} %copy-done.1, f32[48,1024]{1,0:T(8,128)S(1)} %copy-done.3, bf16[4,320,256]{2,1,0:T(8,128)(2,1)S(1)} %get-tuple-element.16.refs_4_.refs_3_, f32[36,128]{1,0:T(8,128)S(1)} %get-tuple-element.17.refs_5_.refs_4_), custom_call_target="tpu_custom_call" | custom-call | flops 1500000000 | bytes 2508800 | tf_op jit(solution)/shard_map/lower/pallas_call | solution.py:412
  37.3 0.3 collective-permute-done.2.refs_0_
  37.6 0.0 copy-done.5
  37.6 0.0 copy-done.7
  37.6 2.0 %finish.1 = f32[768,128]{1,0:T(8,128)} custom-call(f32[16,24,128]{2,1,0:T(8,128)S(1)} %collective-permute-done.2.refs_0_, f32[48,1024]{1,0:T(8,128)S(1)} %copy-done.5, f32[48,1024]{1,0:T(8,128)S(1)} %copy-done.7, bf16[4,320,256]{2,1,0:T(8,128)(2,1)S(1)} %get-tuple-element.16.refs_4_.refs_3_, f32[36,128]{1,0:T(8,128)S(1)} %get-tuple-element.17.refs_5_.refs_4_, ...), custom_call_target="tpu_custom_call" | custom-call | flops 1500000000 | bytes 2705408 | tf_op jit(solution)/shard_map/finish/pallas_call | solution.py:412
Async XLA Ops:
  0.6 2.3 %collective-permute-start.1 = (f32[768,128]{1,0:T(8,128)}, f32[768,128]{1,0:T(8,128)S(1)}, u32[]{:S(2)}, u32[]{:S(2)}) collective-permute-start(f32[768,128]{1,0:T(8,128)} %bitcast.25), channel_id=1, source_target_pairs={{0,1},{1,0},{2,3},{3,2},{4,5},{5,4},{6,7},{7,6},{8,9},{9,8},{10,11... | collective-permute-start | bytes 1179656 | tf_op jit(solution)/shard_map/ppermute | solution.py:447
  2.9 11.7 %copy-start.8 = (f32[8,6,1024]{2,0,1:T(8,128)S(1)}, f32[8,6,1024]{2,0,1:T(8,128)}, u32[]{:S(2)}) copy-start(f32[8,6,1024]{2,0,1:T(8,128)} %param.12) | copy-start | bytes 589828
  5.3 0.7 %copy-start = (f32[48,1024]{1,0:T(8,128)}, f32[48,1024]{1,0:T(8,128)S(1)}, u32[]{:S(2)}) copy-start(f32[48,1024]{1,0:T(8,128)S(1)} %get-tuple-element.14.refs_2_.refs_1_) | copy-start | bytes 589828
  5.9 0.7 %copy-start.2 = (f32[48,1024]{1,0:T(8,128)}, f32[48,1024]{1,0:T(8,128)S(1)}, u32[]{:S(2)}) copy-start(f32[48,1024]{1,0:T(8,128)S(1)} %get-tuple-element.15.refs_3_.refs_2_) | copy-start | bytes 589828
  6.6 17.2 %all-to-all-start = ((f32[16,24,128]{2,1,0:T(8,128)}), f32[16,24,128]{2,1,0:T(8,128)S(1)}, u32[]{:S(2)}, u32[]{:S(2)}) async-start(f32[16,24,128]{2,1,0:T(8,128)} %aggregate.1.refs_4_), calls=%async_computation | async-start | bytes 393216 | tf_op jit(solution)/shard_map/all_to_all | solution.py:429
  14.7 1.5 %collective-permute-start = (f32[48,1024]{1,0:T(8,128)S(1)}, f32[48,1024]{1,0:T(8,128)S(1)}, u32[]{:S(2)}, u32[]{:S(2)}) collective-permute-start(f32[48,1024]{1,0:T(8,128)S(1)} %bitcast.28), channel_id=1, source_target_pairs={{1,0},{0,1},{3,2},{2,3},{5,4},{4,5},{7,6},{6,7},{9,8},{8,9},{11,10... | collective-permute-start | bytes 589832 | tf_op jit(solution)/shard_map/ppermute | solution.py:452
  18.4 0.7 %copy-start.4 = (f32[48,1024]{1,0:T(8,128)}, f32[48,1024]{1,0:T(8,128)S(1)}, u32[]{:S(2)}) copy-start(f32[48,1024]{1,0:T(8,128)S(1)} %get-tuple-element.21.refs_1_) | copy-start | bytes 589828
  19.1 0.7 %copy-start.6 = (f32[48,1024]{1,0:T(8,128)}, f32[48,1024]{1,0:T(8,128)S(1)}, u32[]{:S(2)}) copy-start(f32[48,1024]{1,0:T(8,128)S(1)} %get-tuple-element.22.refs_2_) | copy-start | bytes 589828
  23.8 12.3 %copy-start.1 = (f32[48,1024]{1,0:T(8,128)S(1)}, f32[48,1024]{1,0:T(8,128)}, u32[]{:S(2)}) copy-start(f32[48,1024]{1,0:T(8,128)} %copy-done) | copy-start | bytes 589828
  23.8 12.3 %copy-start.3 = (f32[48,1024]{1,0:T(8,128)S(1)}, f32[48,1024]{1,0:T(8,128)}, u32[]{:S(2)}) copy-start(f32[48,1024]{1,0:T(8,128)} %copy-done.2) | copy-start | bytes 589828
  36.1 1.4 %copy-start.5 = (f32[48,1024]{1,0:T(8,128)S(1)}, f32[48,1024]{1,0:T(8,128)}, u32[]{:S(2)}) copy-start(f32[48,1024]{1,0:T(8,128)} %copy-done.4) | copy-start | bytes 589828
  36.1 1.4 %copy-start.7 = (f32[48,1024]{1,0:T(8,128)S(1)}, f32[48,1024]{1,0:T(8,128)}, u32[]{:S(2)}) copy-start(f32[48,1024]{1,0:T(8,128)} %copy-done.6) | copy-start | bytes 589828
  36.1 1.4 %collective-permute-start.2 = (f32[16,24,128]{2,1,0:T(8,128)S(1)}, f32[16,24,128]{2,1,0:T(8,128)S(1)}, u32[]{:S(2)}, u32[]{:S(2)}) collective-permute-start(f32[16,24,128]{2,1,0:T(8,128)S(1)} %all_to_all.10.refs_0_), channel_id=1, source_target_pairs={{1,0},{0,1},{3,2},{2,3},{5,4},{4,5},{7,6},{6,7},{9,8},{8,9},{11,10... | collective-permute-start | bytes 589832 | tf_op jit(solution)/shard_map/ppermute | solution.py:511

commit v13 on v12

--- a/solution.py
+++ b/solution.py
@@ -10,7 +10,7 @@
 TILE = 128
 PAIR = 2 * TILE
 HALF = TILE // 2
-VMEM_BYTES = 8 * 1024 * 1024
+VMEM_BYTES = 4 * 1024 * 1024
 F32 = jnp.float32
 BF16 = jnp.bfloat16
 
@@ -415,7 +415,7 @@
         in_specs=[away] * len(remote) + [near] * len(args) + [free] * len(after),
         out_specs=[free if place in far else near for place in range(len(outs))],
         scratch_shapes=scratch,
-        compiler_params=pltpu.CompilerParams(vmem_limit_bytes=max(VMEM_BYTES, 8 * max(arg.size for arg in (*remote, *args)))),
+        compiler_params=pltpu.CompilerParams(vmem_limit_bytes=max(VMEM_BYTES, 6 * max(arg.size for arg in (*remote, *args)))),
         cost_estimate=pl.CostEstimate(flops=flops, bytes_accessed=held, transcendentals=0),
         name=name,
     )(*remote, *args, *after)

time: 39.9 us -> 39.9 us (level)
  no operation moved by 1% of the time
where the time goes in v13:
time: 39.9 us; the launch traced here: 39.5 us
  blocking collectives  11.7 us (29%)
  Pallas kernels  10 us (25%)
  starting transfers between devices  8.68 us (22%)
  waiting for transfers between devices  5.71 us (14%)
  local copies, waits for them, and re-layouts  2.74 us (7%)
  between operations  0.72 us (2%)
    all_to_all x1, blocking collectives, exchange(): lax.all_to_all(blocks, 'clus', split_axis=0, concat_axis=0, tiled=True)  11.7 us
    pallas_call x6, Pallas kernels, call(): pl.pallas_call(kernel, out_shape=outs, in_specs=[away] * len(remote) + [n...  10 us
    all_to_all x1, starting transfers between devices, exchange(): lax.all_to_all(blocks, 'clus', split_axis=0, concat_axis=0, tiled=True)  8.01 us
    all_to_all x1, waiting for transfers between devices, exchange(): lax.all_to_all(blocks, 'clus', split_axis=0, concat_axis=0, tiled=True)  4.08 us
    unnamed x18, local copies, waits for them, and re-layouts  2.74 us
    ppermute x1, waiting for transfers between devices, per_device(): phases = [lax.ppermute(phase, 'samp', way) for way in ways]  1.36 us
  transfers between devices with their start and end apart: 4, of which 3 were waited for; matrix products, arithmetic and copies ran while one was open for 0% of the time, Pallas kernels for 13%

profile of v13, /device:TPU:0, one launch (start us, length us, event | category | flops | bytes accessed | tf_op | source)
XLA Modules:
  0.0 39.5 jit_solution(2710974345239344279)
XLA Ops:
  0.6 0.5 %collective-permute-start.1 = (f32[768,128]{1,0:T(8,128)}, f32[768,128]{1,0:T(8,128)S(1)}, u32[]{:S(2)}, u32[]{:S(2)}) collective-permute-start(f32[768,128]{1,0:T(8,128)} %bitcast.25), channel_id=1, source_target_pairs={{0,1},{1,0},{2,3},{3,2},{4,5},{5,4},{6,7},{7,6},{8,9},{9,8},{10,11... | collective-permute-start | bytes 1179656 | tf_op jit(solution)/shard_map/ppermute | solution.py:447
  1.1 1.8 %prepare.1 = (f32[48,1024]{1,0:T(8,128)S(1)}, f32[48,1024]{1,0:T(8,128)S(1)}, bf16[4,320,256]{2,1,0:T(8,128)(2,1)S(1)}, f32[36,128]{1,0:T(8,128)S(1)}, f32[768,128]{1,0:T(8,128)S(1)}) custom-call(f32[6,9]{1,0:T(8,128)} %refs_0_.1, f32[48,1024]{1,0:T(8,128)} %bitcast.27, s32[6,1024]{1,0:T(8,128)} %bitcast.30, f32[6,1024]{1,0:T(8,128)} %bitcast.31, ...), custom_call_target="tpu_custom_call" | custom-call | flops 400000000 | bytes 2754776 | tf_op jit(solution)/shard_map/prepare/pallas_call | solution.py:412
  2.9 0.0 collective-permute-done.1.refs_1_
  2.9 0.0 copy-start.8
  3.0 2.3 %aggregate.1.refs_4_ = f32[16,24,128]{2,1,0:T(8,128)} custom-call(f32[768,128]{1,0:T(8,128)S(1)} %get-tuple-element.13.refs_0_, f32[768,128]{1,0:T(8,128)S(1)} %collective-permute-done.1.refs_1_, f32[48,1024]{1,0:T(8,128)S(1)} %get-tuple-element.14.refs_2_.refs_1_, f32[48,1024]{1,0:T(8,128)S(1)} %get-tuple-element.15.refs_3_.refs_2_, ...), custom_call_target="tpu_custom_call" | custom-call | flops 1500000000 | bytes 2705408 | tf_op jit(solution)/shard_map/aggregate/pallas_call | solution.py:412
  5.3 0.0 copy-start
  5.3 0.7 %copy-done = f32[48,1024]{1,0:T(8,128)} copy-done((f32[48,1024]{1,0:T(8,128)}, f32[48,1024]{1,0:T(8,128)S(1)}, u32[]{:S(2)}) %copy-start) | copy-done | bytes 196632
  5.9 0.0 copy-start.2
  5.9 0.7 %copy-done.2 = f32[48,1024]{1,0:T(8,128)} copy-done((f32[48,1024]{1,0:T(8,128)}, f32[48,1024]{1,0:T(8,128)S(1)}, u32[]{:S(2)}) %copy-start.2) | copy-done | bytes 196632
  6.6 8.0 %all-to-all-start = ((f32[16,24,128]{2,1,0:T(8,128)}), f32[16,24,128]{2,1,0:T(8,128)S(1)}, u32[]{:S(2)}, u32[]{:S(2)}) async-start(f32[16,24,128]{2,1,0:T(8,128)} %aggregate.1.refs_4_), calls=%async_computation | async-start | bytes 393216 | tf_op jit(solution)/shard_map/all_to_all | solution.py:429
  14.6 0.0 copy-done.8
  14.7 0.1 collective-permute-start
  14.8 1.4 %collective-permute-done.refs_3_ = f32[48,1024]{1,0:T(8,128)S(1)} collective-permute-done((f32[48,1024]{1,0:T(8,128)S(1)}, f32[48,1024]{1,0:T(8,128)S(1)}, u32[]{:S(2)}, u32[]{:S(2)}) %collective-permute-start) | collective-permute-done | bytes 196640 | tf_op jit(solution)/shard_map/ppermute | solution.py:452
  16.2 2.2 %tables.1 = (bf16[768,128]{1,0:T(8,128)(2,1)S(1)}, f32[768,768]{1,0:T(8,128)S(1)}, f32[48,1024]{1,0:T(8,128)S(1)}, f32[48,1024]{1,0:T(8,128)S(1)}) custom-call(s32[12,64]{1,0:T(8,128)} %bitcast.32, s32[12,64]{1,0:T(8,128)} %bitcast.33, f32[192,64]{1,0:T(8,128)} %bitcast.29, f32[48,1024]{1,0:T(8,128)S(1)} %collective-permute-done.refs_3_, ...), custom_call_target="tpu_custom_call" | custom-call | flops 600000000 | bytes 3397632 | tf_op jit(solution)/shard_map/tables/pallas_call | solution.py:412
  18.4 0.0 copy-start.4
  18.4 0.7 %copy-done.4 = f32[48,1024]{1,0:T(8,128)} copy-done((f32[48,1024]{1,0:T(8,128)}, f32[48,1024]{1,0:T(8,128)S(1)}, u32[]{:S(2)}) %copy-start.4) | copy-done | bytes 196632
  19.1 0.0 copy-start.6
  19.1 0.7 %copy-done.6 = f32[48,1024]{1,0:T(8,128)} copy-done((f32[48,1024]{1,0:T(8,128)}, f32[48,1024]{1,0:T(8,128)S(1)}, u32[]{:S(2)}) %copy-start.6) | copy-done | bytes 196632
  19.7 4.1 %all-to-all-done.refs_2_ = f32[16,24,128]{2,1,0:T(8,128)S(1)} async-done(((f32[16,24,128]{2,1,0:T(8,128)}), f32[16,24,128]{2,1,0:T(8,128)S(1)}, u32[]{:S(2)}, u32[]{:S(2)}) %all-to-all-start) | async-done | bytes 196640 | tf_op jit(solution)/shard_map/all_to_all | solution.py:429
  23.8 0.0 copy-start.1
  23.8 0.0 copy-start.3
  23.8 0.6 %translate.1 = f32[16,24,128]{2,1,0:T(8,128)S(1)} custom-call(bf16[768,128]{1,0:T(8,128)(2,1)S(1)} %get-tuple-element.18.refs_0_, f32[768,768]{1,0:T(8,128)S(1)} %get-tuple-element.19.refs_1_, f32[16,24,128]{2,1,0:T(8,128)S(1)} %all-to-all-done.refs_2_), custom_call_target="tpu_custom_call" | custom-call | flops 600000000 | bytes 3145728 | tf_op jit(solution)/shard_map/translate/pallas_call | solution.py:412
  24.5 11.7 %all_to_all.10.refs_0_ = f32[16,24,128]{2,1,0:T(8,128)S(1)} all-to-all(f32[16,24,128]{2,1,0:T(8,128)S(1)} %translate.1), channel_id=1, replica_groups=mesh['clus'=16,'samp'=2] {'clus'}, dimensions={0} | all-to-all | bytes 393216 | tf_op jit(solution)/shard_map/all_to_all | solution.py:429
  36.1 0.0 copy-start.5
  36.1 0.0 copy-start.7
  36.1 0.0 collective-permute-start.2
  36.1 0.0 copy-done.1
  36.1 0.0 copy-done.3
  36.2 1.1 %lower.1 = (f32[384,128]{1,0:T(8,128)}, f32[192,512]{1,0:T(8,128)S(1)}) custom-call(f32[16,24,128]{2,1,0:T(8,128)S(1)} %all_to_all.10.refs_0_, f32[48,1024]{1,0:T(8,128)S(1)} %copy-done.1, f32[48,1024]{1,0:T(8,128)S(1)} %copy-done.3, bf16[4,320,256]{2,1,0:T(8,128)(2,1)S(1)} %get-tuple-element.16.refs_4_.refs_3_, f32[36,128]{1,0:T(8,128)S(1)} %get-tuple-element.17.refs_5_.refs_4_), custom_call_target="tpu_custom_call" | custom-call | flops 1500000000 | bytes 2508800 | tf_op jit(solution)/shard_map/lower/pallas_call | solution.py:412
  37.3 0.3 collective-permute-done.2.refs_0_
  37.6 0.0 copy-done.5
  37.6 0.0 copy-done.7
  37.6 2.0 %finish.1 = f32[768,128]{1,0:T(8,128)} custom-call(f32[16,24,128]{2,1,0:T(8,128)S(1)} %collective-permute-done.2.refs_0_, f32[48,1024]{1,0:T(8,128)S(1)} %copy-done.5, f32[48,1024]{1,0:T(8,128)S(1)} %copy-done.7, bf16[4,320,256]{2,1,0:T(8,128)(2,1)S(1)} %get-tuple-element.16.refs_4_.refs_3_, f32[36,128]{1,0:T(8,128)S(1)} %get-tuple-element.17.refs_5_.refs_4_, ...), custom_call_target="tpu_custom_call" | custom-call | flops 1500000000 | bytes 2705408 | tf_op jit(solution)/shard_map/finish/pallas_call | solution.py:412
Async XLA Ops:
  0.6 2.3 %collective-permute-start.1 = (f32[768,128]{1,0:T(8,128)}, f32[768,128]{1,0:T(8,128)S(1)}, u32[]{:S(2)}, u32[]{:S(2)}) collective-permute-start(f32[768,128]{1,0:T(8,128)} %bitcast.25), channel_id=1, source_target_pairs={{0,1},{1,0},{2,3},{3,2},{4,5},{5,4},{6,7},{7,6},{8,9},{9,8},{10,11... | collective-permute-start | bytes 1179656 | tf_op jit(solution)/shard_map/ppermute | solution.py:447
  2.9 11.7 %copy-start.8 = (f32[8,6,1024]{2,0,1:T(8,128)S(1)}, f32[8,6,1024]{2,0,1:T(8,128)}, u32[]{:S(2)}) copy-start(f32[8,6,1024]{2,0,1:T(8,128)} %param.12) | copy-start | bytes 589828
  5.3 0.7 %copy-start = (f32[48,1024]{1,0:T(8,128)}, f32[48,1024]{1,0:T(8,128)S(1)}, u32[]{:S(2)}) copy-start(f32[48,1024]{1,0:T(8,128)S(1)} %get-tuple-element.14.refs_2_.refs_1_) | copy-start | bytes 589828
  5.9 0.7 %copy-start.2 = (f32[48,1024]{1,0:T(8,128)}, f32[48,1024]{1,0:T(8,128)S(1)}, u32[]{:S(2)}) copy-start(f32[48,1024]{1,0:T(8,128)S(1)} %get-tuple-element.15.refs_3_.refs_2_) | copy-start | bytes 589828
  6.6 17.2 %all-to-all-start = ((f32[16,24,128]{2,1,0:T(8,128)}), f32[16,24,128]{2,1,0:T(8,128)S(1)}, u32[]{:S(2)}, u32[]{:S(2)}) async-start(f32[16,24,128]{2,1,0:T(8,128)} %aggregate.1.refs_4_), calls=%async_computation | async-start | bytes 393216 | tf_op jit(solution)/shard_map/all_to_all | solution.py:429
  14.7 1.5 %collective-permute-start = (f32[48,1024]{1,0:T(8,128)S(1)}, f32[48,1024]{1,0:T(8,128)S(1)}, u32[]{:S(2)}, u32[]{:S(2)}) collective-permute-start(f32[48,1024]{1,0:T(8,128)S(1)} %bitcast.28), channel_id=1, source_target_pairs={{1,0},{0,1},{3,2},{2,3},{5,4},{4,5},{7,6},{6,7},{9,8},{8,9},{11,10... | collective-permute-start | bytes 589832 | tf_op jit(solution)/shard_map/ppermute | solution.py:452
  18.4 0.7 %copy-start.4 = (f32[48,1024]{1,0:T(8,128)}, f32[48,1024]{1,0:T(8,128)S(1)}, u32[]{:S(2)}) copy-start(f32[48,1024]{1,0:T(8,128)S(1)} %get-tuple-element.21.refs_1_) | copy-start | bytes 589828
  19.1 0.7 %copy-start.6 = (f32[48,1024]{1,0:T(8,128)}, f32[48,1024]{1,0:T(8,128)S(1)}, u32[]{:S(2)}) copy-start(f32[48,1024]{1,0:T(8,128)S(1)} %get-tuple-element.22.refs_2_) | copy-start | bytes 589828
  23.8 12.3 %copy-start.1 = (f32[48,1024]{1,0:T(8,128)S(1)}, f32[48,1024]{1,0:T(8,128)}, u32[]{:S(2)}) copy-start(f32[48,1024]{1,0:T(8,128)} %copy-done) | copy-start | bytes 589828
  23.8 12.3 %copy-start.3 = (f32[48,1024]{1,0:T(8,128)S(1)}, f32[48,1024]{1,0:T(8,128)}, u32[]{:S(2)}) copy-start(f32[48,1024]{1,0:T(8,128)} %copy-done.2) | copy-start | bytes 589828
  36.1 1.4 %copy-start.5 = (f32[48,1024]{1,0:T(8,128)S(1)}, f32[48,1024]{1,0:T(8,128)}, u32[]{:S(2)}) copy-start(f32[48,1024]{1,0:T(8,128)} %copy-done.4) | copy-start | bytes 589828
  36.1 1.4 %copy-start.7 = (f32[48,1024]{1,0:T(8,128)S(1)}, f32[48,1024]{1,0:T(8,128)}, u32[]{:S(2)}) copy-start(f32[48,1024]{1,0:T(8,128)} %copy-done.6) | copy-start | bytes 589828
  36.1 1.4 %collective-permute-start.2 = (f32[16,24,128]{2,1,0:T(8,128)S(1)}, f32[16,24,128]{2,1,0:T(8,128)S(1)}, u32[]{:S(2)}, u32[]{:S(2)}) collective-permute-start(f32[16,24,128]{2,1,0:T(8,128)S(1)} %all_to_all.10.refs_0_), channel_id=1, source_target_pairs={{1,0},{0,1},{3,2},{2,3},{5,4},{4,5},{7,6},{6,7},{9,8},{8,9},{11,10... | collective-permute-start | bytes 589832 | tf_op jit(solution)/shard_map/ppermute | solution.py:511
